TPU v7x, 256 devices: a whole 4x4x8 slice. The times are simulated.
256 devices in a mesh: pipe: 4 (over y), expert: 32 (over z, x), dp: 2 (over core).
Axes of the slice: x: 4, y: 4, z: 8, core: 2. Of those that a mesh axis runs over, the one named last changes fastest.
Arguments:
- tokens: bfloat16 [2, 4096, 2048], P(None, ('expert', 'dp')), may hold values from -6 to 6
- cotangent: bfloat16 [2, 4096, 2048], P(None, ('expert', 'dp')), may hold values from -6 to 6
- routes: int32 [4, 2, 4096, 2], P('pipe', None, ('expert', 'dp')), may hold values from 0 to 31, all different within a row; in each aligned block of 64 rows (0 to 63, 64 to 127, ..., all dimensions but the last counted through in order) at most 6 rows name the same one
- gates: float32 [4, 2, 4096, 2], P('pipe', None, ('expert', 'dp')), may hold values from 0.1 to 0.6
- norm_gain: float32 [4, 2048], P('pipe'), may hold values from 0.5 to 1.5
- w_gate: bfloat16 [4, 32, 2048, 768], P('pipe', 'expert'), may hold values from -0.125 to 0.125
- w_up: bfloat16 [4, 32, 2048, 768], P('pipe', 'expert'), may hold values from -0.125 to 0.125
- w_down: bfloat16 [4, 32, 768, 2048], P('pipe', 'expert'), may hold values from -0.21875 to 0.21875
- in_a: bfloat16 [4, 32, 2048, 32], P('pipe', 'expert'), may hold values from -0.125 to 0.125
- in_b: bfloat16 [4, 32, 2, 16, 768], P('pipe', 'expert'), may hold values from -1.5 to 1.5
- down_a: bfloat16 [4, 32, 768, 16], P('pipe', 'expert'), may hold values from -0.21875 to 0.21875
- down_b: bfloat16 [4, 32, 16, 2048], P('pipe', 'expert'), may hold values from -1.5 to 1.5
Outputs:
- hidden: bfloat16 [4, 2, 4096, 2048], P('pipe', None, ('expert', 'dp'))
- input_grads: bfloat16 [4, 2, 4096, 2048], P('pipe', None, ('expert', 'dp'))
- grad_in_a: float32 [4, 32, 2048, 32], P('pipe', 'expert')
- grad_in_b: float32 [4, 32, 2, 16, 768], P('pipe', 'expert')
- grad_down_a: float32 [4, 32, 768, 16], P('pipe', 'expert')
- grad_down_b: float32 [4, 32, 16, 2048], P('pipe', 'expert')
Inputs may be any that keep to these rules, and one draw needn't show every extreme that they name: `routes`: each token names 2 different experts; among the 64 tokens of one device's block (one section, one micro-batch, tokens b * 64 to (b + 1) * 64 - 1), no expert is named by more than 6 tokens.
All inputs are finite; a program needn't handle non-finite values.
Results may differ from a plain program's by a relative error of at most 0.039.
Values may be sent and summed in bfloat16 or wider, within the bound.
No kernel may reach another device: no remote copies, remote signals or barrier semaphores. Data moves between devices by JAX's collectives and lax.ppermute only.
A program may use at most 128 MiB of HBM per device.

v0:
```python
import jax
import jax.numpy as jnp
from jax import lax
from jax.sharding import PartitionSpec as P

EPS = 1e-06


def shifted(x, axis, by):
    length = lax.axis_size(axis)
    pairs = [(i, i + by) for i in range(length) if 0 <= i + by < length]
    return lax.ppermute(x, axis, pairs)


def normalize(section_in, norm_scale):
    values = section_in.astype(jnp.float32)
    inverse = lax.rsqrt(jnp.mean(values * values, axis=-1, keepdims=True) + EPS)
    return ((values * inverse * norm_scale).astype(jnp.bfloat16), inverse)


def normalize_back(grad_norm, section_in, inverse, norm_scale):
    normed = section_in.astype(jnp.float32) * inverse
    scaled = grad_norm * norm_scale
    return inverse * (scaled - normed * jnp.mean(scaled * normed, axis=-1, keepdims=True))


def times_transposed(left, right):
    return lax.dot_general(
        left, right, (((1,), (1,)), ((), ())), preferred_element_type=jnp.float32
    )


def transposed_times(left, right):
    return lax.dot_general(
        left, right, (((0,), (0,)), ((), ())), preferred_element_type=jnp.float32
    )


def expert_forward(slot_rows, w_gate, w_up, w_down, in_a, in_b, down_a, down_b):
    low_rank = down_a.shape[1]
    low_in = jnp.dot(slot_rows, in_a, preferred_element_type=jnp.float32).astype(jnp.bfloat16)
    gate_pre = jnp.dot(slot_rows, w_gate, preferred_element_type=jnp.float32) + jnp.dot(
        low_in[:, :low_rank], in_b[0], preferred_element_type=jnp.float32
    )
    up_pre = jnp.dot(slot_rows, w_up, preferred_element_type=jnp.float32) + jnp.dot(
        low_in[:, low_rank:], in_b[1], preferred_element_type=jnp.float32
    )
    activated = (jax.nn.silu(gate_pre) * up_pre).astype(jnp.bfloat16)
    low_down = jnp.dot(activated, down_a, preferred_element_type=jnp.float32).astype(jnp.bfloat16)
    expert_out = (
        jnp.dot(activated, w_down, preferred_element_type=jnp.float32)
        + jnp.dot(low_down, down_b, preferred_element_type=jnp.float32)
    ).astype(jnp.bfloat16)
    return (expert_out, (low_in, gate_pre, up_pre, activated, low_down))


def expert_backward(
    slot_rows, grad_out, saved_state, w_gate, w_up, w_down, in_a, in_b, down_a, down_b
):
    low_in, gate_pre, up_pre, activated, low_down = saved_state
    low_rank = down_a.shape[1]
    grad_low_down = times_transposed(grad_out, down_b).astype(jnp.bfloat16)
    grad_down_b = transposed_times(low_down, grad_out)
    grad_down_a = transposed_times(activated, grad_low_down)
    grad_act = times_transposed(grad_out, w_down) + times_transposed(grad_low_down, down_a)
    sigmoid = jax.nn.sigmoid(gate_pre)
    grad_gate = (grad_act * up_pre * sigmoid * (1.0 + gate_pre * (1.0 - sigmoid))).astype(
        jnp.bfloat16
    )
    grad_up = (grad_act * gate_pre * sigmoid).astype(jnp.bfloat16)
    grad_in_b = jnp.stack(
        [
            transposed_times(low_in[:, :low_rank], grad_gate),
            transposed_times(low_in[:, low_rank:], grad_up),
        ]
    )
    grad_low_in = jnp.concatenate(
        [times_transposed(grad_gate, in_b[0]), times_transposed(grad_up, in_b[1])], axis=1
    ).astype(jnp.bfloat16)
    grad_in_a = transposed_times(slot_rows, grad_low_in)
    grad_rows = (
        times_transposed(grad_gate, w_gate)
        + times_transposed(grad_up, w_up)
        + times_transposed(grad_low_in, in_a)
    ).astype(jnp.bfloat16)
    return (grad_rows, (grad_in_a, grad_in_b, grad_down_a, grad_down_b))


def send_rows(buffer):
    return lax.all_to_all(buffer, "expert", split_axis=0, concat_axis=0, tiled=True)


def return_rows(buffer):
    return lax.all_to_all(buffer, "expert", split_axis=0, concat_axis=0, tiled=True)


def slot_targets(routes_micro, expert_count, capacity, copy_count):
    flat_routes = routes_micro.reshape(-1)
    onehot = (flat_routes[:, None] == jnp.arange(expert_count, dtype=jnp.int32)[None, :]).astype(
        jnp.int32
    )
    earlier = jnp.cumsum(onehot, axis=0) - onehot
    position = jnp.sum(earlier * onehot, axis=1)
    slot_width = capacity // copy_count
    target = (
        flat_routes * copy_count + position // slot_width
    ) * slot_width + position % slot_width
    return target.reshape(routes_micro.shape)


def store_slot(stored_array, new_value, micro_index, active):
    previous = lax.dynamic_index_in_dim(stored_array, micro_index, 0, keepdims=False)
    return lax.dynamic_update_index_in_dim(
        stored_array, jnp.where(active, new_value, previous), micro_index, 0
    )


def body(
    tokens, cotangent, routes, gates, norm_gain, w_gate, w_up, w_down, in_a, in_b, down_a, down_b
):
    section_index = lax.axis_index("pipe")
    section_count = lax.axis_size("pipe")
    expert_count = lax.axis_size("expert")
    micro_count, tok_rows, model_width = tokens.shape
    top_count = routes.shape[3]
    hidden_width = w_gate.shape[3]
    low_rank = down_a.shape[3]
    copy_count = 1
    capacity = 2 * ((5 * tok_rows * top_count + 8 * expert_count - 1) // (8 * expert_count))
    peer_count = expert_count * copy_count
    slot_width = capacity // copy_count
    slot_count = peer_count * slot_width
    tick_count = micro_count + section_count - 1
    norm_scale = norm_gain[0]
    weights = (
        w_gate[0, 0],
        w_up[0, 0],
        w_down[0, 0],
        in_a[0, 0],
        in_b[0, 0],
        down_a[0, 0],
        down_b[0, 0],
    )

    def busy_forward(slot_rows):
        return expert_forward(
            slot_rows,
            weights[0],
            weights[1],
            weights[2],
            weights[3],
            weights[4],
            weights[5],
            weights[6],
        )

    def spare_forward(slot_rows):
        return (
            jnp.zeros((slot_count, model_width), jnp.bfloat16),
            (
                jnp.zeros((slot_count, 2 * low_rank), jnp.bfloat16),
                jnp.zeros((slot_count, hidden_width), jnp.float32),
                jnp.zeros((slot_count, hidden_width), jnp.float32),
                jnp.zeros((slot_count, hidden_width), jnp.bfloat16),
                jnp.zeros((slot_count, low_rank), jnp.bfloat16),
            ),
        )

    def busy_backward(operands):
        return expert_backward(
            operands[0],
            operands[1],
            operands[2],
            weights[0],
            weights[1],
            weights[2],
            weights[3],
            weights[4],
            weights[5],
            weights[6],
        )

    def spare_backward(operands):
        return (
            jnp.zeros((slot_count, model_width), jnp.bfloat16),
            (
                jnp.zeros(in_a.shape[2:], jnp.float32),
                jnp.zeros(in_b.shape[2:], jnp.float32),
                jnp.zeros(down_a.shape[2:], jnp.float32),
                jnp.zeros(down_b.shape[2:], jnp.float32),
            ),
        )

    rows_store = jnp.zeros((micro_count, slot_count, model_width), jnp.bfloat16)
    saved_store = (
        jnp.zeros((micro_count, slot_count, 2 * low_rank), jnp.bfloat16),
        jnp.zeros((micro_count, slot_count, hidden_width), jnp.float32),
        jnp.zeros((micro_count, slot_count, hidden_width), jnp.float32),
        jnp.zeros((micro_count, slot_count, hidden_width), jnp.bfloat16),
        jnp.zeros((micro_count, slot_count, low_rank), jnp.bfloat16),
    )
    inputs_store = jnp.zeros((micro_count, tok_rows, model_width), jnp.bfloat16)
    hidden_store = jnp.zeros((micro_count, tok_rows, model_width), jnp.bfloat16)
    incoming = jnp.zeros((tok_rows, model_width), jnp.bfloat16)
    for tick_index in range(tick_count):
        offset = tick_index - section_index
        active = (offset >= 0) & (offset < micro_count)
        micro_index = jnp.clip(offset, 0, micro_count - 1)
        first_input = lax.dynamic_index_in_dim(tokens, micro_index, 0, keepdims=False)
        current = jnp.where(section_index == 0, first_input, incoming)
        routes_micro = lax.dynamic_index_in_dim(routes[0], micro_index, 0, keepdims=False)
        gates_micro = lax.dynamic_index_in_dim(gates[0], micro_index, 0, keepdims=False)
        targets = slot_targets(routes_micro, expert_count, capacity, copy_count)
        normed, inverse = normalize(current, norm_scale)
        placed = (
            jnp.zeros((slot_count, model_width), jnp.bfloat16)
            .at[targets.reshape(-1)]
            .set(jnp.repeat(normed, top_count, axis=0))
        )
        received = send_rows(placed.reshape(peer_count, slot_width, model_width)).reshape(
            slot_count, model_width
        )
        expert_out, saved_state = lax.cond(active, busy_forward, spare_forward, received)
        rows_store = store_slot(rows_store, received, micro_index, active)
        saved_store = tuple(
            (
                store_slot(stored_array, new_value, micro_index, active)
                for stored_array, new_value in zip(saved_store, saved_state)
            )
        )
        returned = return_rows(expert_out.reshape(peer_count, slot_width, model_width)).reshape(
            slot_count, model_width
        )
        picked = returned[targets].astype(jnp.float32)
        mixed_out = (
            current.astype(jnp.float32) + jnp.sum(gates_micro[:, :, None] * picked, axis=1)
        ).astype(jnp.bfloat16)
        inputs_store = store_slot(inputs_store, current, micro_index, active)
        hidden_store = store_slot(hidden_store, mixed_out, micro_index, active)
        if tick_index + 1 < tick_count:
            incoming = shifted(mixed_out, "pipe", 1)
    grad_store = jnp.zeros((micro_count, tok_rows, model_width), jnp.bfloat16)
    totals = (
        jnp.zeros(in_a.shape[2:], jnp.float32),
        jnp.zeros(in_b.shape[2:], jnp.float32),
        jnp.zeros(down_a.shape[2:], jnp.float32),
        jnp.zeros(down_b.shape[2:], jnp.float32),
    )
    incoming_grad = jnp.zeros((tok_rows, model_width), jnp.bfloat16)
    for tick_index in range(tick_count):
        offset = tick_index - (section_count - 1 - section_index)
        active = (offset >= 0) & (offset < micro_count)
        micro_index = jnp.clip(offset, 0, micro_count - 1)
        last_grad = lax.dynamic_index_in_dim(cotangent, micro_index, 0, keepdims=False)
        grad_next = jnp.where(section_index == section_count - 1, last_grad, incoming_grad)
        current = lax.dynamic_index_in_dim(inputs_store, micro_index, 0, keepdims=False)
        routes_micro = lax.dynamic_index_in_dim(routes[0], micro_index, 0, keepdims=False)
        gates_micro = lax.dynamic_index_in_dim(gates[0], micro_index, 0, keepdims=False)
        targets = slot_targets(routes_micro, expert_count, capacity, copy_count)
        normed, inverse = normalize(current, norm_scale)
        grad_slots = (gates_micro[:, :, None] * grad_next.astype(jnp.float32)[:, None, :]).astype(
            jnp.bfloat16
        )
        placed = (
            jnp.zeros((slot_count, model_width), jnp.bfloat16)
            .at[targets.reshape(-1)]
            .set(grad_slots.reshape(-1, model_width))
        )
        received = send_rows(placed.reshape(peer_count, slot_width, model_width)).reshape(
            slot_count, model_width
        )
        slot_rows = lax.dynamic_index_in_dim(rows_store, micro_index, 0, keepdims=False)
        saved_micro = tuple(
            (
                lax.dynamic_index_in_dim(stored_array, micro_index, 0, keepdims=False)
                for stored_array in saved_store
            )
        )
        grad_rows, adapter_grads = lax.cond(
            active, busy_backward, spare_backward, (slot_rows, received, saved_micro)
        )
        totals = tuple((totals[item] + adapter_grads[item] for item in range(4)))
        returned = return_rows(grad_rows.reshape(peer_count, slot_width, model_width)).reshape(
            slot_count, model_width
        )
        grad_norm = jnp.sum(returned[targets].astype(jnp.float32), axis=1)
        grad_in = (
            grad_next.astype(jnp.float32) + normalize_back(grad_norm, current, inverse, norm_scale)
        ).astype(jnp.bfloat16)
        grad_store = store_slot(grad_store, grad_in, micro_index, active)
        if tick_index + 1 < tick_count:
            incoming_grad = shifted(grad_in, "pipe", -1)
    summed = (
        lax.psum(totals[0].astype(jnp.bfloat16), "dp").astype(jnp.float32),
        lax.psum(totals[1].astype(jnp.bfloat16), "dp").astype(jnp.float32),
        lax.psum(totals[2].astype(jnp.bfloat16), "dp").astype(jnp.float32),
        lax.psum(totals[3].astype(jnp.bfloat16), "dp").astype(jnp.float32),
    )
    return (
        hidden_store[None],
        grad_store[None],
        summed[0][None, None],
        summed[1][None, None],
        summed[2][None, None],
        summed[3][None, None],
    )


def solution(mesh):
    placed = (
        P(None, ("expert", "dp"), None),
        P(None, ("expert", "dp"), None),
        P("pipe", None, ("expert", "dp"), None),
        P("pipe", None, ("expert", "dp"), None),
        P("pipe", None),
        P("pipe", "expert", None, None),
        P("pipe", "expert", None, None),
        P("pipe", "expert", None, None),
        P("pipe", "expert", None, None),
        P("pipe", "expert", None, None, None),
        P("pipe", "expert", None, None),
        P("pipe", "expert", None, None),
    )
    return jax.shard_map(
        body,
        mesh=mesh,
        in_specs=placed,
        out_specs=(
            P("pipe", None, ("expert", "dp"), None),
            P("pipe", None, ("expert", "dp"), None),
            P("pipe", "expert", None, None),
            P("pipe", "expert", None, None, None),
            P("pipe", "expert", None, None),
            P("pipe", "expert", None, None),
        ),
        check_vma=False,
    )
```

profile of v0, /device:TPU:1, one launch (start us, length us, event | category | flops | bytes accessed | tf_op | source)
XLA Modules:
  0.0 1172.3 jit_solution(9122193292972573082)
XLA Ops:
  15.2 12.3 %all-to-all-start = ((bf16[32,6,2048]{2,1,0:T(8,128)(2,1)}), bf16[32,6,2048]{2,1,0:T(8,128)(2,1)}, u32[]{:S(2)}, u32[]{:S(2)}) async-start(bf16[32,6,2048]{2,1,0:T(8,128)(2,1)} %reshape.2163), calls=%async_computation | async-start | bytes 2097152 | tf_op jit(solution)/shard_map/all_to_all | solution.py:90
  38.8 14.9 %all-to-all-done = bf16[32,6,2048]{2,1,0:T(8,128)(2,1)} async-done(((bf16[32,6,2048]{2,1,0:T(8,128)(2,1)}), bf16[32,6,2048]{2,1,0:T(8,128)(2,1)}, u32[]{:S(2)}, u32[]{:S(2)}) %all-to-all-start) | async-done | bytes 786464 | tf_op jit(solution)/shard_map/all_to_all | solution.py:90
  53.7 16.8 %conditional.10 = (bf16[192,2048]{1,0:T(8,128)(2,1)}, f32[192,768]{1,0:T(8,128)}, f32[192,768]{1,0:T(8,128)}, bf16[192,768]{1,0:T(8,128)(2,1)}, bf16[192,16]{0,1:T(8,128)(2,1)}, /*index=5*/bf16[192,32]{1,0:T(8,128)(2,1)S(1)}) conditional(s32[]{:T(128)} %convert_element_type.447, () %tuple.108, (bf16[32,6,2048]{2,1,0:T(8,128)(2,1)}, ...), branch_computations={%region_4.5_spmd, %region_5.6_spmd} | conditional | flops 1865819136 | bytes 38379624 | solution.py:223
  83.4 21.3 %all-to-all-done.1 = bf16[32,6,2048]{2,1,0:T(8,128)(2,1)} async-done(((bf16[32,6,2048]{2,1,0:T(8,128)(2,1)}), bf16[32,6,2048]{2,1,0:T(8,128)(2,1)}, u32[]{:S(2)}, u32[]{:S(2)}) %all-to-all-start.1) | async-done | bytes 786464 | tf_op jit(solution)/shard_map/all_to_all | solution.py:94
  142.7 6.9 all-to-all-start.2
  179.9 19.1 %conditional.11 = (bf16[192,2048]{1,0:T(8,128)(2,1)}, f32[192,768]{1,0:T(8,128)}, f32[192,768]{1,0:T(8,128)}, bf16[192,768]{1,0:T(8,128)(2,1)}, bf16[192,16]{0,1:T(8,128)(2,1)}, /*index=5*/bf16[192,32]{1,0:T(8,128)(2,1)}) conditional(s32[]{:T(128)} %convert_element_type.456, () %tuple.110, (bf16[32,6,2048]{2,1,0:T(8,128)(2,1)}, ...), branch_computations={%region_11.12_spmd, %region_12.13_spmd} | conditional | flops 1865819136 | bytes 38428804 | solution.py:223
  201.3 9.3 all-to-all-start.3
  222.6 12.5 %all-to-all-done.3 = bf16[32,6,2048]{2,1,0:T(8,128)(2,1)} async-done(((bf16[32,6,2048]{2,1,0:T(8,128)(2,1)}), bf16[32,6,2048]{2,1,0:T(8,128)(2,1)}, u32[]{:S(2)}, u32[]{:S(2)}) %all-to-all-start.3) | async-done | bytes 786464 | tf_op jit(solution)/shard_map/all_to_all | solution.py:94
  261.2 6.9 all-to-all-start.4
  319.4 9.7 all-to-all-done.5
  341.2 18.2 %collective-permute-start.2 = (bf16[64,2048]{1,0:T(8,128)(2,1)S(1)}, bf16[64,2048]{1,0:T(8,128)(2,1)S(1)}, u32[]{:S(2)}, u32[]{:S(2)}) collective-permute-start(bf16[64,2048]{1,0:T(8,128)(2,1)S(1)} %get-tuple-element.991), channel_id=1, source_target_pairs={{0,64},{64,128},{128,192},{1,65},{65,129},{129,193},{2,66},{66,130... | collective-permute-start | bytes 786440 | tf_op jit(solution)/shard_map/ppermute | solution.py:12
  372.1 7.1 all-to-all-start.6
  408.0 8.0 all-to-all-start.7
  425.2 12.7 %all-to-all-done.7 = bf16[32,6,2048]{2,1,0:T(8,128)(2,1)} async-done(((bf16[32,6,2048]{2,1,0:T(8,128)(2,1)}), bf16[32,6,2048]{2,1,0:T(8,128)(2,1)}, u32[]{:S(2)}, u32[]{:S(2)}) %all-to-all-start.7) | async-done | bytes 786464 | tf_op jit(solution)/shard_map/all_to_all | solution.py:94
  465.3 7.4 all-to-all-start.8
  493.5 7.1 all-to-all-start.10
  527.4 7.2 all-to-all-start.11
  592.6 16.8 %collective-permute-done.4 = bf16[64,2048]{1,0:T(8,128)(2,1)} collective-permute-done((bf16[64,2048]{1,0:T(8,128)(2,1)}, bf16[64,2048]{1,0:T(8,128)(2,1)}, u32[]{:S(2)}, u32[]{:S(2)}) %collective-permute-start.4) | collective-permute-done | bytes 262176 | tf_op jit(solution)/shard_map/ppermute | solution.py:12
  621.1 9.5 all-to-all-start.12
  640.2 11.4 all-to-all-done.12
  730.3 9.3 all-to-all-start.14
  739.6 19.2 %all-to-all-done.14 = bf16[32,6,2048]{2,1,0:T(8,128)(2,1)} async-done(((bf16[32,6,2048]{2,1,0:T(8,128)(2,1)}), bf16[32,6,2048]{2,1,0:T(8,128)(2,1)}, u32[]{:S(2)}, u32[]{:S(2)}) %all-to-all-start.14) | async-done | bytes 786464 | tf_op jit(solution)/shard_map/all_to_all | solution.py:90
  764.6 7.2 all-to-all-start.15
  813.9 58.0 %collective-permute-done.6 = bf16[64,2048]{1,0:T(8,128)(2,1)} collective-permute-done((bf16[64,2048]{1,0:T(8,128)(2,1)}, bf16[64,2048]{1,0:T(8,128)(2,1)}, u32[]{:S(2)}, u32[]{:S(2)}) %collective-permute-start.6) | collective-permute-done | bytes 262176 | tf_op jit(solution)/shard_map/ppermute | solution.py:12
  908.3 21.0 %conditional.18 = (bf16[192,2048]{1,0:T(8,128)(2,1)}, f32[2048,32]{0,1:T(8,128)}, f32[2,16,768]{2,1,0:T(8,128)}, f32[768,16]{0,1:T(8,128)}, f32[16,2048]{1,0:T(8,128)}) conditional(s32[]{:T(128)} %convert_element_type.510, () %tuple.124, (bf16[32,6,2048]{2,1,0:T(8,128)(2,1)}, bf16[768,2048]{1,0:T(8,128)(2,1)}, bf16[16,2048]{1,0:T(8,128)(2,1)S(1)}, ...), branch_computations={%region_63.64_spmd, %region_64.65_spmd} | conditional | flops 1919075328 | bytes 43622020 | solution.py:279
  931.6 9.3 all-to-all-start.17
  964.1 9.5 all-to-all-start.9
  1011.7 9.2 all-to-all-start.18
  1045.3 20.7 %conditional.19 = (bf16[192,2048]{1,0:T(8,128)(2,1)}, f32[2048,32]{0,1:T(8,128)S(1)}, f32[2,16,768]{2,1,0:T(8,128)}, f32[768,16]{0,1:T(8,128)S(1)}, f32[16,2048]{1,0:T(8,128)}) conditional(s32[]{:T(128)} %convert_element_type.518, () %tuple.126, (bf16[32,6,2048]{2,1,0:T(8,128)(2,1)}, bf16[768,2048]{1,0:T(8,128)(2,1)}, ...), branch_computations={%region_71.72_spmd, %region_72.73_spmd} | conditional | flops 1919075328 | bytes 43818656 | solution.py:279
  1068.2 9.1 all-to-all-start.19
  1085.3 36.9 %all-reduce.5.cloned.1.call-done = (bf16[1,1,2,16,768]{4,3,2,1,0:T(8,128)(2,1)}, bf16[1,1,768,16]{2,3,1,0:T(8,128)(2,1)}) async-done(((bf16[1,1,2,16,768]{4,3,2,1,0:T(8,128)(2,1)}, bf16[1,1,768,16]{2,3,1,0:T(8,128)(2,1)}), (bf16[1,1,2,16,768]{4,3,2,1,0:T(8,128)(2,1)}, bf16[1,1,768,16]{2,3,1,0:T(8,128)(2,1)})) %all-reduce.5.cloned.1.call-update) | async-done | bytes 73744 | tf_op jit(solution)/shard_map/psum | solution.py:295
  1125.0 30.7 %all-reduce.7.cloned.1.call-done = (bf16[1,1,2048,32]{2,3,1,0:T(8,128)(2,1)}, bf16[1,1,16,2048]{3,2,1,0:T(8,128)(2,1)}) async-done(((bf16[1,1,2048,32]{2,3,1,0:T(8,128)(2,1)}, bf16[1,1,16,2048]{3,2,1,0:T(8,128)(2,1)}), (bf16[1,1,2048,32]{2,3,1,0:T(8,128)(2,1)}, bf16[1,1,16,2048]{3,2,1,0:T(8,128)(2,1)})) %all-reduce.7.cloned.1.call-update) | async-done | bytes 196624 | tf_op jit(solution)/shard_map/psum | solution.py:294
  (698 shorter events, 783.2 us)
Async XLA Ops:
  15.2 38.5 %copy-start = (bf16[1,1,2048,768]{3,2,1,0:T(8,128)(2,1)S(1)}, bf16[1,1,2048,768]{3,2,1,0:T(8,128)(2,1)}, u32[]{:S(2)}) copy-start(bf16[1,1,2048,768]{3,2,1,0:T(8,128)(2,1)} %param.37) | copy-start | bytes 9437188
  15.2 38.4 %all-to-all-start = ((bf16[32,6,2048]{2,1,0:T(8,128)(2,1)}), bf16[32,6,2048]{2,1,0:T(8,128)(2,1)}, u32[]{:S(2)}, u32[]{:S(2)}) async-start(bf16[32,6,2048]{2,1,0:T(8,128)(2,1)} %reshape.2163), calls=%async_computation | async-start | bytes 2097152 | tf_op jit(solution)/shard_map/all_to_all | solution.py:90
  72.8 32.0 %all-to-all-start.1 = ((bf16[32,6,2048]{2,1,0:T(8,128)(2,1)}), bf16[32,6,2048]{2,1,0:T(8,128)(2,1)}, u32[]{:S(2)}, u32[]{:S(2)}) async-start(bf16[32,6,2048]{2,1,0:T(8,128)(2,1)} %reshape.2164), calls=%async_computation.1 | async-start | bytes 2097152 | tf_op jit(solution)/shard_map/all_to_all | solution.py:94
  116.9 14.3 %collective-permute-start = (bf16[64,2048]{1,0:T(8,128)(2,1)}, bf16[64,2048]{1,0:T(8,128)(2,1)}, u32[]{:S(2)}, u32[]{:S(2)}) collective-permute-start(bf16[64,2048]{1,0:T(8,128)(2,1)} %fusion.228), channel_id=1, source_target_pairs={{0,64},{64,128},{128,192},{1,65},{65,129},{129,193},{2,66},{66,130... | collective-permute-start | bytes 786440 | tf_op jit(solution)/shard_map/ppermute | solution.py:12
  142.7 37.2 %all-to-all-start.2 = ((bf16[32,6,2048]{2,1,0:T(8,128)(2,1)}), bf16[32,6,2048]{2,1,0:T(8,128)(2,1)}, u32[]{:S(2)}, u32[]{:S(2)}) async-start(bf16[32,6,2048]{2,1,0:T(8,128)(2,1)} %reshape.2169), calls=%async_computation.2 | async-start | bytes 2097152 | tf_op jit(solution)/shard_map/all_to_all | solution.py:90
  201.3 33.8 %all-to-all-start.3 = ((bf16[32,6,2048]{2,1,0:T(8,128)(2,1)}), bf16[32,6,2048]{2,1,0:T(8,128)(2,1)}, u32[]{:S(2)}, u32[]{:S(2)}) async-start(bf16[32,6,2048]{2,1,0:T(8,128)(2,1)} %reshape.2170), calls=%async_computation.3 | async-start | bytes 2097152 | tf_op jit(solution)/shard_map/all_to_all | solution.py:94
  247.3 4.6 collective-permute-start.1
  261.2 30.7 %all-to-all-start.4 = ((bf16[32,6,2048]{2,1,0:T(8,128)(2,1)}), bf16[32,6,2048]{2,1,0:T(8,128)(2,1)}, u32[]{:S(2)}, u32[]{:S(2)}) async-start(bf16[32,6,2048]{2,1,0:T(8,128)(2,1)} %reshape.2175), calls=%async_computation.4 | async-start | bytes 2097152 | tf_op jit(solution)/shard_map/all_to_all | solution.py:90
  299.1 30.0 %all-to-all-start.5 = ((bf16[32,6,2048]{2,1,0:T(8,128)(2,1)}), bf16[32,6,2048]{2,1,0:T(8,128)(2,1)}, u32[]{:S(2)}, u32[]{:S(2)}) async-start(bf16[32,6,2048]{2,1,0:T(8,128)(2,1)} %reshape.2176), calls=%async_computation.5 | async-start | bytes 2097152 | tf_op jit(solution)/shard_map/all_to_all | solution.py:94
  341.2 21.5 %collective-permute-start.2 = (bf16[64,2048]{1,0:T(8,128)(2,1)S(1)}, bf16[64,2048]{1,0:T(8,128)(2,1)S(1)}, u32[]{:S(2)}, u32[]{:S(2)}) collective-permute-start(bf16[64,2048]{1,0:T(8,128)(2,1)S(1)} %get-tuple-element.991), channel_id=1, source_target_pairs={{0,64},{64,128},{128,192},{1,65},{65,129},{129,193},{2,66},{66,130... | collective-permute-start | bytes 786440 | tf_op jit(solution)/shard_map/ppermute | solution.py:12
  372.1 28.9 %all-to-all-start.6 = ((bf16[32,6,2048]{2,1,0:T(8,128)(2,1)}), bf16[32,6,2048]{2,1,0:T(8,128)(2,1)}, u32[]{:S(2)}, u32[]{:S(2)}) async-start(bf16[32,6,2048]{2,1,0:T(8,128)(2,1)} %reshape.2181), calls=%async_computation.6 | async-start | bytes 2097152 | tf_op jit(solution)/shard_map/all_to_all | solution.py:90
  408.0 29.9 %all-to-all-start.7 = ((bf16[32,6,2048]{2,1,0:T(8,128)(2,1)}), bf16[32,6,2048]{2,1,0:T(8,128)(2,1)}, u32[]{:S(2)}, u32[]{:S(2)}) async-start(bf16[32,6,2048]{2,1,0:T(8,128)(2,1)} %reshape.2182), calls=%async_computation.7 | async-start | bytes 2097152 | tf_op jit(solution)/shard_map/all_to_all | solution.py:94
  450.1 5.9 collective-permute-start.3
  465.3 28.2 %all-to-all-start.8 = ((bf16[32,6,2048]{2,1,0:T(8,128)(2,1)}), bf16[32,6,2048]{2,1,0:T(8,128)(2,1)}, u32[]{:S(2)}, u32[]{:S(2)}) async-start(bf16[32,6,2048]{2,1,0:T(8,128)(2,1)} %reshape.2187), calls=%async_computation.8 | async-start | bytes 2097152 | tf_op jit(solution)/shard_map/all_to_all | solution.py:90
  493.5 28.0 %all-to-all-start.10 = ((bf16[32,6,2048]{2,1,0:T(8,128)(2,1)}), bf16[32,6,2048]{2,1,0:T(8,128)(2,1)}, u32[]{:S(2)}, u32[]{:S(2)}) async-start(bf16[32,6,2048]{2,1,0:T(8,128)(2,1)} %reshape.2192), calls=%async_computation.10 | async-start | bytes 2097152 | tf_op jit(solution)/shard_map/all_to_all | solution.py:90
  527.4 41.4 %all-to-all-start.11 = ((bf16[32,6,2048]{2,1,0:T(8,128)(2,1)}), bf16[32,6,2048]{2,1,0:T(8,128)(2,1)}, u32[]{:S(2)}, u32[]{:S(2)}) async-start(bf16[32,6,2048]{2,1,0:T(8,128)(2,1)} %reshape.2197), calls=%async_computation.11 | async-start | bytes 2097152 | tf_op jit(solution)/shard_map/all_to_all | solution.py:94
  585.2 24.3 %collective-permute-start.4 = (bf16[64,2048]{1,0:T(8,128)(2,1)}, bf16[64,2048]{1,0:T(8,128)(2,1)}, u32[]{:S(2)}, u32[]{:S(2)}) collective-permute-start(bf16[64,2048]{1,0:T(8,128)(2,1)} %fusion.224), channel_id=1, source_target_pairs={{64,0},{128,64},{192,128},{65,1},{129,65},{193,129},{66,2},{130,66... | collective-permute-start | bytes 786440 | tf_op jit(solution)/shard_map/ppermute | solution.py:12
  621.1 30.5 %all-to-all-start.12 = ((bf16[32,6,2048]{2,1,0:T(8,128)(2,1)}), bf16[32,6,2048]{2,1,0:T(8,128)(2,1)}, u32[]{:S(2)}, u32[]{:S(2)}) async-start(bf16[32,6,2048]{2,1,0:T(8,128)(2,1)} %reshape.2201), calls=%async_computation.12 | async-start | bytes 2097152 | tf_op jit(solution)/shard_map/all_to_all | solution.py:90
  657.6 36.6 %all-to-all-start.13 = ((bf16[32,6,2048]{2,1,0:T(8,128)(2,1)}), bf16[32,6,2048]{2,1,0:T(8,128)(2,1)}, u32[]{:S(2)}, u32[]{:S(2)}) async-start(bf16[32,6,2048]{2,1,0:T(8,128)(2,1)} %reshape.2202), calls=%async_computation.13 | async-start | bytes 2097152 | tf_op jit(solution)/shard_map/all_to_all | solution.py:94
  709.8 8.5 collective-permute-start.5
  730.3 28.5 %all-to-all-start.14 = ((bf16[32,6,2048]{2,1,0:T(8,128)(2,1)}), bf16[32,6,2048]{2,1,0:T(8,128)(2,1)}, u32[]{:S(2)}, u32[]{:S(2)}) async-start(bf16[32,6,2048]{2,1,0:T(8,128)(2,1)} %reshape.2206), calls=%async_computation.14 | async-start | bytes 2097152 | tf_op jit(solution)/shard_map/all_to_all | solution.py:90
  764.6 26.1 %all-to-all-start.15 = ((bf16[32,6,2048]{2,1,0:T(8,128)(2,1)}), bf16[32,6,2048]{2,1,0:T(8,128)(2,1)}, u32[]{:S(2)}, u32[]{:S(2)}) async-start(bf16[32,6,2048]{2,1,0:T(8,128)(2,1)} %reshape.2207), calls=%async_computation.15 | async-start | bytes 2097152 | tf_op jit(solution)/shard_map/all_to_all | solution.py:94
  806.2 65.7 %collective-permute-start.6 = (bf16[64,2048]{1,0:T(8,128)(2,1)}, bf16[64,2048]{1,0:T(8,128)(2,1)}, u32[]{:S(2)}, u32[]{:S(2)}) collective-permute-start(bf16[64,2048]{1,0:T(8,128)(2,1)} %get-tuple-element.967), channel_id=1, source_target_pairs={{64,0},{128,64},{192,128},{65,1},{129,65},{193,129},{66,2},{130,66... | collective-permute-start | bytes 786440 | tf_op jit(solution)/shard_map/ppermute | solution.py:12
  883.6 24.7 %all-to-all-start.16 = ((bf16[32,6,2048]{2,1,0:T(8,128)(2,1)}), bf16[32,6,2048]{2,1,0:T(8,128)(2,1)}, u32[]{:S(2)}, u32[]{:S(2)}) async-start(bf16[32,6,2048]{2,1,0:T(8,128)(2,1)} %reshape.2211), calls=%async_computation.16 | async-start | bytes 2097152 | tf_op jit(solution)/shard_map/all_to_all | solution.py:90
  931.6 32.6 %all-to-all-start.17 = ((bf16[32,6,2048]{2,1,0:T(8,128)(2,1)}), bf16[32,6,2048]{2,1,0:T(8,128)(2,1)}, u32[]{:S(2)}, u32[]{:S(2)}) async-start(bf16[32,6,2048]{2,1,0:T(8,128)(2,1)} %reshape.2212), calls=%async_computation.17 | async-start | bytes 2097152 | tf_op jit(solution)/shard_map/all_to_all | solution.py:94
  964.1 47.6 %all-to-all-start.9 = ((bf16[32,6,2048]{2,1,0:T(8,128)(2,1)}), bf16[32,6,2048]{2,1,0:T(8,128)(2,1)}, u32[]{:S(2)}, u32[]{:S(2)}) async-start(bf16[32,6,2048]{2,1,0:T(8,128)(2,1)} %reshape.2188), calls=%async_computation.9 | async-start | bytes 2097152 | tf_op jit(solution)/shard_map/all_to_all | solution.py:94
  989.2 10.7 collective-permute-start.7
  1011.7 33.5 %all-to-all-start.18 = ((bf16[32,6,2048]{2,1,0:T(8,128)(2,1)}), bf16[32,6,2048]{2,1,0:T(8,128)(2,1)}, u32[]{:S(2)}, u32[]{:S(2)}) async-start(bf16[32,6,2048]{2,1,0:T(8,128)(2,1)} %reshape.2216), calls=%async_computation.18 | async-start | bytes 2097152 | tf_op jit(solution)/shard_map/all_to_all | solution.py:90
  1068.2 90.6 %all-to-all-start.19 = ((bf16[32,6,2048]{2,1,0:T(8,128)(2,1)}), bf16[32,6,2048]{2,1,0:T(8,128)(2,1)S(1)}, u32[]{:S(2)}, u32[]{:S(2)}) async-start(bf16[32,6,2048]{2,1,0:T(8,128)(2,1)} %reshape.2217), calls=%async_computation.19 | async-start | bytes 2097152 | tf_op jit(solution)/shard_map/all_to_all | solution.py:94
  1077.3 44.9 %all-reduce.5.cloned.1.call-start = ((), (), s32[]{:S(2)}) async-start(), calls=%async_computation.20 | async-start | bytes 147456 | tf_op jit(solution)/shard_map/psum | solution.py:295
  1080.7 75.0 %all-reduce.7.cloned.1.call-start = ((), (), s32[]{:S(2)}) async-start(), calls=%async_computation.21 | async-start | bytes 393216 | tf_op jit(solution)/shard_map/psum | solution.py:294
  1085.3 73.7 %copy-start.57 = (s32[1024]{0:T(1024)S(1)}, s32[1024]{0:T(1024)}, u32[]{:S(2)}) copy-start(s32[1024]{0:T(1024)} %pad_clamp_fusion) | copy-start | bytes 12292
  (72 other events, 454.5 us)
Sparse Core Ops, SparseCore 0:
  1081.3 40.8 all-reduce.4
  1125.4 30.2 all-reduce.6
where the time goes:
time: 1190 us; the launch traced here: 1170 us
  local copies, waits for them, and re-layouts  398 us (33%)
  waiting for transfers between devices  287 us (24%)
  other arithmetic  216 us (18%)
  starting transfers between devices  192 us (16%)
  matrix products  62.2 us (5%)
  between operations  15.8 us (1%)
    ppermute x8, waiting for transfers between devices, shifted(): return lax.ppermute(x, axis, pairs)  88.4 us
    all_to_all x10, starting transfers between devices, send_rows(): lax.all_to_all(buffer, 'expert', split_axis=0, concat_axis=0, tiled=True)  82.5 us
    all_to_all x10, starting transfers between devices, return_rows(): lax.all_to_all(buffer, 'expert', split_axis=0, concat_axis=0, tiled=True)  79.8 us
    all_to_all x10, waiting for transfers between devices, send_rows(): lax.all_to_all(buffer, 'expert', split_axis=0, concat_axis=0, tiled=True)  68.6 us
    dynamic_update_slice x43, other arithmetic, store_slot(): lax.dynamic_update_index_in_dim(stored_array, jnp.where(active, new_value...  65.2 us
    all_to_all x10, waiting for transfers between devices, return_rows(): lax.all_to_all(buffer, 'expert', split_axis=0, concat_axis=0, tiled=True)  62.4 us
    dynamic_slice x25, local copies, waits for them, and re-layouts, store_slot(): lax.dynamic_index_in_dim(stored_array, micro_index, 0, keepdims=False)  40 us
    psum x1, waiting for transfers between devices, body(): lax.psum(totals[1].astype(jnp.bfloat16), 'dp').astype(jnp.float32)  36.9 us
  transfers between devices with their start and end apart: 30, of which 21 were waited for; matrix products, arithmetic and copies ran while one was open for 32% of the time, Pallas kernels for 0%

commit v1 on v0

v1 whole, which is shorter than its diff:
```python
import functools

import jax
import jax.numpy as jnp
import numpy as np
from jax import lax
from jax.experimental import pallas as pl
from jax.experimental.pallas import tpu as pltpu
from jax.sharding import PartitionSpec as P

EPS = 1e-06
SLOTS = 6
LANES = 128
F32 = jnp.float32
BF16 = jnp.bfloat16


def dot(left, right):
    return jnp.dot(left, right, preferred_element_type=F32)


def dot_nt(left, right):
    return lax.dot_general(left, right, (((1,), (1,)), ((), ())), preferred_element_type=F32)


def dot_tn(left, right):
    return lax.dot_general(left, right, (((0,), (0,)), ((), ())), preferred_element_type=F32)


def pack(read, out_ref, wide, peers, chunks):
    stride = SLOTS * chunks
    for slot in range(SLOTS):
        for chunk in range(chunks):
            wide[pl.ds(slot * chunks + chunk, peers, stride=stride), :] = read(slot, chunk)
    for peer in range(peers):
        out_ref[peer] = wide[peer * stride : (peer + 1) * stride, :].astype(BF16)


def unpack(in_ref, rows, wide, peers, chunks):
    stride = SLOTS * chunks
    for peer in range(peers):
        wide[peer * stride : (peer + 1) * stride, :] = in_ref[peer].astype(F32)
    for slot in range(SLOTS):
        for chunk in range(chunks):
            rows[slot * peers : (slot + 1) * peers, chunk * LANES : (chunk + 1) * LANES] = wide[
                pl.ds(slot * chunks + chunk, peers, stride=stride), :
            ].astype(BF16)


def tables_kernel(peers, routes, routes_t, gates, gates_t, place, scale_hi, scale_lo, pick, mix_hi, mix_lo):
    micros, rows, _ = routes.shape
    slots = SLOTS * peers
    assert peers & (peers - 1) == 0
    shift = peers.bit_length() - 1
    for micro in range(micros):
        number = lax.broadcasted_iota(jnp.int32, (slots, rows), 0)
        expert, position = number & (peers - 1), (number >> shift).astype(F32)
        first = routes_t[micro, 0:1, :] == expert
        second = routes_t[micro, 1:2, :] == expert
        named = jnp.where(first | second, 1.0, 0.0)
        earlier = lax.broadcasted_iota(jnp.int32, (rows, rows), 0) < lax.broadcasted_iota(
            jnp.int32, (rows, rows), 1
        )
        before = dot(named.astype(BF16), jnp.where(earlier, 1.0, 0.0).astype(BF16))
        chosen = jnp.where(before == position, named, 0.0)
        weight = jnp.where(first, gates_t[micro, 0:1, :], 0.0) + jnp.where(
            second, gates_t[micro, 1:2, :], 0.0
        )
        weight = weight * chosen
        high = weight.astype(BF16)
        place[micro] = chosen.astype(BF16)
        scale_hi[micro] = high
        scale_lo[micro] = (weight - high.astype(F32)).astype(BF16)

        number = lax.broadcasted_iota(jnp.int32, (rows, slots), 1)
        expert, position = number & (peers - 1), (number >> shift).astype(F32)
        first = routes[micro, :, 0:1] == expert
        second = routes[micro, :, 1:2] == expert
        named = jnp.where(first | second, 1.0, 0.0)
        earlier = lax.broadcasted_iota(jnp.int32, (rows, rows), 1) < lax.broadcasted_iota(
            jnp.int32, (rows, rows), 0
        )
        before = dot(jnp.where(earlier, 1.0, 0.0).astype(BF16), named.astype(BF16))
        chosen = jnp.where(before == position, named, 0.0)
        weight = jnp.where(first, gates[micro, :, 0:1], 0.0) + jnp.where(
            second, gates[micro, :, 1:2], 0.0
        )
        weight = weight * chosen
        high = weight.astype(BF16)
        pick[micro] = chosen.astype(BF16)
        mix_hi[micro] = high
        mix_lo[micro] = (weight - high.astype(F32)).astype(BF16)


def choose(refs, which):
    value = refs[0][...]
    for index in range(1, len(refs)):
        value = jnp.where(which == index, refs[index][...], value)
    return value


def dispatch_kernel(dims, kinds, source_count, flags, *refs):
    peers, chunks, base = dims
    sources = refs[:source_count]
    gain, place, scale_hi, scale_lo = refs[source_count : source_count + 4]
    out_ref = refs[source_count + 4]
    wide, rows = refs[-2:]
    is_forward, micro = flags[base], flags[base + 1]
    current = choose(sources, flags[base + 2])
    if source_count > 1:
        refs[source_count + 5][...] = current

    def forward():
        values = current.astype(F32)
        inverse = lax.rsqrt(jnp.mean(values * values, axis=-1, keepdims=True) + EPS)
        rows[...] = dot(place[micro], (values * inverse * gain[...]).astype(BF16))

    def backward():
        rows[...] = dot(scale_hi[micro], current) + dot(scale_lo[micro], current)

    if kinds == "F":
        forward()
    elif kinds == "B":
        backward()
    else:
        pl.when(is_forward == 1)(forward)
        pl.when(is_forward == 0)(backward)
    pack(
        lambda slot, chunk: rows[
            slot * peers : (slot + 1) * peers, chunk * LANES : (chunk + 1) * LANES
        ],
        out_ref,
        wide,
        peers,
        chunks,
    )


def combine_kernel(dims, kinds, section_count, grad_count, flags, *refs):
    peers, chunks, base = dims
    returned = refs[0]
    sections = refs[1 : 1 + section_count]
    grads = refs[1 + section_count : 1 + section_count + grad_count]
    gain, pick, mix_hi, mix_lo, out_ref, wide, rows = refs[1 + section_count + grad_count :]
    is_forward, micro = flags[base], flags[base + 1]
    unpack(returned, rows, wide, peers, chunks)

    def forward():
        mixed = dot(mix_hi[micro], rows[...]) + dot(mix_lo[micro], rows[...])
        out_ref[...] = (choose(sections, flags[base + 2]).astype(F32) + mixed).astype(BF16)

    def backward():
        section_in = choose(sections, flags[base + 2]).astype(F32)
        grad_next = choose(grads, flags[base + 3]).astype(F32)
        inverse = lax.rsqrt(jnp.mean(section_in * section_in, axis=-1, keepdims=True) + EPS)
        scaled = dot(pick[micro], rows[...]) * gain[...]
        normed = section_in * inverse
        shared = jnp.mean(scaled * normed, axis=-1, keepdims=True)
        out_ref[...] = (grad_next + inverse * (scaled - normed * shared)).astype(BF16)

    if kinds == "F":
        forward()
    elif kinds == "B":
        backward()
    else:
        pl.when(is_forward == 1)(forward)
        pl.when(is_forward == 0)(backward)


def forward_kernel(dims, has_store, received, w_gate, w_up, w_down, in_a, in_b, down_a, down_b, *refs):
    peers, chunks, low_rank = dims
    sent, rows, low_in, gate_pre, up_pre, wide, total, low_total = refs[4 * has_store :]
    step = pl.program_id(0)

    @pl.when(step == 0)
    def _():
        unpack(received, rows.at[0], wide, peers, chunks)
        low_in[0] = dot_nt(rows[0], in_a[...]).astype(BF16)

    slot_rows, low = rows[0], low_in[0]
    gate = dot(slot_rows, w_gate[...]) + dot(low[:, :low_rank], in_b[0])
    up = dot(slot_rows, w_up[...]) + dot(low[:, low_rank:], in_b[1])
    gate_pre[0] = gate
    up_pre[0] = up
    activated = (gate * jax.nn.sigmoid(gate) * up).astype(BF16)
    low_part = dot_nt(activated, down_a[...])
    part = dot(activated, w_down[...])

    @pl.when(step == 0)
    def _():
        total[...] = part
        low_total[...] = low_part

    @pl.when(step > 0)
    def _():
        total[...] += part
        low_total[...] += low_part

    @pl.when(step == pl.num_programs(0) - 1)
    def _():
        total[...] += dot(low_total[...].astype(BF16), down_b[...])
        pack(
            lambda slot, chunk: total[
                slot * peers : (slot + 1) * peers, chunk * LANES : (chunk + 1) * LANES
            ],
            sent,
            wide,
            peers,
            chunks,
        )


def backward_kernel(dims, received_count, has_other, flags, *refs):
    peers, chunks, low_rank, base = dims
    received = refs[:received_count]
    other = refs[received_count]
    refs = refs[received_count + has_other :]
    (rows, low_in, gate_pre, up_pre, w_gate, w_up, w_down, in_a, in_b, down_a, down_b) = refs[:11]
    (sent, grad_in_a, grad_in_b, grad_down_a, grad_down_b) = refs[11:16]
    (wide, grad_out, grad_low_down, total, low_total, grad_low_in) = refs[16:]
    step = pl.program_id(0)
    last = step == pl.num_programs(0) - 1
    active = flags[base] == 1

    @pl.when(active)
    def _():
        @pl.when(step == 0)
        def _():
            if received_count == 1:
                unpack(received[0], grad_out, wide, peers, chunks)
            else:
                for index in range(received_count):

                    @pl.when(flags[base + 2] == index)
                    def _():
                        unpack(received[index], grad_out, wide, peers, chunks)

            grad_low_down[...] = dot_nt(grad_out[...], down_b[...]).astype(BF16)

        low = low_in[0]
        gate, up = gate_pre[0], up_pre[0]
        sigmoid = jax.nn.sigmoid(gate)
        silu = gate * sigmoid
        activated = (silu * up).astype(BF16)
        grad_act = dot_nt(grad_out[...], w_down[...]) + dot(grad_low_down[...], down_a[...])
        grad_gate = (grad_act * up * sigmoid * (1.0 + gate * (1.0 - sigmoid))).astype(BF16)
        grad_up = (grad_act * silu).astype(BF16)
        grad_in_b[0] = dot_tn(low[:, :low_rank], grad_gate)
        grad_in_b[1] = dot_tn(low[:, low_rank:], grad_up)
        grad_down_a[...] = dot_tn(grad_low_down[...], activated)
        low_part = dot_nt(activated, down_a[...])
        in_part = jnp.concatenate([dot_nt(grad_gate, in_b[0]), dot_nt(grad_up, in_b[1])], axis=1)
        part = dot_nt(grad_gate, w_gate[...]) + dot_nt(grad_up, w_up[...])

        @pl.when(step == 0)
        def _():
            total[...] = part
            low_total[...] = low_part
            grad_low_in[...] = in_part

        @pl.when(step > 0)
        def _():
            total[...] += part
            low_total[...] += low_part
            grad_low_in[...] += in_part

        @pl.when(last)
        def _():
            low_grad = grad_low_in[...].astype(BF16)
            total[...] += dot(low_grad, in_a[...])
            pack(
                lambda slot, chunk: total[
                    slot * peers : (slot + 1) * peers, chunk * LANES : (chunk + 1) * LANES
                ],
                sent,
                wide,
                peers,
                chunks,
            )
            grad_in_a[...] = dot_tn(low_grad, rows[0])
            grad_down_b[...] = dot_tn(low_total[...].astype(BF16), grad_out[...])

    if has_other:

        @pl.when(jnp.logical_not(active) & last)
        def _():
            sent[...] = other[...]


def params(megabytes):
    return pltpu.CompilerParams(vmem_limit_bytes=megabytes * 1024 * 1024)


def whole(shape):
    zeros = (0,) * len(shape)
    return pl.BlockSpec(shape, lambda *_: zeros)


def rank_flags(sections, micros):
    assert sections == 4 and micros == 2
    last = sections - 1
    ticks = 2 * sections
    table = np.zeros((sections, ticks, 12), np.int32)
    for rank in range(sections):
        for tick in range(ticks):
            row = table[rank, tick]
            forward = tick - rank if tick - rank in (0, 1) else None
            backward = tick - (2 * last - rank)
            backward = backward if backward in (0, 1) else None
            if forward is not None:
                row[0:2] = 1, forward
            elif backward is not None:
                row[0:2] = 0, backward
            elif rank == last and tick < 2:
                row[0:2] = 0, tick
            if tick == 0:
                row[2] = 1 if rank == last else 0
            elif tick == 1:
                row[2] = 2 if rank == last else (0 if rank == 0 else 1)
            if backward is not None:
                row[4:6] = 1, rank + backward
                row[6] = 0 if rank == last else 1
                row[8:10] = 0, backward
            elif forward is not None:
                row[8:10] = 1, forward
            elif rank == last and tick in (5, 6):
                row[8:10] = 1, tick - 5
            if tick == 4:
                row[10:12] = (0, 0) if rank == last else (1, 1)
            elif tick == 5:
                row[10] = 1 if rank == 1 else 0
            elif tick == 6:
                row[10] = {1: 0, 0: 1, 3: 2}.get(rank, 0)
    return table.reshape(sections, -1)


def body(
    tokens, cotangent, routes, gates, norm_gain, w_gate, w_up, w_down, in_a, in_b, down_a, down_b
):
    section_index = lax.axis_index("pipe")
    sections = lax.axis_size("pipe")
    peers = lax.axis_size("expert")
    micros, tok_rows, model = tokens.shape
    hidden_width = w_gate.shape[3]
    low_rank = down_a.shape[3]
    slots = SLOTS * peers
    chunks = model // LANES
    ticks = 2 * sections
    forward_ticks = sections + micros - 1
    block = hidden_width // 3
    flags = lax.dynamic_index_in_dim(
        jnp.asarray(rank_flags(sections, micros)), section_index, 0, keepdims=False
    )
    w_gate, w_up, w_down = w_gate[0, 0], w_up[0, 0], w_down[0, 0]
    in_a, in_b, down_a, down_b = in_a[0, 0].T, in_b[0, 0], down_a[0, 0].T, down_b[0, 0]
    buffer = jax.ShapeDtypeStruct((peers, SLOTS * chunks, LANES), BF16)
    block_rows = jax.ShapeDtypeStruct((tok_rows, model), BF16)
    wide = pltpu.VMEM((peers * SLOTS * chunks, LANES), F32)

    routes, gates = routes[0], gates[0]
    table_in = jax.ShapeDtypeStruct((micros, slots, tok_rows), BF16)
    table_out = jax.ShapeDtypeStruct((micros, tok_rows, slots), BF16)
    place, scale_hi, scale_lo, pick, mix_hi, mix_lo = pl.pallas_call(
        functools.partial(tables_kernel, peers),
        out_shape=[table_in] * 3 + [table_out] * 3,
        name="tables",
    )(routes, routes.transpose(0, 2, 1), gates, gates.transpose(0, 2, 1))

    def exchange(rows):
        return lax.all_to_all(rows, "expert", split_axis=0, concat_axis=0, tiled=True)

    def dispatch(tick, kinds, sources):
        arrays = [source if source.ndim == 2 else source for source in sources]
        specs = [
            whole(source.shape)
            if source.ndim == 2
            else pl.BlockSpec((pl.squeezed,) + source.shape[1:], lambda *_, t=tick: (t, 0, 0))
            for source in sources
        ]
        single = len(sources) == 1
        operands = arrays + [norm_gain, place, scale_hi, scale_lo]
        specs += [whole(x.shape) for x in operands[len(arrays) :]]
        result = pl.pallas_call(
            functools.partial(dispatch_kernel, (peers, chunks, tick * 12), kinds, len(sources)),
            out_shape=[buffer] if single else [buffer, block_rows],
            grid_spec=pltpu.PrefetchScalarGridSpec(
                num_scalar_prefetch=1,
                grid=(1,),
                in_specs=specs,
                out_specs=[whole(buffer.shape)] + ([] if single else [whole(block_rows.shape)]),
                scratch_shapes=[wide, pltpu.VMEM((slots, model), F32)],
            ),
            compiler_params=params(24),
            name="dispatch",
        )(flags, *operands)
        return result[0], sources[0] if single else result[1]

    def combine(tick, kinds, returned, section_inputs, grads):
        operands = [returned] + list(section_inputs)
        specs = [whole(x.shape) for x in operands]
        for grad in grads:
            operands.append(grad)
            specs.append(
                whole(grad.shape)
                if grad.ndim == 2
                else pl.BlockSpec(
                    (pl.squeezed,) + grad.shape[1:], lambda *_, m=tick - 3: (m, 0, 0)
                )
            )
        more = [norm_gain, pick, mix_hi, mix_lo]
        return pl.pallas_call(
            functools.partial(
                combine_kernel,
                (peers, chunks, tick * 12 + 8),
                kinds,
                len(section_inputs),
                len(grads),
            ),
            out_shape=block_rows,
            grid_spec=pltpu.PrefetchScalarGridSpec(
                num_scalar_prefetch=1,
                grid=(1,),
                in_specs=specs + [whole(x.shape) for x in more],
                out_specs=whole(block_rows.shape),
                scratch_shapes=[wide, pltpu.VMEM((slots, model), BF16)],
            ),
            compiler_params=params(24),
            name="combine",
        )(flags, *operands, *more)

    weights = (w_gate, w_up, w_down, in_a, in_b, down_a, down_b)
    weight_specs = [
        pl.BlockSpec((model, block), lambda f, *_: (0, f)),
        pl.BlockSpec((model, block), lambda f, *_: (0, f)),
        pl.BlockSpec((block, model), lambda f, *_: (f, 0)),
        whole(in_a.shape),
        pl.BlockSpec((2, low_rank, block), lambda f, *_: (0, 0, f)),
        pl.BlockSpec((low_rank, block), lambda f, *_: (0, f)),
        whole(down_b.shape),
    ]
    state_shapes = [
        jax.ShapeDtypeStruct((forward_ticks, slots, model), BF16),
        jax.ShapeDtypeStruct((forward_ticks, slots, 2 * low_rank), BF16),
        jax.ShapeDtypeStruct((forward_ticks, slots, hidden_width), F32),
        jax.ShapeDtypeStruct((forward_ticks, slots, hidden_width), F32),
    ]

    def state_specs(slot_of):
        return [
            pl.BlockSpec((1, slots, model), lambda f, *s: (slot_of(s), 0, 0)),
            pl.BlockSpec((1, slots, 2 * low_rank), lambda f, *s: (slot_of(s), 0, 0)),
            pl.BlockSpec((1, slots, block), lambda f, *s: (slot_of(s), 0, f)),
            pl.BlockSpec((1, slots, block), lambda f, *s: (slot_of(s), 0, f)),
        ]

    def expert_forward(tick, received, state):
        has_store = state is not None
        result = pl.pallas_call(
            functools.partial(forward_kernel, (peers, chunks, low_rank), has_store),
            out_shape=[buffer] + state_shapes,
            grid=(hidden_width // block,),
            in_specs=[whole(buffer.shape)]
            + weight_specs
            + ([pl.BlockSpec(memory_space=pl.ANY)] * 4 if has_store else []),
            out_specs=[whole(buffer.shape)] + state_specs(lambda s: tick),
            scratch_shapes=[
                wide,
                pltpu.VMEM((slots, model), F32),
                pltpu.VMEM((slots, low_rank), F32),
            ],
            input_output_aliases={8: 1, 9: 2, 10: 3, 11: 4} if has_store else {},
            compiler_params=params(40),
            name="expert_forward",
        )(received, *weights, *(state if has_store else ()))
        return result[0], result[1:]

    def expert_backward(tick, received, other, state):
        base = tick * 12 + 4
        others = [] if other is None else [other]
        return pl.pallas_call(
            functools.partial(
                backward_kernel, (peers, chunks, low_rank, base), len(received), len(others)
            ),
            out_shape=[
                buffer,
                jax.ShapeDtypeStruct((2 * low_rank, model), F32),
                jax.ShapeDtypeStruct((2, low_rank, hidden_width), F32),
                jax.ShapeDtypeStruct((low_rank, hidden_width), F32),
                jax.ShapeDtypeStruct((low_rank, model), F32),
            ],
            grid_spec=pltpu.PrefetchScalarGridSpec(
                num_scalar_prefetch=1,
                grid=(hidden_width // block,),
                in_specs=[whole(buffer.shape)] * (len(received) + len(others))
                + state_specs(lambda s: s[0][base + 1])
                + weight_specs,
                out_specs=[
                    whole(buffer.shape),
                    whole((2 * low_rank, model)),
                    pl.BlockSpec((2, low_rank, block), lambda f, *_: (0, 0, f)),
                    pl.BlockSpec((low_rank, block), lambda f, *_: (0, f)),
                    whole((low_rank, model)),
                ],
                scratch_shapes=[
                    wide,
                    pltpu.VMEM((slots, model), BF16),
                    pltpu.VMEM((slots, low_rank), BF16),
                    pltpu.VMEM((slots, model), F32),
                    pltpu.VMEM((slots, low_rank), F32),
                    pltpu.VMEM((slots, 2 * low_rank), F32),
                ],
            ),
            compiler_params=params(40),
            name="expert_backward",
        )(flags, *received, *others, *state, *weights)

    hops = [
        [(0, 1)],
        [(1, 2), (0, 1)],
        [(2, 3), (1, 2)],
        [(2, 3), (3, 2)],
        [(2, 1), (3, 2)],
        [(1, 0), (2, 1)],
        [(1, 0)],
    ]
    inputs, got, sent, mixed, adapter = {}, {}, {}, {}, {}
    state = None
    for tick in range(ticks):
        if tick == 0:
            sources = [tokens, cotangent]
        elif tick == 1:
            sources = [tokens, incoming, cotangent]
        else:
            sources = [incoming]
        kinds = {0: "FB", 1: "FB", 2: "F", 3: "F", 4: "FB"}.get(tick, "B")
        placed, inputs[tick] = dispatch(tick, kinds, sources)
        got[tick] = exchange(placed)
        if tick < forward_ticks:
            sent[tick], state = expert_forward(tick, got[tick], state)
            answer = sent[tick]
        if tick >= 3:
            received = [got[index] for index in {3: (0,), 4: (1, 4)}.get(tick, (tick,))]
            other = sent[{3: 3, 5: 3, 6: 4}[tick]] if tick in (3, 5, 6) else None
            answer, *adapter[tick] = expert_backward(tick, received, other, state)
        returned = exchange(answer)
        section_inputs = {4: (4, 2), 5: (3, 1), 6: (2, 0, 4), 7: (1,)}.get(tick, (tick,))
        grads = {3: [cotangent], 4: [cotangent, inputs[tick]]}.get(
            tick, [inputs[tick]] if tick > 4 else []
        )
        kinds = "F" if tick < 3 else "B" if tick in (4, 7) else "FB"
        mixed[tick] = combine(
            tick, kinds, returned, [inputs[index] for index in section_inputs], grads
        )
        if tick < ticks - 1:
            incoming = lax.ppermute(mixed[tick], "pipe", hops[tick])

    def by_rank(choices):
        value = choices[0]
        for rank in range(1, sections):
            value = jnp.where(section_index == rank, choices[rank], value)
        return value

    hidden = jnp.stack(
        [by_rank([mixed[m], mixed[1 + m], mixed[2 + m], mixed[5 + m]]) for m in range(micros)]
    )
    input_grads = jnp.stack([by_rank([mixed[6 - r + m] for r in range(4)]) for m in range(micros)])

    def summed(item):
        total = by_rank([adapter[6 - r][item] + adapter[7 - r][item] for r in range(4)]).astype(BF16)
        across = lax.ppermute(total, "dp", [(0, 1), (1, 0)])
        return total.astype(F32) + across.astype(F32)

    return (
        hidden[None],
        input_grads[None],
        summed(0).T[None, None],
        summed(1)[None, None],
        summed(2).T[None, None],
        summed(3)[None, None],
    )


def solution(mesh):
    placed = (
        P(None, ("expert", "dp"), None),
        P(None, ("expert", "dp"), None),
        P("pipe", None, ("expert", "dp"), None),
        P("pipe", None, ("expert", "dp"), None),
        P("pipe", None),
        P("pipe", "expert", None, None),
        P("pipe", "expert", None, None),
        P("pipe", "expert", None, None),
        P("pipe", "expert", None, None),
        P("pipe", "expert", None, None, None),
        P("pipe", "expert", None, None),
        P("pipe", "expert", None, None),
    )
    return jax.shard_map(
        body,
        mesh=mesh,
        in_specs=placed,
        out_specs=(
            P("pipe", None, ("expert", "dp"), None),
            P("pipe", None, ("expert", "dp"), None),
            P("pipe", "expert", None, None),
            P("pipe", "expert", None, None, None),
            P("pipe", "expert", None, None),
            P("pipe", "expert", None, None),
        ),
        check_vma=False,
    )
```

time: 1190 us -> 618 us (0.52)
  local copies, waits for them, and re-layouts: 398 us -> 27.8 us
  blocking collectives: 0 us -> 343 us
  waiting for transfers between devices: 287 us -> 73.3 us
  other arithmetic: 216 us -> 6.96 us
  starting transfers between devices: 192 us -> 40.1 us
  Pallas kernels: 0 us -> 115 us
  matrix products: 62.2 us -> 0 us
  between operations: 15.8 us -> 1.67 us
    all_to_all x0 -> x14, blocking collectives: none -> 343 us  [exchange(): lax.all_to_all(rows, 'expert', split_axis=0, concat_axis=0, tiled=True)]
    all_to_all x20 -> x2, starting transfers between devices: 162 us -> 9.68 us  [exchange(): lax.all_to_all(rows, 'expert', split_axis=0, concat_axis=0, tiled=True)]
    pallas_call x0 -> x27, Pallas kernels: none -> 115 us  [the longest x5 42 us: expert_forward(): pl.pallas_call(functools.partial(forward_kernel, (peers, chunks, low_rank...]
    all_to_all x20 -> x2, waiting for transfers between devices: 131 us -> 30.3 us  [exchange(): lax.all_to_all(rows, 'expert', split_axis=0, concat_axis=0, tiled=True)]
    reshape x53 -> x0, local copies, waits for them, and re-layouts: 97.9 us -> none  [the longest x10 21.3 us: body(): placed.reshape(peer_count, slot_width, model_width)]
    psum x2 -> x0, waiting for transfers between devices: 67.5 us -> none  [the longest x1 36.9 us: body(): lax.psum(totals[1].astype(jnp.bfloat16), 'dp').astype(jnp.float32)]
    dynamic_update_slice x43 -> x0, other arithmetic: 65.2 us -> none  [store_slot(): lax.dynamic_update_index_in_dim(stored_array, jnp.where(active, new_value...]
    dot_general x42 -> x0, matrix products: 62.2 us -> none  [the longest x16 20.5 us: times_transposed(): lax.dot_general(left, right, (((1,), (1,)), ((), ())), preferred_element_...]
  transfers between devices with their start and end apart: 30 -> 13, of which waited for: 21 -> 6; matrix products, arithmetic and copies ran while one was open for 32% -> 1% of each run, Pallas kernels for 0% -> 0%
where the time goes in v1:
time: 618 us; the launch traced here: 608 us
  blocking collectives  343 us (56%)
  Pallas kernels  115 us (19%)
  waiting for transfers between devices  73.3 us (12%)
  starting transfers between devices  40.1 us (6%)
  local copies, waits for them, and re-layouts  27.8 us (4%)
  other arithmetic  6.96 us (1%)
    all_to_all x14, blocking collectives, exchange(): lax.all_to_all(rows, 'expert', split_axis=0, concat_axis=0, tiled=True)  343 us
    ppermute x7, waiting for transfers between devices, body(): incoming = lax.ppermute(mixed[tick], 'pipe', hops[tick])  43.1 us
    pallas_call x5, Pallas kernels, expert_forward(): pl.pallas_call(functools.partial(forward_kernel, (peers, chunks, low_rank...  42 us
    pallas_call x5, Pallas kernels, expert_backward(): pl.pallas_call(functools.partial(backward_kernel, (peers, chunks, low_ran...  37.7 us
    all_to_all x2, waiting for transfers between devices, exchange(): lax.all_to_all(rows, 'expert', split_axis=0, concat_axis=0, tiled=True)  30.3 us
    unnamed x172, local copies, waits for them, and re-layouts  24.2 us
    ppermute x4, starting transfers between devices, summed(): across = lax.ppermute(total, 'dp', [(0, 1), (1, 0)])  18.4 us
    pallas_call x8, Pallas kernels, dispatch(): pl.pallas_call(functools.partial(dispatch_kernel, (peers, chunks, tick *...  17.4 us
  transfers between devices with their start and end apart: 13, of which 6 were waited for; matrix products, arithmetic and copies ran while one was open for 1% of the time, Pallas kernels for 0%

profile of v1, /device:TPU:1, one launch (start us, length us, event | category | flops | bytes accessed | tf_op | source)
XLA Modules:
  0.0 607.8 jit_solution(5093166168454589024)
XLA Ops:
  14.4 32.7 %all_to_all.80.received.refs_0_ = bf16[32,96,128]{2,1,0:T(8,128)(2,1)S(1)} all-to-all(bf16[32,96,128]{2,1,0:T(8,128)(2,1)S(1)} %get-tuple-element.69), channel_id=1, replica_groups=mesh['pipe'=4,'expert'=32,'dp'=2] {'expert'}, dimensions={0} | all-to-all | bytes 1572864 | tf_op jit(solution)/shard_map/all_to_all | solution.py:370
  50.7 8.4 %expert_forward.5 = (bf16[32,96,128]{2,1,0:T(8,128)(2,1)S(1)}, bf16[5,192,2048]{2,1,0:T(8,128)(2,1)}, bf16[5,192,32]{2,1,0:T(8,128)(2,1)S(1)}, f32[5,192,768]{2,1,0:T(8,128)S(1)}, f32[5,192,768]{2,1,0:T(8,128)S(1)}) custom-call(bf16[32,96,128]{2,1,0:T(8,128)(2,1)S(1)} %all_to_all.80.received.refs_0_, bf16[2048,768]{1,0:T(8,128)(2,1)S(1)} %bitcast.43, ...), custom_call_target="tpu_custom_call" | custom-call | tf_op jit(solution)/shard_map/expert_forward/pallas_call | solution.py:458
  59.2 25.5 %all_to_all.81.refs_0_ = bf16[32,96,128]{2,1,0:T(8,128)(2,1)S(1)} all-to-all(bf16[32,96,128]{2,1,0:T(8,128)(2,1)S(1)} %get-tuple-element.70), channel_id=1, replica_groups=mesh['pipe'=4,'expert'=32,'dp'=2] {'expert'}, dimensions={0} | all-to-all | bytes 1572864 | tf_op jit(solution)/shard_map/all_to_all | solution.py:370
  95.9 27.0 %all_to_all.82.received.refs_0_ = bf16[32,96,128]{2,1,0:T(8,128)(2,1)S(1)} all-to-all(bf16[32,96,128]{2,1,0:T(8,128)(2,1)S(1)} %get-tuple-element.75), channel_id=1, replica_groups=mesh['pipe'=4,'expert'=32,'dp'=2] {'expert'}, dimensions={0} | all-to-all | bytes 1572864 | tf_op jit(solution)/shard_map/all_to_all | solution.py:370
  123.0 8.4 %expert_forward.6 = (bf16[32,96,128]{2,1,0:T(8,128)(2,1)S(1)}, bf16[5,192,2048]{2,1,0:T(8,128)(2,1)}, bf16[5,192,32]{2,1,0:T(8,128)(2,1)S(1)}, f32[5,192,768]{2,1,0:T(8,128)S(1)}, f32[5,192,768]{2,1,0:T(8,128)S(1)}) custom-call(bf16[32,96,128]{2,1,0:T(8,128)(2,1)S(1)} %all_to_all.82.receive, ...), custom_call_target="tpu_custom_call", output_to_operand_aliasing={{1}: (8, {}), {2}: (9, {}), {3}: (10, {}), {4}: (11, {})} | custom-call | tf_op jit(solution)/shard_map/expert_forward/pallas_call | solution.py:458
  131.4 24.6 %all_to_all.83.refs_0_ = bf16[32,96,128]{2,1,0:T(8,128)(2,1)S(1)} all-to-all(bf16[32,96,128]{2,1,0:T(8,128)(2,1)S(1)} %get-tuple-element.80), channel_id=1, replica_groups=mesh['pipe'=4,'expert'=32,'dp'=2] {'expert'}, dimensions={0} | all-to-all | bytes 1572864 | tf_op jit(solution)/shard_map/all_to_all | solution.py:370
  157.9 4.1 collective-permute-start.1
  167.2 24.2 %all_to_all.84.received = bf16[32,96,128]{2,1,0:T(8,128)(2,1)S(1)} all-to-all(bf16[32,96,128]{2,1,0:T(8,128)(2,1)S(1)} %dispatch.10), channel_id=1, replica_groups=mesh['pipe'=4,'expert'=32,'dp'=2] {'expert'}, dimensions={0} | all-to-all | bytes 1572864 | tf_op jit(solution)/shard_map/all_to_all | solution.py:370
  191.4 8.4 %expert_forward.7 = (bf16[32,96,128]{2,1,0:T(8,128)(2,1)S(1)}, bf16[5,192,2048]{2,1,0:T(8,128)(2,1)}, bf16[5,192,32]{2,1,0:T(8,128)(2,1)S(1)}, f32[5,192,768]{2,1,0:T(8,128)S(1)}, f32[5,192,768]{2,1,0:T(8,128)S(1)}) custom-call(bf16[32,96,128]{2,1,0:T(8,128)(2,1)S(1)} %all_to_all.84.receive, ...), custom_call_target="tpu_custom_call", output_to_operand_aliasing={{1}: (8, {}), {2}: (9, {}), {3}: (10, {}), {4}: (11, {})} | custom-call | tf_op jit(solution)/shard_map/expert_forward/pallas_call | solution.py:458
  199.8 24.7 %all_to_all.85.refs_0_ = bf16[32,96,128]{2,1,0:T(8,128)(2,1)S(1)} all-to-all(bf16[32,96,128]{2,1,0:T(8,128)(2,1)S(1)} %get-tuple-element.86), channel_id=1, replica_groups=mesh['pipe'=4,'expert'=32,'dp'=2] {'expert'}, dimensions={0} | all-to-all | bytes 1572864 | tf_op jit(solution)/shard_map/all_to_all | solution.py:370
  229.0 24.2 %all_to_all.86.received = bf16[32,96,128]{2,1,0:T(8,128)(2,1)S(1)} all-to-all(bf16[32,96,128]{2,1,0:T(8,128)(2,1)S(1)} %dispatch.11), channel_id=1, replica_groups=mesh['pipe'=4,'expert'=32,'dp'=2] {'expert'}, dimensions={0} | all-to-all | bytes 1572864 | tf_op jit(solution)/shard_map/all_to_all | solution.py:370
  253.3 8.4 %expert_forward.8 = (bf16[32,96,128]{2,1,0:T(8,128)(2,1)S(1)}, bf16[5,192,2048]{2,1,0:T(8,128)(2,1)}, bf16[5,192,32]{2,1,0:T(8,128)(2,1)S(1)}, f32[5,192,768]{2,1,0:T(8,128)S(1)}, f32[5,192,768]{2,1,0:T(8,128)S(1)}) custom-call(bf16[32,96,128]{2,1,0:T(8,128)(2,1)S(1)} %all_to_all.86.receive, ...), custom_call_target="tpu_custom_call", output_to_operand_aliasing={{1}: (8, {}), {2}: (9, {}), {3}: (10, {}), {4}: (11, {})} | custom-call | tf_op jit(solution)/shard_map/expert_forward/pallas_call | solution.py:458
  261.7 4.4 expert_backward.5
  268.6 24.5 %all_to_all.87.refs_0_ = bf16[32,96,128]{2,1,0:T(8,128)(2,1)S(1)} all-to-all(bf16[32,96,128]{2,1,0:T(8,128)(2,1)S(1)} %get-tuple-element.96), channel_id=1, replica_groups=mesh['pipe'=4,'expert'=32,'dp'=2] {'expert'}, dimensions={0} | all-to-all | bytes 1572864 | tf_op jit(solution)/shard_map/all_to_all | solution.py:370
  298.5 24.3 %all_to_all.88.received.refs_1_ = bf16[32,96,128]{2,1,0:T(8,128)(2,1)S(1)} all-to-all(bf16[32,96,128]{2,1,0:T(8,128)(2,1)S(1)} %dispatch.12), channel_id=1, replica_groups=mesh['pipe'=4,'expert'=32,'dp'=2] {'expert'}, dimensions={0} | all-to-all | bytes 1572864 | tf_op jit(solution)/shard_map/all_to_all | solution.py:370
  322.8 8.4 %expert_forward.9 = (bf16[32,96,128]{2,1,0:T(8,128)(2,1)S(1)}, bf16[5,192,2048]{2,1,0:T(8,128)(2,1)}, bf16[5,192,32]{2,1,0:T(8,128)(2,1)S(1)}, f32[5,192,768]{2,1,0:T(8,128)S(1)}, f32[5,192,768]{2,1,0:T(8,128)S(1)}) custom-call(bf16[32,96,128]{2,1,0:T(8,128)(2,1)S(1)} %all_to_all.88.receive, ...), custom_call_target="tpu_custom_call", output_to_operand_aliasing={{1}: (8, {}), {2}: (9, {}), {3}: (10, {}), {4}: (11, {})} | custom-call | tf_op jit(solution)/shard_map/expert_forward/pallas_call | solution.py:458
  331.2 5.7 expert_backward.6
  338.9 24.1 %all_to_all.89.refs_0_ = bf16[32,96,128]{2,1,0:T(8,128)(2,1)S(1)} all-to-all(bf16[32,96,128]{2,1,0:T(8,128)(2,1)S(1)} %get-tuple-element.101), channel_id=1, replica_groups=mesh['pipe'=4,'expert'=32,'dp'=2] {'expert'}, dimensions={0} | all-to-all | bytes 1572864 | tf_op jit(solution)/shard_map/all_to_all | solution.py:370
  367.7 24.0 %all_to_all.90.refs_0_ = bf16[32,96,128]{2,1,0:T(8,128)(2,1)S(1)} all-to-all(bf16[32,96,128]{2,1,0:T(8,128)(2,1)S(1)} %dispatch.13), channel_id=1, replica_groups=mesh['pipe'=4,'expert'=32,'dp'=2] {'expert'}, dimensions={0} | all-to-all | bytes 1572864 | tf_op jit(solution)/shard_map/all_to_all | solution.py:370
  391.7 4.4 expert_backward.7
  396.8 23.9 %all_to_all.91.refs_0_ = bf16[32,96,128]{2,1,0:T(8,128)(2,1)S(1)} all-to-all(bf16[32,96,128]{2,1,0:T(8,128)(2,1)S(1)} %get-tuple-element.102), channel_id=1, replica_groups=mesh['pipe'=4,'expert'=32,'dp'=2] {'expert'}, dimensions={0} | all-to-all | bytes 1572864 | tf_op jit(solution)/shard_map/all_to_all | solution.py:370
  424.0 30.4 %collective-permute-done.5.refs_0_.refs_4_ = bf16[64,2048]{1,0:T(8,128)(2,1)S(1)} collective-permute-done((bf16[64,2048]{1,0:T(8,128)(2,1)S(1)}, bf16[64,2048]{1,0:T(8,128)(2,1)S(1)}, u32[]{:S(2)}, u32[]{:S(2)}) %collective-permute-start.5) | collective-permute-done | bytes 262176 | tf_op jit(solution)/shard_map/ppermute | solution.py:555
  456.3 19.7 %all_to_all.92.refs_0_ = bf16[32,96,128]{2,1,0:T(8,128)(2,1)S(1)} all-to-all(bf16[32,96,128]{2,1,0:T(8,128)(2,1)S(1)} %dispatch.14), channel_id=1, replica_groups=mesh['pipe'=4,'expert'=32,'dp'=2] {'expert'}, dimensions={0} | all-to-all | bytes 1572864 | tf_op jit(solution)/shard_map/all_to_all | solution.py:370
  476.1 11.6 %expert_backward.8 = (bf16[32,96,128]{2,1,0:T(8,128)(2,1)S(1)}, f32[32,2048]{1,0:T(8,128)S(1)}, f32[2,16,768]{2,1,0:T(8,128)S(1)}, f32[16,768]{1,0:T(8,128)S(1)}, f32[16,2048]{1,0:T(8,128)S(1)}) custom-call(s32[96]{0:T(128)S(1)} %dynamic-slice_bitcast_fusion.flags, bf16[32,96,128]{2,1,0:T(8,128)(2,1)S(1)} %all_to_all.92.refs_0_, ...), custom_call_target="tpu_custom_call" | custom-call | tf_op jit(solution)/shard_map/expert_backward/pallas_call | solution.py:480
  488.3 19.4 %all_to_all.93.refs_0_ = bf16[32,96,128]{2,1,0:T(8,128)(2,1)S(1)} all-to-all(bf16[32,96,128]{2,1,0:T(8,128)(2,1)S(1)} %get-tuple-element.104), channel_id=1, replica_groups=mesh['pipe'=4,'expert'=32,'dp'=2] {'expert'}, dimensions={0} | all-to-all | bytes 1572864 | tf_op jit(solution)/shard_map/all_to_all | solution.py:370
  511.7 6.1 %collective-permute-done.6.refs_0_.refs_2_ = bf16[64,2048]{1,0:T(8,128)(2,1)S(1)} collective-permute-done((bf16[64,2048]{1,0:T(8,128)(2,1)S(1)}, bf16[64,2048]{1,0:T(8,128)(2,1)S(1)}, u32[]{:S(2)}, u32[]{:S(2)}) %collective-permute-start.6) | collective-permute-done | bytes 262176 | tf_op jit(solution)/shard_map/ppermute | solution.py:555
  521.4 5.0 all-to-all-start.14
  526.4 14.9 %all-to-all-done.14.refs_0_ = bf16[32,96,128]{2,1,0:T(8,128)(2,1)} async-done(((bf16[32,96,128]{2,1,0:T(8,128)(2,1)}), bf16[32,96,128]{2,1,0:T(8,128)(2,1)}, u32[]{:S(2)}, u32[]{:S(2)}) %all-to-all-start.14) | async-done | bytes 786464 | tf_op jit(solution)/shard_map/all_to_all | solution.py:370
  547.3 11.8 %expert_backward.9 = (bf16[32,96,128]{2,1,0:T(8,128)(2,1)S(1)}, f32[32,2048]{1,0:T(8,128)S(1)}, f32[2,16,768]{2,1,0:T(8,128)S(1)}, f32[16,768]{1,0:T(8,128)S(1)}, f32[16,2048]{1,0:T(8,128)S(1)}) custom-call(s32[96]{0:T(128)S(1)} %copy-done.60, bf16[32,96,128]{2,1,0:T(8,128)(2,1)} %all-to-all-done.14.refs_0_, ...), custom_call_target="tpu_custom_call" | custom-call | tf_op jit(solution)/shard_map/expert_backward/pallas_call | solution.py:480
  559.9 17.2 %collective-permute-start.10 = (bf16[16,2048]{1,0:T(8,128)(2,1)S(1)}, bf16[16,2048]{1,0:T(8,128)(2,1)}, u32[]{:S(2)}, u32[]{:S(2)}) collective-permute-start(bf16[16,2048]{1,0:T(8,128)(2,1)S(1)} %select_convert_fusion.1), channel_id=1, source_target_pairs={{0,1},{1,0},{2,3},{3,2},{4,5},{5,4},{6,7},{7,6},{8,9},{9,8},{10,11... | collective-permute-start | bytes 196616 | tf_op jit(solution)/shard_map/ppermute | solution.py:570
  577.9 4.7 all-to-all-start.15
  588.9 15.4 %all-to-all-done.15.refs_0_ = bf16[32,96,128]{2,1,0:T(8,128)(2,1)S(1)} async-done(((bf16[32,96,128]{2,1,0:T(8,128)(2,1)}), bf16[32,96,128]{2,1,0:T(8,128)(2,1)S(1)}, u32[]{:S(2)}, u32[]{:S(2)}) %all-to-all-start.15) | async-done | bytes 786464 | tf_op jit(solution)/shard_map/all_to_all | solution.py:370
  (220 shorter events, 86.0 us)
Async XLA Ops:
  0.6 46.5 %copy-start = (bf16[1,1,2048,768]{3,2,1,0:T(8,128)(2,1)S(1)}, bf16[1,1,2048,768]{3,2,1,0:T(8,128)(2,1)}, u32[]{:S(2)}) copy-start(bf16[1,1,2048,768]{3,2,1,0:T(8,128)(2,1)} %param.18) | copy-start | bytes 9437188
  4.3 471.7 %copy-start.58 = (s32[96]{0:T(128)}, s32[96]{0:T(128)S(1)}, u32[]{:S(2)}) copy-start(s32[96]{0:T(128)S(1)} %dynamic-slice_bitcast_fusion.flags) | copy-start | bytes 1156
  11.7 35.4 %copy-start.11 = (bf16[1,1,16,2048]{3,2,1,0:T(8,128)(2,1)S(1)}, bf16[1,1,16,2048]{3,2,1,0:T(8,128)(2,1)}, u32[]{:S(2)}) copy-start(bf16[1,1,16,2048]{3,2,1,0:T(8,128)(2,1)} %param.24) | copy-start | bytes 196612
  11.7 35.4 %copy-start.29 = (bf16[1,1,768,16]{2,3,1,0:T(8,128)(2,1)S(1)}, bf16[1,1,768,16]{2,3,1,0:T(8,128)(2,1)}, u32[]{:S(2)}) copy-start(bf16[1,1,768,16]{2,3,1,0:T(8,128)(2,1)} %param.23) | copy-start | bytes 73732
  86.7 36.3 %copy-start.42 = (bf16[64,2048]{1,0:T(8,128)(2,1)}, bf16[64,2048]{1,0:T(8,128)(2,1)S(1)}, u32[]{:S(2)}) copy-start(bf16[64,2048]{1,0:T(8,128)(2,1)S(1)} %combine.8) | copy-start | bytes 786436
  86.7 6.6 %collective-permute-start = (bf16[64,2048]{1,0:T(8,128)(2,1)S(1)}, bf16[64,2048]{1,0:T(8,128)(2,1)S(1)}, u32[]{:S(2)}, u32[]{:S(2)}) collective-permute-start(bf16[64,2048]{1,0:T(8,128)(2,1)S(1)} %combine.8), channel_id=1, source_target_pairs={{0,64},{1,65},{2,66},{3,67},{4,68},{5,69},{6,70},{7,71},{8,72},{9,... | collective-permute-start | bytes 786440 | tf_op jit(solution)/shard_map/ppermute | solution.py:555
  95.9 324.7 %copy-start.30 = (bf16[64,2048]{1,0:T(8,128)(2,1)}, bf16[64,2048]{1,0:T(8,128)(2,1)S(1)}, u32[]{:S(2)}) copy-start(bf16[64,2048]{1,0:T(8,128)(2,1)S(1)} %get-tuple-element.81.refs_1_.refs_2_) | copy-start | bytes 786436
  157.9 7.4 %collective-permute-start.1 = (bf16[64,2048]{1,0:T(8,128)(2,1)S(1)}, bf16[64,2048]{1,0:T(8,128)(2,1)S(1)}, u32[]{:S(2)}, u32[]{:S(2)}) collective-permute-start(bf16[64,2048]{1,0:T(8,128)(2,1)S(1)} %combine.9), channel_id=1, source_target_pairs={{64,128},{0,64},{65,129},{1,65},{66,130},{2,66},{67,131},{3,67},{6... | collective-permute-start | bytes 786440 | tf_op jit(solution)/shard_map/ppermute | solution.py:555
  226.5 0.7 collective-permute-start.2
  268.6 54.2 %copy-start.2 = (bf16[1,1,2048,768]{3,2,1,0:T(8,128)(2,1)S(1)}, bf16[1,1,2048,768]{3,2,1,0:T(8,128)(2,1)}, u32[]{:S(2)}) copy-start(bf16[1,1,2048,768]{3,2,1,0:T(8,128)(2,1)} %param.19) | copy-start | bytes 9437188
  295.1 0.7 collective-permute-start.3
  331.2 144.8 %copy-start.3 = (f32[5,192,768]{2,1,0:T(8,128)}, f32[5,192,768]{2,1,0:T(8,128)S(1)}, u32[]{:S(2)}) copy-start(f32[5,192,768]{2,1,0:T(8,128)S(1)} %get-tuple-element.99.refs_4_.refs_3_) | copy-start | bytes 8847364
  331.2 144.9 %copy-start.5 = (f32[5,192,768]{2,1,0:T(8,128)}, f32[5,192,768]{2,1,0:T(8,128)S(1)}, u32[]{:S(2)}) copy-start(f32[5,192,768]{2,1,0:T(8,128)S(1)} %get-tuple-element.100.refs_5_.refs_4_) | copy-start | bytes 8847364
  338.9 52.8 %copy-start.80 = (f32[16,768]{1,0:T(8,128)}, f32[16,768]{1,0:T(8,128)S(1)}, u32[]{:S(2)}) copy-start(f32[16,768]{1,0:T(8,128)S(1)} %get-tuple-element.117) | copy-start | bytes 147460
  365.0 0.7 collective-permute-start.4
  396.8 79.3 %copy-start.66 = (f32[16,2048]{1,0:T(8,128)}, f32[16,2048]{1,0:T(8,128)S(1)}, u32[]{:S(2)}) copy-start(f32[16,2048]{1,0:T(8,128)S(1)} %get-tuple-element.123) | copy-start | bytes 393220
  396.8 79.3 %copy-start.74 = (f32[2,16,768]{2,1,0:T(8,128)}, f32[2,16,768]{2,1,0:T(8,128)S(1)}, u32[]{:S(2)}) copy-start(f32[2,16,768]{2,1,0:T(8,128)S(1)} %get-tuple-element.113) | copy-start | bytes 294916
  396.8 79.3 %copy-start.82 = (f32[16,768]{1,0:T(8,128)}, f32[16,768]{1,0:T(8,128)S(1)}, u32[]{:S(2)}) copy-start(f32[16,768]{1,0:T(8,128)S(1)} %get-tuple-element.118) | copy-start | bytes 147460
  422.7 31.7 %collective-permute-start.5 = (bf16[64,2048]{1,0:T(8,128)(2,1)S(1)}, bf16[64,2048]{1,0:T(8,128)(2,1)S(1)}, u32[]{:S(2)}, u32[]{:S(2)}) collective-permute-start(bf16[64,2048]{1,0:T(8,128)(2,1)S(1)} %combine.13), channel_id=1, source_target_pairs={{64,0},{128,64},{65,1},{129,65},{66,2},{130,66},{67,3},{131,67},{6... | collective-permute-start | bytes 786440 | tf_op jit(solution)/shard_map/ppermute | solution.py:555
  510.4 7.4 %collective-permute-start.6 = (bf16[64,2048]{1,0:T(8,128)(2,1)S(1)}, bf16[64,2048]{1,0:T(8,128)(2,1)S(1)}, u32[]{:S(2)}, u32[]{:S(2)}) collective-permute-start(bf16[64,2048]{1,0:T(8,128)(2,1)S(1)} %combine.14), channel_id=1, source_target_pairs={{64,0},{65,1},{66,2},{67,3},{68,4},{69,5},{70,6},{71,7},{72,8},{73... | collective-permute-start | bytes 786440 | tf_op jit(solution)/shard_map/ppermute | solution.py:555
  521.4 19.9 %all-to-all-start.14 = ((bf16[32,96,128]{2,1,0:T(8,128)(2,1)}), bf16[32,96,128]{2,1,0:T(8,128)(2,1)}, u32[]{:S(2)}, u32[]{:S(2)}) async-start(bf16[32,96,128]{2,1,0:T(8,128)(2,1)} %copy-done.28), calls=%async_computation.14 | async-start | bytes 1572864 | tf_op jit(solution)/shard_map/all_to_all | solution.py:370
  559.8 44.5 %copy-start.23 = (bf16[2,64,192]{2,1,0:T(8,128)(2,1)S(1)}, bf16[2,64,192]{2,1,0:T(8,128)(2,1)}, u32[]{:S(2)}) copy-start(bf16[2,64,192]{2,1,0:T(8,128)(2,1)} %get-tuple-element.72.refs_3_.refs_4_.refs_6_.refs_5_) | copy-start | bytes 147460
  559.8 44.5 %copy-start.25 = (bf16[2,64,192]{2,1,0:T(8,128)(2,1)S(1)}, bf16[2,64,192]{2,1,0:T(8,128)(2,1)}, u32[]{:S(2)}) copy-start(bf16[2,64,192]{2,1,0:T(8,128)(2,1)} %get-tuple-element.73.refs_4_.refs_5_.refs_7_.refs_6_) | copy-start | bytes 147460
  559.8 44.5 %copy-start.27 = (bf16[2,64,192]{2,1,0:T(8,128)(2,1)S(1)}, bf16[2,64,192]{2,1,0:T(8,128)(2,1)}, u32[]{:S(2)}) copy-start(bf16[2,64,192]{2,1,0:T(8,128)(2,1)} %get-tuple-element.74.refs_5_.refs_6_.refs_8_.refs_7_) | copy-start | bytes 147460
  559.8 44.5 %copy-start.31 = (bf16[64,2048]{1,0:T(8,128)(2,1)S(1)}, bf16[64,2048]{1,0:T(8,128)(2,1)}, u32[]{:S(2)}) copy-start(bf16[64,2048]{1,0:T(8,128)(2,1)} %copy-done.30) | copy-start | bytes 786436
  559.8 44.5 %copy-start.49 = (bf16[64,2048]{1,0:T(8,128)(2,1)S(1)}, bf16[64,2048]{1,0:T(8,128)(2,1)}, u32[]{:S(2)}) copy-start(bf16[64,2048]{1,0:T(8,128)(2,1)} %copy-done.48) | copy-start | bytes 786436
  559.8 44.5 %copy-start.61 = (s32[96]{0:T(128)S(1)}, s32[96]{0:T(128)}, u32[]{:S(2)}) copy-start(s32[96]{0:T(128)} %copy-done.58) | copy-start | bytes 1156
  559.9 26.7 %collective-permute-start.10 = (bf16[16,2048]{1,0:T(8,128)(2,1)S(1)}, bf16[16,2048]{1,0:T(8,128)(2,1)}, u32[]{:S(2)}, u32[]{:S(2)}) collective-permute-start(bf16[16,2048]{1,0:T(8,128)(2,1)S(1)} %select_convert_fusion.1), channel_id=1, source_target_pairs={{0,1},{1,0},{2,3},{3,2},{4,5},{5,4},{6,7},{7,6},{8,9},{9,8},{10,11... | collective-permute-start | bytes 196616 | tf_op jit(solution)/shard_map/ppermute | solution.py:570
  577.1 7.4 %collective-permute-start.9 = (bf16[16,768]{1,0:T(8,128)(2,1)S(1)}, bf16[16,768]{1,0:T(8,128)(2,1)S(1)}, u32[]{:S(2)}, u32[]{:S(2)}) collective-permute-start(bf16[16,768]{1,0:T(8,128)(2,1)S(1)} %select_convert_fusion.3), channel_id=1, source_target_pairs={{0,1},{1,0},{2,3},{3,2},{4,5},{5,4},{6,7},{7,6},{8,9},{9,8},{10,11... | collective-permute-start | bytes 73736 | tf_op jit(solution)/shard_map/ppermute | solution.py:570
  577.4 7.8 %collective-permute-start.8 = (bf16[2,16,768]{2,1,0:T(8,128)(2,1)S(1)}, bf16[2,16,768]{2,1,0:T(8,128)(2,1)}, u32[]{:S(2)}, u32[]{:S(2)}) collective-permute-start(bf16[2,16,768]{2,1,0:T(8,128)(2,1)S(1)} %select_convert_fusion.2), channel_id=1, source_target_pairs={{0,1},{1,0},{2,3},{3,2},{4,5},{5,4},{6,7},{7,6},{8,9},{9,8},{10,11... | collective-permute-start | bytes 147464 | tf_op jit(solution)/shard_map/ppermute | solution.py:570
  577.9 26.3 %all-to-all-start.15 = ((bf16[32,96,128]{2,1,0:T(8,128)(2,1)}), bf16[32,96,128]{2,1,0:T(8,128)(2,1)S(1)}, u32[]{:S(2)}, u32[]{:S(2)}) async-start(bf16[32,96,128]{2,1,0:T(8,128)(2,1)} %copy-done.52), calls=%async_computation.15 | async-start | bytes 1572864 | tf_op jit(solution)/shard_map/all_to_all | solution.py:370
  584.0 4.1 collective-permute-start.7
  (67 other events, 980.2 us)

commit v2 on v1

v2 whole, which is shorter than its diff:
```python
import functools

import jax
import jax.numpy as jnp
import numpy as np
from jax import lax
from jax.experimental import pallas as pl
from jax.experimental.pallas import tpu as pltpu
from jax.sharding import PartitionSpec as P

EPS = 1e-06
SLOTS = 6
LANES = 128
F32 = jnp.float32
BF16 = jnp.bfloat16


def dot(left, right):
    return jnp.dot(left, right, preferred_element_type=F32)


def dot_nt(left, right):
    return lax.dot_general(left, right, (((1,), (1,)), ((), ())), preferred_element_type=F32)


def dot_tn(left, right):
    return lax.dot_general(left, right, (((0,), (0,)), ((), ())), preferred_element_type=F32)


def pack(read, out_ref, wide, peers, chunks):
    stride = SLOTS * chunks
    for slot in range(SLOTS):
        for chunk in range(chunks):
            wide[pl.ds(slot * chunks + chunk, peers, stride=stride), :] = read(slot, chunk)
    for peer in range(peers):
        out_ref[peer] = wide[peer * stride : (peer + 1) * stride, :].astype(BF16)


def pack_from(rows, out_ref, wide, peers, chunks):
    pack(
        lambda slot, chunk: rows[
            slot * peers : (slot + 1) * peers, chunk * LANES : (chunk + 1) * LANES
        ],
        out_ref,
        wide,
        peers,
        chunks,
    )


def unpack(in_ref, rows, wide, peers, chunks):
    stride = SLOTS * chunks
    for peer in range(peers):
        wide[peer * stride : (peer + 1) * stride, :] = in_ref[peer].astype(F32)
    for slot in range(SLOTS):
        for chunk in range(chunks):
            rows[slot * peers : (slot + 1) * peers, chunk * LANES : (chunk + 1) * LANES] = wide[
                pl.ds(slot * chunks + chunk, peers, stride=stride), :
            ].astype(BF16)


def split(weight):
    high = weight.astype(BF16)
    return high, (weight - high.astype(F32)).astype(BF16)


def tables_kernel(peers, routes, gates, place, scale_hi, scale_lo, pick, mix_hi, mix_lo):
    micros, _, rows = routes.shape
    slots = SLOTS * peers
    assert peers & (peers - 1) == 0
    number = lax.broadcasted_iota(jnp.int32, (slots, rows), 0)
    expert, position = number & (peers - 1), (number >> (peers.bit_length() - 1)).astype(F32)
    down = lax.broadcasted_iota(jnp.int32, (rows, rows), 0)
    across = lax.broadcasted_iota(jnp.int32, (rows, rows), 1)
    earlier = jnp.where(down < across, 1.0, 0.0).astype(BF16)
    for micro in range(micros):
        first = routes[micro, 0:1, :] == expert
        second = routes[micro, 1:2, :] == expert
        named = jnp.where(first | second, 1.0, 0.0)
        before = dot(named.astype(BF16), earlier)
        chosen = jnp.where(before == position, named, 0.0)
        weight = chosen * (
            jnp.where(first, gates[micro, 0:1, :], 0.0) + jnp.where(second, gates[micro, 1:2, :], 0.0)
        )
        place[micro] = chosen.astype(BF16)
        scale_hi[micro], scale_lo[micro] = split(weight)
        pick[micro] = chosen.T.astype(BF16)
        mix_hi[micro], mix_lo[micro] = split(weight.T)


def choose(refs, micro, which):
    blocks = [ref[...] if len(ref.shape) == 2 else ref[micro] for ref in refs]
    value = blocks[0]
    for index in range(1, len(blocks)):
        value = jnp.where(which == index, blocks[index], value)
    return value


def dispatch_kernel(dims, kinds, source_count, flags, *refs):
    peers, chunks, base, tick = dims
    sources = refs[:source_count]
    gain, place, scale_hi, scale_lo = refs[source_count : source_count + 4]
    out_ref = refs[source_count + 4]
    wide, rows = refs[-2:]
    is_forward, micro = flags[base], flags[base + 1]
    current = choose(sources, tick, flags[base + 2])
    if source_count > 1:
        refs[source_count + 5][...] = current

    def forward():
        values = current.astype(F32)
        inverse = lax.rsqrt(jnp.mean(values * values, axis=-1, keepdims=True) + EPS)
        rows[...] = dot(place[micro], (values * inverse * gain[...]).astype(BF16))

    def backward():
        rows[...] = dot(scale_hi[micro], current) + dot(scale_lo[micro], current)

    if kinds == "F":
        forward()
    elif kinds == "B":
        backward()
    else:
        pl.when(is_forward == 1)(forward)
        pl.when(is_forward == 0)(backward)
    pack_from(rows, out_ref, wide, peers, chunks)


def combine_kernel(dims, kinds, section_count, grad_count, flags, *refs):
    peers, chunks, base, grad_micro = dims
    returned = refs[0]
    sections = refs[1 : 1 + section_count]
    grads = refs[1 + section_count : 1 + section_count + grad_count]
    gain, pick, mix_hi, mix_lo, out_ref, wide, rows = refs[1 + section_count + grad_count :]
    is_forward, micro = flags[base], flags[base + 1]
    unpack(returned, rows, wide, peers, chunks)

    def forward():
        mixed = dot(mix_hi[micro], rows[...]) + dot(mix_lo[micro], rows[...])
        out_ref[...] = (choose(sections, 0, flags[base + 2]).astype(F32) + mixed).astype(BF16)

    def backward():
        section_in = choose(sections, 0, flags[base + 2]).astype(F32)
        grad_next = choose(grads, grad_micro, flags[base + 3]).astype(F32)
        inverse = lax.rsqrt(jnp.mean(section_in * section_in, axis=-1, keepdims=True) + EPS)
        scaled = dot(pick[micro], rows[...]) * gain[...]
        normed = section_in * inverse
        shared = jnp.mean(scaled * normed, axis=-1, keepdims=True)
        out_ref[...] = (grad_next + inverse * (scaled - normed * shared)).astype(BF16)

    if kinds == "F":
        forward()
    elif kinds == "B":
        backward()
    else:
        pl.when(is_forward == 1)(forward)
        pl.when(is_forward == 0)(backward)


def forward_kernel(
    dims, has_store, received, w_gate, w_up, w_down, in_a, in_b, down_a, down_b, *refs
):
    peers, chunks, low_rank, block, slot = dims
    sent, rows, low_in, gate_pre, up_pre, wide, total = refs[4 * has_store :]
    slots = rows.shape[1]
    unpack(received, rows.at[slot], wide, peers, chunks)
    slot_rows = rows[slot]
    low = dot_nt(slot_rows, in_a[...]).astype(BF16)
    low_in[slot] = low
    low_total = jnp.zeros((slots, low_rank), F32)
    for start in range(0, w_gate.shape[1], block):
        piece = pl.ds(start, block)
        gate = dot(slot_rows, w_gate[:, piece]) + dot(low[:, :low_rank], in_b[0, :, piece])
        up = dot(slot_rows, w_up[:, piece]) + dot(low[:, low_rank:], in_b[1, :, piece])
        gate_pre[slot, :, piece] = gate
        up_pre[slot, :, piece] = up
        activated = (gate * jax.nn.sigmoid(gate) * up).astype(BF16)
        low_total += dot_nt(activated, down_a[:, piece])
        part = dot(activated, w_down[piece, :])
        total[...] = part if start == 0 else total[...] + part
    total[...] += dot(low_total.astype(BF16), down_b[...])
    pack_from(total, sent, wide, peers, chunks)


def backward_kernel(dims, received_count, has_other, has_totals, flags, *refs):
    peers, chunks, low_rank, block, base = dims
    received = refs[:received_count]
    other = refs[received_count]
    refs = refs[received_count + has_other + 4 * has_totals :]
    (rows, low_in, gate_pre, up_pre, w_gate, w_up, w_down, in_a, in_b, down_a, down_b) = refs[:11]
    (sent, grad_in_a, grad_in_b, grad_down_a, grad_down_b) = refs[11:16]
    (wide, grad_out, total) = refs[16:]
    active, slot = flags[base] == 1, flags[base + 1]
    slots = rows.shape[1]

    def store(ref, where, value):
        ref[where] = jnp.where(flags[base + 3] == 1, ref[where] + value, value) if has_totals else value

    @pl.when(active)
    def _():
        if received_count == 1:
            unpack(received[0], grad_out, wide, peers, chunks)
        else:
            for index in range(received_count):

                @pl.when(flags[base + 2] == index)
                def _():
                    unpack(received[index], grad_out, wide, peers, chunks)

        grad = grad_out[...]
        grad_low_down = dot_nt(grad, down_b[...]).astype(BF16)
        low = low_in[slot]
        low_total = jnp.zeros((slots, low_rank), F32)
        gate_low = jnp.zeros((slots, low_rank), F32)
        up_low = jnp.zeros((slots, low_rank), F32)
        for start in range(0, w_gate.shape[1], block):
            piece = pl.ds(start, block)
            gate, up = gate_pre[slot, :, piece], up_pre[slot, :, piece]
            sigmoid = jax.nn.sigmoid(gate)
            silu = gate * sigmoid
            activated = (silu * up).astype(BF16)
            grad_act = dot_nt(grad, w_down[piece, :]) + dot(grad_low_down, down_a[:, piece])
            grad_gate = (grad_act * up * sigmoid * (1.0 + gate * (1.0 - sigmoid))).astype(BF16)
            grad_up = (grad_act * silu).astype(BF16)
            store(grad_in_b, (0, slice(None), piece), dot_tn(low[:, :low_rank], grad_gate))
            store(grad_in_b, (1, slice(None), piece), dot_tn(low[:, low_rank:], grad_up))
            store(grad_down_a, (slice(None), piece), dot_tn(grad_low_down, activated))
            low_total += dot_nt(activated, down_a[:, piece])
            gate_low += dot_nt(grad_gate, in_b[0, :, piece])
            up_low += dot_nt(grad_up, in_b[1, :, piece])
            part = dot_nt(grad_gate, w_gate[:, piece]) + dot_nt(grad_up, w_up[:, piece])
            total[...] = part if start == 0 else total[...] + part
        low_grad = jnp.concatenate([gate_low, up_low], axis=1).astype(BF16)
        total[...] += dot(low_grad, in_a[...])
        pack_from(total, sent, wide, peers, chunks)
        store(grad_in_a, ..., dot_tn(low_grad, rows[slot]))
        store(grad_down_b, ..., dot_tn(low_total.astype(BF16), grad))

    if has_other:

        @pl.when(jnp.logical_not(active))
        def _():
            sent[...] = other[...]


def params(megabytes):
    return pltpu.CompilerParams(vmem_limit_bytes=megabytes * 1024 * 1024)


def rank_flags(sections, micros):
    assert sections == 4 and micros == 2
    last = sections - 1
    ticks = 2 * sections
    table = np.zeros((sections, ticks, 12), np.int32)
    for rank in range(sections):
        for tick in range(ticks):
            row = table[rank, tick]
            forward = tick - rank if tick - rank in (0, 1) else None
            backward = tick - (2 * last - rank)
            backward = backward if backward in (0, 1) else None
            if forward is not None:
                row[0:2] = 1, forward
            elif backward is not None:
                row[0:2] = 0, backward
            elif rank == last and tick < 2:
                row[0:2] = 0, tick
            if tick == 0:
                row[2] = 1 if rank == last else 0
            elif tick == 1:
                row[2] = 2 if rank == last else (0 if rank == 0 else 1)
            if backward is not None:
                row[4:6] = 1, rank + backward
                row[6] = 0 if rank == last else 1
                row[7] = backward
                row[8:10] = 0, backward
            elif forward is not None:
                row[8:10] = 1, forward
            elif rank == last and tick in (5, 6):
                row[8:10] = 1, tick - 5
            if tick == 4:
                row[10:12] = (0, 0) if rank == last else (1, 1)
            elif tick == 5:
                row[10] = 1 if rank == 1 else 0
            elif tick == 6:
                row[10] = {1: 0, 0: 1, 3: 2}.get(rank, 0)
    return table.reshape(sections, -1)


def body(
    tokens, cotangent, routes, gates, norm_gain, w_gate, w_up, w_down, in_a, in_b, down_a, down_b
):
    section_index = lax.axis_index("pipe")
    sections = lax.axis_size("pipe")
    peers = lax.axis_size("expert")
    micros, tok_rows, model = tokens.shape
    hidden_width = w_gate.shape[3]
    low_rank = down_a.shape[3]
    slots = SLOTS * peers
    chunks = model // LANES
    ticks = 2 * sections
    forward_ticks = sections + micros - 1
    block = hidden_width // 3
    flags = lax.dynamic_index_in_dim(
        jnp.asarray(rank_flags(sections, micros)), section_index, 0, keepdims=False
    )
    w_gate, w_up, w_down = w_gate[0, 0], w_up[0, 0], w_down[0, 0]
    in_a, in_b, down_a, down_b = in_a[0, 0].T, in_b[0, 0], down_a[0, 0].T, down_b[0, 0]
    buffer = jax.ShapeDtypeStruct((peers, SLOTS * chunks, LANES), BF16)
    block_rows = jax.ShapeDtypeStruct((tok_rows, model), BF16)
    wide = pltpu.VMEM((peers * SLOTS * chunks, LANES), F32)

    routes, gates = routes[0], gates[0]
    held = pl.BlockSpec(memory_space=pltpu.VMEM)
    scalars = pl.BlockSpec(memory_space=pltpu.SMEM)
    table_in = jax.ShapeDtypeStruct((micros, slots, tok_rows), BF16)
    table_out = jax.ShapeDtypeStruct((micros, tok_rows, slots), BF16)
    place, scale_hi, scale_lo, pick, mix_hi, mix_lo = pl.pallas_call(
        functools.partial(tables_kernel, peers),
        out_shape=[table_in] * 3 + [table_out] * 3,
        in_specs=[held] * 2,
        out_specs=[held] * 6,
        compiler_params=params(8),
        name="tables",
    )(routes.transpose(0, 2, 1), gates.transpose(0, 2, 1))

    def exchange(rows):
        return lax.all_to_all(rows, "expert", split_axis=0, concat_axis=0, tiled=True)

    def dispatch(tick, kinds, sources):
        single = len(sources) == 1
        operands = [*sources, norm_gain, place, scale_hi, scale_lo]
        result = pl.pallas_call(
            functools.partial(
                dispatch_kernel, (peers, chunks, tick * 12, tick), kinds, len(sources)
            ),
            out_shape=[buffer] if single else [buffer, block_rows],
            in_specs=[scalars] + [held] * len(operands),
            out_specs=[held] * (1 if single else 2),
            scratch_shapes=[wide, pltpu.VMEM((slots, model), F32)],
            compiler_params=params(20),
            name="dispatch",
        )(flags, *operands)
        return result[0], sources[0] if single else result[1]

    def combine(tick, kinds, returned, section_inputs, grads):
        operands = [returned, *section_inputs, *grads, norm_gain, pick, mix_hi, mix_lo]
        return pl.pallas_call(
            functools.partial(
                combine_kernel,
                (peers, chunks, tick * 12 + 8, tick - sections + 1),
                kinds,
                len(section_inputs),
                len(grads),
            ),
            out_shape=block_rows,
            in_specs=[scalars] + [held] * len(operands),
            out_specs=held,
            scratch_shapes=[wide, pltpu.VMEM((slots, model), BF16)],
            compiler_params=params(20),
            name="combine",
        )(flags, *operands)

    weights = (w_gate, w_up, w_down, in_a, in_b, down_a, down_b)
    state_shapes = [
        jax.ShapeDtypeStruct((forward_ticks, slots, model), BF16),
        jax.ShapeDtypeStruct((forward_ticks, slots, 2 * low_rank), BF16),
        jax.ShapeDtypeStruct((forward_ticks, slots, hidden_width), F32),
        jax.ShapeDtypeStruct((forward_ticks, slots, hidden_width), F32),
    ]

    def expert_forward(tick, received, state):
        has_store = state is not None
        result = pl.pallas_call(
            functools.partial(forward_kernel, (peers, chunks, low_rank, block, tick), has_store),
            out_shape=[buffer] + state_shapes,
            in_specs=[held] * (12 if has_store else 8),
            out_specs=[held] * 5,
            scratch_shapes=[wide, pltpu.VMEM((slots, model), F32)],
            input_output_aliases={8: 1, 9: 2, 10: 3, 11: 4} if has_store else {},
            compiler_params=params(20),
            name="expert_forward",
        )(received, *weights, *(state if has_store else ()))
        return result[0], result[1:]

    def expert_backward(tick, received, other, state, totals):
        base = tick * 12 + 4
        others = [] if other is None else [other]
        operands = [*received, *others, *totals, *state, *weights]
        first = 1 + len(received) + len(others)
        return pl.pallas_call(
            functools.partial(
                backward_kernel,
                (peers, chunks, low_rank, block, base),
                len(received),
                len(others),
                len(totals) > 0,
            ),
            out_shape=[
                buffer,
                jax.ShapeDtypeStruct((2 * low_rank, model), F32),
                jax.ShapeDtypeStruct((2, low_rank, hidden_width), F32),
                jax.ShapeDtypeStruct((low_rank, hidden_width), F32),
                jax.ShapeDtypeStruct((low_rank, model), F32),
            ],
            in_specs=[scalars] + [held] * len(operands),
            out_specs=[held] * 5,
            input_output_aliases={first + item: 1 + item for item in range(len(totals))},
            scratch_shapes=[
                wide,
                pltpu.VMEM((slots, model), BF16),
                pltpu.VMEM((slots, model), F32),
            ],
            compiler_params=params(20),
            name="expert_backward",
        )(flags, *operands)

    hops = [
        [(0, 1)],
        [(1, 2), (0, 1)],
        [(2, 3), (1, 2)],
        [(2, 3), (3, 2)],
        [(2, 1), (3, 2)],
        [(1, 0), (2, 1)],
        [(1, 0)],
    ]
    inputs, got, sent, mixed = {}, {}, {}, {}
    state, totals = None, ()
    for tick in range(ticks):
        if tick == 0:
            sources = [tokens, cotangent]
        elif tick == 1:
            sources = [tokens, incoming, cotangent]
        else:
            sources = [incoming]
        kinds = {0: "FB", 1: "FB", 2: "F", 3: "F", 4: "FB"}.get(tick, "B")
        placed, inputs[tick] = dispatch(tick, kinds, sources)
        got[tick] = exchange(placed)
        if tick < forward_ticks:
            sent[tick], state = expert_forward(tick, got[tick], state)
            answer = sent[tick]
        if tick >= 3:
            received = [got[index] for index in {3: (0,), 4: (1, 4)}.get(tick, (tick,))]
            other = sent[{3: 3, 5: 3, 6: 4}[tick]] if tick in (3, 5, 6) else None
            answer, *totals = expert_backward(tick, received, other, state, totals)
        returned = exchange(answer)
        section_inputs = {4: (4, 2), 5: (3, 1), 6: (2, 0, 4), 7: (1,)}.get(tick, (tick,))
        grads = {3: [cotangent], 4: [cotangent, inputs[tick]]}.get(
            tick, [inputs[tick]] if tick > 4 else []
        )
        kinds = "F" if tick < 3 else "B" if tick in (4, 7) else "FB"
        mixed[tick] = combine(
            tick, kinds, returned, [inputs[index] for index in section_inputs], grads
        )
        if tick < ticks - 1:
            incoming = lax.ppermute(mixed[tick], "pipe", hops[tick])

    mixed, totals = lax.optimization_barrier((mixed, totals))

    def by_rank(choices):
        value = choices[0]
        for rank in range(1, sections):
            value = jnp.where(section_index == rank, choices[rank], value)
        return value

    def summed(total):
        total = total.astype(BF16)
        across = lax.ppermute(total, "dp", [(0, 1), (1, 0)])
        return total.astype(F32) + across.astype(F32)

    totals = [summed(total) for total in totals]
    hidden = jnp.stack(
        [by_rank([mixed[m], mixed[1 + m], mixed[2 + m], mixed[5 + m]]) for m in range(micros)]
    )
    input_grads = jnp.stack([by_rank([mixed[6 - r + m] for r in range(4)]) for m in range(micros)])
    return (
        hidden[None],
        input_grads[None],
        totals[0].T[None, None],
        totals[1][None, None],
        totals[2].T[None, None],
        totals[3][None, None],
    )


def solution(mesh):
    placed = (
        P(None, ("expert", "dp"), None),
        P(None, ("expert", "dp"), None),
        P("pipe", None, ("expert", "dp"), None),
        P("pipe", None, ("expert", "dp"), None),
        P("pipe", None),
        P("pipe", "expert", None, None),
        P("pipe", "expert", None, None),
        P("pipe", "expert", None, None),
        P("pipe", "expert", None, None),
        P("pipe", "expert", None, None, None),
        P("pipe", "expert", None, None),
        P("pipe", "expert", None, None),
    )
    return jax.shard_map(
        body,
        mesh=mesh,
        in_specs=placed,
        out_specs=(
            P("pipe", None, ("expert", "dp"), None),
            P("pipe", None, ("expert", "dp"), None),
            P("pipe", "expert", None, None),
            P("pipe", "expert", None, None, None),
            P("pipe", "expert", None, None),
            P("pipe", "expert", None, None),
        ),
        check_vma=False,
    )
```

time: 618 us -> 558 us (0.903)
  Pallas kernels: 115 us -> 77.4 us
  blocking collectives: 343 us -> 361 us
  waiting for transfers between devices: 73.3 us -> 55.8 us
  local copies, waits for them, and re-layouts: 27.8 us -> 12.4 us
    pallas_call x5, Pallas kernels: 37.7 us -> 16.1 us  [expert_backward(): pl.pallas_call(functools.partial(backward_kernel, (peers, chunks, low_ran...]
    all_to_all x14 -> x15, blocking collectives: 343 us -> 361 us  [exchange(): lax.all_to_all(rows, 'expert', split_axis=0, concat_axis=0, tiled=True)]
    all_to_all x2 -> x1, waiting for transfers between devices: 30.3 us -> 14.9 us  [exchange(): lax.all_to_all(rows, 'expert', split_axis=0, concat_axis=0, tiled=True)]
    pallas_call x5, Pallas kernels: 42 us -> 26.9 us  [expert_forward(): pl.pallas_call(functools.partial(forward_kernel, (peers, chunks, low_rank...]
    unnamed x172 -> x44, local copies, waits for them, and re-layouts: 24.2 us -> 11.7 us
  transfers between devices with their start and end apart: 13 -> 12, of which waited for: 6 -> 5; matrix products, arithmetic and copies ran while one was open for 1% -> 1% of each run, Pallas kernels for 0% -> 0%
where the time goes in v2:
time: 558 us; the launch traced here: 550 us
  blocking collectives  361 us (65%)
  Pallas kernels  77.4 us (14%)
  waiting for transfers between devices  55.8 us (10%)
  starting transfers between devices  36.4 us (7%)
  local copies, waits for them, and re-layouts  12.4 us (2%)
    all_to_all x15, blocking collectives, exchange(): lax.all_to_all(rows, 'expert', split_axis=0, concat_axis=0, tiled=True)  361 us
    ppermute x7, waiting for transfers between devices, body(): incoming = lax.ppermute(mixed[tick], 'pipe', hops[tick])  40.9 us
    pallas_call x5, Pallas kernels, expert_forward(): pl.pallas_call(functools.partial(forward_kernel, (peers, chunks, low_rank...  26.9 us
    ppermute x4, starting transfers between devices, summed(): across = lax.ppermute(total, 'dp', [(0, 1), (1, 0)])  19.3 us
    pallas_call x8, Pallas kernels, dispatch(): pl.pallas_call(functools.partial(dispatch_kernel, (peers, chunks, tick *...  17.8 us
    pallas_call x8, Pallas kernels, combine(): pl.pallas_call(functools.partial(combine_kernel, (peers, chunks, tick * 1...  16.2 us
    pallas_call x5, Pallas kernels, expert_backward(): pl.pallas_call(functools.partial(backward_kernel, (peers, chunks, low_ran...  16.1 us
    all_to_all x1, waiting for transfers between devices, exchange(): lax.all_to_all(rows, 'expert', split_axis=0, concat_axis=0, tiled=True)  14.9 us
  transfers between devices with their start and end apart: 12, of which 5 were waited for; matrix products, arithmetic and copies ran while one was open for 1% of the time, Pallas kernels for 0%

profile of v2, /device:TPU:1, one launch (start us, length us, event | category | flops | bytes accessed | tf_op | source)
XLA Modules:
  0.0 549.5 jit_solution(3051522788219386706)
XLA Ops:
  8.5 32.7 %all_to_all.80.received.refs_0_ = bf16[32,96,128]{2,1,0:T(8,128)(2,1)S(1)} all-to-all(bf16[32,96,128]{2,1,0:T(8,128)(2,1)S(1)} %get-tuple-element.81), channel_id=1, replica_groups=mesh['pipe'=4,'expert'=32,'dp'=2] {'expert'}, dimensions={0} | all-to-all | bytes 1572864 | tf_op jit(solution)/shard_map/all_to_all | solution.py:326
  46.9 5.4 expert_forward.5
  52.3 25.6 %all_to_all.81.refs_0_ = bf16[32,96,128]{2,1,0:T(8,128)(2,1)S(1)} all-to-all(bf16[32,96,128]{2,1,0:T(8,128)(2,1)S(1)} %get-tuple-element.82), channel_id=1, replica_groups=mesh['pipe'=4,'expert'=32,'dp'=2] {'expert'}, dimensions={0} | all-to-all | bytes 1572864 | tf_op jit(solution)/shard_map/all_to_all | solution.py:326
  80.0 3.3 collective-permute-start
  83.3 3.3 collective-permute-done.refs_1_
  89.2 27.1 %all_to_all.82.received.refs_0_ = bf16[32,96,128]{2,1,0:T(8,128)(2,1)S(1)} all-to-all(bf16[32,96,128]{2,1,0:T(8,128)(2,1)S(1)} %get-tuple-element.87), channel_id=1, replica_groups=mesh['pipe'=4,'expert'=32,'dp'=2] {'expert'}, dimensions={0} | all-to-all | bytes 1572864 | tf_op jit(solution)/shard_map/all_to_all | solution.py:326
  116.3 5.4 expert_forward.6
  121.7 24.6 %all_to_all.83.refs_0_ = bf16[32,96,128]{2,1,0:T(8,128)(2,1)S(1)} all-to-all(bf16[32,96,128]{2,1,0:T(8,128)(2,1)S(1)} %get-tuple-element.92), channel_id=1, replica_groups=mesh['pipe'=4,'expert'=32,'dp'=2] {'expert'}, dimensions={0} | all-to-all | bytes 1572864 | tf_op jit(solution)/shard_map/all_to_all | solution.py:326
  148.3 4.5 collective-permute-start.1
  152.8 3.3 collective-permute-done.1.refs_0_.refs_1_.refs_2_
  157.9 24.3 %all_to_all.84.received = bf16[32,96,128]{2,1,0:T(8,128)(2,1)S(1)} all-to-all(bf16[32,96,128]{2,1,0:T(8,128)(2,1)S(1)} %dispatch.10), channel_id=1, replica_groups=mesh['pipe'=4,'expert'=32,'dp'=2] {'expert'}, dimensions={0} | all-to-all | bytes 1572864 | tf_op jit(solution)/shard_map/all_to_all | solution.py:326
  182.2 5.4 expert_forward.7
  187.6 24.2 %all_to_all.85.refs_0_ = bf16[32,96,128]{2,1,0:T(8,128)(2,1)S(1)} all-to-all(bf16[32,96,128]{2,1,0:T(8,128)(2,1)S(1)} %get-tuple-element.98), channel_id=1, replica_groups=mesh['pipe'=4,'expert'=32,'dp'=2] {'expert'}, dimensions={0} | all-to-all | bytes 1572864 | tf_op jit(solution)/shard_map/all_to_all | solution.py:326
  216.3 24.4 %all_to_all.86.received = bf16[32,96,128]{2,1,0:T(8,128)(2,1)S(1)} all-to-all(bf16[32,96,128]{2,1,0:T(8,128)(2,1)S(1)} %dispatch.11), channel_id=1, replica_groups=mesh['pipe'=4,'expert'=32,'dp'=2] {'expert'}, dimensions={0} | all-to-all | bytes 1572864 | tf_op jit(solution)/shard_map/all_to_all | solution.py:326
  240.8 5.4 expert_forward.8
  246.8 24.2 %all_to_all.87.refs_0_ = bf16[32,96,128]{2,1,0:T(8,128)(2,1)S(1)} all-to-all(bf16[32,96,128]{2,1,0:T(8,128)(2,1)S(1)} %get-tuple-element.108), channel_id=1, replica_groups=mesh['pipe'=4,'expert'=32,'dp'=2] {'expert'}, dimensions={0} | all-to-all | bytes 1572864 | tf_op jit(solution)/shard_map/all_to_all | solution.py:326
  273.6 3.1 dispatch.12
  276.7 24.1 %all_to_all.88.received.refs_1_ = bf16[32,96,128]{2,1,0:T(8,128)(2,1)S(1)} all-to-all(bf16[32,96,128]{2,1,0:T(8,128)(2,1)S(1)} %dispatch.12), channel_id=1, replica_groups=mesh['pipe'=4,'expert'=32,'dp'=2] {'expert'}, dimensions={0} | all-to-all | bytes 1572864 | tf_op jit(solution)/shard_map/all_to_all | solution.py:326
  300.9 5.4 expert_forward.9
  307.0 24.1 %all_to_all.89.refs_0_ = bf16[32,96,128]{2,1,0:T(8,128)(2,1)S(1)} all-to-all(bf16[32,96,128]{2,1,0:T(8,128)(2,1)S(1)} %get-tuple-element.117), channel_id=1, replica_groups=mesh['pipe'=4,'expert'=32,'dp'=2] {'expert'}, dimensions={0} | all-to-all | bytes 1572864 | tf_op jit(solution)/shard_map/all_to_all | solution.py:326
  335.8 24.0 %all_to_all.90.refs_0_ = bf16[32,96,128]{2,1,0:T(8,128)(2,1)S(1)} all-to-all(bf16[32,96,128]{2,1,0:T(8,128)(2,1)S(1)} %dispatch.13), channel_id=1, replica_groups=mesh['pipe'=4,'expert'=32,'dp'=2] {'expert'}, dimensions={0} | all-to-all | bytes 1572864 | tf_op jit(solution)/shard_map/all_to_all | solution.py:326
  360.4 23.9 %all_to_all.91.refs_0_ = bf16[32,96,128]{2,1,0:T(8,128)(2,1)S(1)} all-to-all(bf16[32,96,128]{2,1,0:T(8,128)(2,1)S(1)} %get-tuple-element.122), channel_id=1, replica_groups=mesh['pipe'=4,'expert'=32,'dp'=2] {'expert'}, dimensions={0} | all-to-all | bytes 1572864 | tf_op jit(solution)/shard_map/all_to_all | solution.py:326
  387.6 28.2 %collective-permute-done.5.refs_0_.refs_4_ = bf16[64,2048]{1,0:T(8,128)(2,1)S(1)} collective-permute-done((bf16[64,2048]{1,0:T(8,128)(2,1)S(1)}, bf16[64,2048]{1,0:T(8,128)(2,1)S(1)}, u32[]{:S(2)}, u32[]{:S(2)}) %collective-permute-start.5) | collective-permute-done | bytes 262176 | tf_op jit(solution)/shard_map/ppermute | solution.py:454
  417.8 19.3 %all_to_all.92.refs_0_ = bf16[32,96,128]{2,1,0:T(8,128)(2,1)S(1)} all-to-all(bf16[32,96,128]{2,1,0:T(8,128)(2,1)S(1)} %dispatch.14), channel_id=1, replica_groups=mesh['pipe'=4,'expert'=32,'dp'=2] {'expert'}, dimensions={0} | all-to-all | bytes 1572864 | tf_op jit(solution)/shard_map/all_to_all | solution.py:326
  437.1 7.0 %expert_backward.8 = (bf16[32,96,128]{2,1,0:T(8,128)(2,1)S(1)}, f32[32,2048]{1,0:T(8,128)S(1)}, f32[2,16,768]{2,1,0:T(8,128)S(1)}, f32[16,768]{1,0:T(8,128)S(1)}, f32[16,2048]{1,0:T(8,128)S(1)}) custom-call(s32[96]{0:T(128)S(1)} %dynamic-slice_bitcast_fusion.flags, ...), custom_call_target="tpu_custom_call", output_to_operand_aliasing={{1}: (3, {}), {2}: (4, {}), {3}: (5, {}), {4}: (6, {})} | custom-call | tf_op jit(solution)/shard_map/expert_backward/pallas_call | solution.py:389
  444.1 19.4 %all_to_all.93.refs_0_ = bf16[32,96,128]{2,1,0:T(8,128)(2,1)S(1)} all-to-all(bf16[32,96,128]{2,1,0:T(8,128)(2,1)S(1)} %get-tuple-element.128), channel_id=1, replica_groups=mesh['pipe'=4,'expert'=32,'dp'=2] {'expert'}, dimensions={0} | all-to-all | bytes 1572864 | tf_op jit(solution)/shard_map/all_to_all | solution.py:326
  466.8 6.1 %collective-permute-done.6.refs_0_.refs_2_ = bf16[64,2048]{1,0:T(8,128)(2,1)S(1)} collective-permute-done((bf16[64,2048]{1,0:T(8,128)(2,1)S(1)}, bf16[64,2048]{1,0:T(8,128)(2,1)S(1)}, u32[]{:S(2)}, u32[]{:S(2)}) %collective-permute-start.6) | collective-permute-done | bytes 262176 | tf_op jit(solution)/shard_map/ppermute | solution.py:454
  474.8 19.4 %all_to_all.94.refs_0_ = bf16[32,96,128]{2,1,0:T(8,128)(2,1)S(1)} all-to-all(bf16[32,96,128]{2,1,0:T(8,128)(2,1)S(1)} %dispatch.15), channel_id=1, replica_groups=mesh['pipe'=4,'expert'=32,'dp'=2] {'expert'}, dimensions={0} | all-to-all | bytes 1572864 | tf_op jit(solution)/shard_map/all_to_all | solution.py:326
  494.2 7.2 %expert_backward.9 = (bf16[32,96,128]{2,1,0:T(8,128)(2,1)S(1)}, f32[32,2048]{1,0:T(8,128)S(1)}, f32[2,16,768]{2,1,0:T(8,128)S(1)}, f32[16,768]{1,0:T(8,128)S(1)}, f32[16,2048]{1,0:T(8,128)S(1)}) custom-call(s32[96]{0:T(128)S(1)} %dynamic-slice_bitcast_fusion.flags, ...), custom_call_target="tpu_custom_call", output_to_operand_aliasing={{1}: (2, {}), {2}: (3, {}), {3}: (4, {}), {4}: (5, {})} | custom-call | tf_op jit(solution)/shard_map/expert_backward/pallas_call | solution.py:389
  502.3 4.7 all-to-all-start.15
  507.0 14.9 %all-to-all-done.15.refs_0_ = bf16[32,96,128]{2,1,0:T(8,128)(2,1)S(1)} async-done(((bf16[32,96,128]{2,1,0:T(8,128)(2,1)}), bf16[32,96,128]{2,1,0:T(8,128)(2,1)S(1)}, u32[]{:S(2)}, u32[]{:S(2)}) %all-to-all-start.15) | async-done | bytes 786464 | tf_op jit(solution)/shard_map/all_to_all | solution.py:326
  524.9 18.6 %collective-permute-start.7 = (bf16[32,2048]{1,0:T(8,128)(2,1)S(1)}, bf16[32,2048]{1,0:T(8,128)(2,1)S(1)}, u32[]{:S(2)}, u32[]{:S(2)}) collective-permute-start(bf16[32,2048]{1,0:T(8,128)(2,1)S(1)} %convert_element_type.36), channel_id=1, source_target_pairs={{0,1},{1,0},{2,3},{3,2},{4,5},{5,4},{6,7},{7,6},{8,9},{9,8},{10,11... | collective-permute-start | bytes 393224 | tf_op jit(solution)/shard_map/ppermute | solution.py:466
  (89 shorter events, 55.8 us)
Async XLA Ops:
  0.6 40.6 %copy-start.6 = (bf16[1,1,2048,32]{2,3,1,0:T(8,128)(2,1)S(1)}, bf16[1,1,2048,32]{2,3,1,0:T(8,128)(2,1)}, u32[]{:S(2)}) copy-start(bf16[1,1,2048,32]{2,3,1,0:T(8,128)(2,1)} %param.21) | copy-start | bytes 393220
  3.1 1.0 copy-start.7
  4.1 0.7 copy-start.12
  4.8 1.0 copy-start.14
  5.9 35.4 %copy-start.9 = (bf16[1,1,16,2048]{3,2,1,0:T(8,128)(2,1)S(1)}, bf16[1,1,16,2048]{3,2,1,0:T(8,128)(2,1)}, u32[]{:S(2)}) copy-start(bf16[1,1,16,2048]{3,2,1,0:T(8,128)(2,1)} %param.24) | copy-start | bytes 196612
  5.9 35.4 %copy-start.10 = (bf16[1,1,2,16,768]{4,3,2,1,0:T(8,128)(2,1)S(1)}, bf16[1,1,2,16,768]{4,3,2,1,0:T(8,128)(2,1)}, u32[]{:S(2)}) copy-start(bf16[1,1,2,16,768]{4,3,2,1,0:T(8,128)(2,1)} %param.22) | copy-start | bytes 147460
  5.9 35.4 %copy-start.11 = (bf16[1,1,768,16]{2,3,1,0:T(8,128)(2,1)S(1)}, bf16[1,1,768,16]{2,3,1,0:T(8,128)(2,1)}, u32[]{:S(2)}) copy-start(bf16[1,1,768,16]{2,3,1,0:T(8,128)(2,1)} %param.23) | copy-start | bytes 73732
  41.3 1.9 copy-start
  43.1 1.9 copy-start.2
  45.0 1.9 copy-start.4
  46.9 31.0 %copy-start.13 = (f32[1,2048]{1,0:T(1,128)S(1)}, f32[1,2048]{1,0:T(1,128)}, u32[]{:S(2)}) copy-start(f32[1,2048]{1,0:T(1,128)} %refs_3_.7) | copy-start | bytes 24580
  46.9 39.6 %copy-start.8 = (bf16[2,64,2048]{2,1,0:T(8,128)(2,1)S(1)}, bf16[2,64,2048]{2,1,0:T(8,128)(2,1)}, u32[]{:S(2)}) copy-start(bf16[2,64,2048]{2,1,0:T(8,128)(2,1)} %refs_3_.6) | copy-start | bytes 1572868
  46.9 39.6 %copy-start.15 = (bf16[2,64,2048]{2,1,0:T(8,128)(2,1)S(1)}, bf16[2,64,2048]{2,1,0:T(8,128)(2,1)}, u32[]{:S(2)}) copy-start(bf16[2,64,2048]{2,1,0:T(8,128)(2,1)} %refs_0_.3) | copy-start | bytes 1572868
  46.9 69.4 %copy-start.5 = (bf16[1,1,768,2048]{3,2,1,0:T(8,128)(2,1)S(1)}, bf16[1,1,768,2048]{3,2,1,0:T(8,128)(2,1)}, u32[]{:S(2)}) copy-start(bf16[1,1,768,2048]{3,2,1,0:T(8,128)(2,1)} %param.20) | copy-start | bytes 9437188
  52.3 64.0 %copy-start.1 = (bf16[1,1,2048,768]{3,2,1,0:T(8,128)(2,1)S(1)}, bf16[1,1,2048,768]{3,2,1,0:T(8,128)(2,1)}, u32[]{:S(2)}) copy-start(bf16[1,1,2048,768]{3,2,1,0:T(8,128)(2,1)} %param.18) | copy-start | bytes 9437188
  52.3 64.0 %copy-start.3 = (bf16[1,1,2048,768]{3,2,1,0:T(8,128)(2,1)S(1)}, bf16[1,1,2048,768]{3,2,1,0:T(8,128)(2,1)}, u32[]{:S(2)}) copy-start(bf16[1,1,2048,768]{3,2,1,0:T(8,128)(2,1)} %param.19) | copy-start | bytes 9437188
  80.0 6.6 %collective-permute-start = (bf16[64,2048]{1,0:T(8,128)(2,1)S(1)}, bf16[64,2048]{1,0:T(8,128)(2,1)S(1)}, u32[]{:S(2)}, u32[]{:S(2)}) collective-permute-start(bf16[64,2048]{1,0:T(8,128)(2,1)S(1)} %combine.8), channel_id=1, source_target_pairs={{0,64},{1,65},{2,66},{3,67},{4,68},{5,69},{6,70},{7,71},{8,72},{9,... | collective-permute-start | bytes 786440 | tf_op jit(solution)/shard_map/ppermute | solution.py:454
  148.3 7.8 %collective-permute-start.1 = (bf16[64,2048]{1,0:T(8,128)(2,1)S(1)}, bf16[64,2048]{1,0:T(8,128)(2,1)S(1)}, u32[]{:S(2)}, u32[]{:S(2)}) collective-permute-start(bf16[64,2048]{1,0:T(8,128)(2,1)S(1)} %combine.9), channel_id=1, source_target_pairs={{64,128},{0,64},{65,129},{1,65},{66,130},{2,66},{67,131},{3,67},{6... | collective-permute-start | bytes 786440 | tf_op jit(solution)/shard_map/ppermute | solution.py:454
  213.8 0.7 collective-permute-start.2
  272.9 0.7 collective-permute-start.3
  333.2 27.2 %copy-start.18 = (bf16[64,2048]{1,0:T(8,128)(2,1)}, bf16[64,2048]{1,0:T(8,128)(2,1)S(1)}, u32[]{:S(2)}) copy-start(bf16[64,2048]{1,0:T(8,128)(2,1)S(1)} %combine.12) | copy-start | bytes 786436
  333.2 0.7 collective-permute-start.4
  386.3 29.5 %collective-permute-start.5 = (bf16[64,2048]{1,0:T(8,128)(2,1)S(1)}, bf16[64,2048]{1,0:T(8,128)(2,1)S(1)}, u32[]{:S(2)}, u32[]{:S(2)}) collective-permute-start(bf16[64,2048]{1,0:T(8,128)(2,1)S(1)} %combine.13), channel_id=1, source_target_pairs={{64,0},{128,64},{65,1},{129,65},{66,2},{130,66},{67,3},{131,67},{6... | collective-permute-start | bytes 786440 | tf_op jit(solution)/shard_map/ppermute | solution.py:454
  465.5 7.4 %collective-permute-start.6 = (bf16[64,2048]{1,0:T(8,128)(2,1)S(1)}, bf16[64,2048]{1,0:T(8,128)(2,1)S(1)}, u32[]{:S(2)}, u32[]{:S(2)}) collective-permute-start(bf16[64,2048]{1,0:T(8,128)(2,1)S(1)} %combine.14), channel_id=1, source_target_pairs={{64,0},{65,1},{66,2},{67,3},{68,4},{69,5},{70,6},{71,7},{72,8},{73... | collective-permute-start | bytes 786440 | tf_op jit(solution)/shard_map/ppermute | solution.py:454
  472.9 21.3 %copy-start.16 = (bf16[64,2048]{1,0:T(8,128)(2,1)}, bf16[64,2048]{1,0:T(8,128)(2,1)S(1)}, u32[]{:S(2)}) copy-start(bf16[64,2048]{1,0:T(8,128)(2,1)S(1)} %collective-permute-done.6.refs_0_.refs_2_) | copy-start | bytes 786436
  501.4 0.9 copy-start.19
  502.3 19.6 %all-to-all-start.15 = ((bf16[32,96,128]{2,1,0:T(8,128)(2,1)}), bf16[32,96,128]{2,1,0:T(8,128)(2,1)S(1)}, u32[]{:S(2)}, u32[]{:S(2)}) async-start(bf16[32,96,128]{2,1,0:T(8,128)(2,1)} %copy-done.19), calls=%async_computation.15 | async-start | bytes 1572864 | tf_op jit(solution)/shard_map/all_to_all | solution.py:326
  521.9 1.0 copy-start.17
  524.9 23.4 %collective-permute-start.7 = (bf16[32,2048]{1,0:T(8,128)(2,1)S(1)}, bf16[32,2048]{1,0:T(8,128)(2,1)S(1)}, u32[]{:S(2)}, u32[]{:S(2)}) collective-permute-start(bf16[32,2048]{1,0:T(8,128)(2,1)S(1)} %convert_element_type.36), channel_id=1, source_target_pairs={{0,1},{1,0},{2,3},{3,2},{4,5},{5,4},{6,7},{7,6},{8,9},{9,8},{10,11... | collective-permute-start | bytes 393224 | tf_op jit(solution)/shard_map/ppermute | solution.py:466
  543.5 3.5 collective-permute-start.8
  543.6 2.8 collective-permute-start.9
  544.1 3.6 collective-permute-start.10
  (2 other events, 1.4 us)

commit v3 on v2

--- a/solution.py
+++ b/solution.py
@@ -27,25 +27,18 @@
     return lax.dot_general(left, right, (((0,), (0,)), ((), ())), preferred_element_type=F32)
 
 
-def pack(read, out_ref, wide, peers, chunks):
+def pack(columns, out_ref, wide, peers, chunks):
     stride = SLOTS * chunks
-    for slot in range(SLOTS):
-        for chunk in range(chunks):
-            wide[pl.ds(slot * chunks + chunk, peers, stride=stride), :] = read(slot, chunk)
+    step = 4
+    for first in range(0, chunks, step):
+        block = columns(first * LANES, step * LANES)
+        for slot in range(SLOTS):
+            for chunk in range(step):
+                wide[pl.ds(slot * chunks + first + chunk, peers, stride=stride), :] = block[
+                    slot * peers : (slot + 1) * peers, chunk * LANES : (chunk + 1) * LANES
+                ]
     for peer in range(peers):
         out_ref[peer] = wide[peer * stride : (peer + 1) * stride, :].astype(BF16)
-
-
-def pack_from(rows, out_ref, wide, peers, chunks):
-    pack(
-        lambda slot, chunk: rows[
-            slot * peers : (slot + 1) * peers, chunk * LANES : (chunk + 1) * LANES
-        ],
-        out_ref,
-        wide,
-        peers,
-        chunks,
-    )
 
 
 def unpack(in_ref, rows, wide, peers, chunks):
@@ -64,7 +57,7 @@
     return high, (weight - high.astype(F32)).astype(BF16)
 
 
-def tables_kernel(peers, routes, gates, place, scale_hi, scale_lo, pick, mix_hi, mix_lo):
+def make_tables(peers, routes, gates, place, scale_hi, scale_lo, pick, mix_hi, mix_lo):
     micros, _, rows = routes.shape
     slots = SLOTS * peers
     assert peers & (peers - 1) == 0
@@ -96,24 +89,32 @@
     return value
 
 
-def dispatch_kernel(dims, kinds, source_count, flags, *refs):
-    peers, chunks, base, tick = dims
-    sources = refs[:source_count]
-    gain, place, scale_hi, scale_lo = refs[source_count : source_count + 4]
-    out_ref = refs[source_count + 4]
-    wide, rows = refs[-2:]
+def dispatch_rows(dims, kinds, current, flags, gain, place, scale_hi, scale_lo, out_ref, wide, rows):
+    peers, chunks, base = dims
     is_forward, micro = flags[base], flags[base + 1]
-    current = choose(sources, tick, flags[base + 2])
-    if source_count > 1:
-        refs[source_count + 5][...] = current
 
     def forward():
         values = current.astype(F32)
         inverse = lax.rsqrt(jnp.mean(values * values, axis=-1, keepdims=True) + EPS)
-        rows[...] = dot(place[micro], (values * inverse * gain[...]).astype(BF16))
+        rows[...] = (values * inverse * gain[...]).astype(BF16)
+        pack(
+            lambda start, size: dot(place[micro], rows[:, start : start + size]),
+            out_ref,
+            wide,
+            peers,
+            chunks,
+        )
 
     def backward():
-        rows[...] = dot(scale_hi[micro], current) + dot(scale_lo[micro], current)
+        rows[...] = current
+        pack(
+            lambda start, size: dot(scale_hi[micro], rows[:, start : start + size])
+            + dot(scale_lo[micro], rows[:, start : start + size]),
+            out_ref,
+            wide,
+            peers,
+            chunks,
+        )
 
     if kinds == "F":
         forward()
@@ -122,15 +123,49 @@
     else:
         pl.when(is_forward == 1)(forward)
         pl.when(is_forward == 0)(backward)
-    pack_from(rows, out_ref, wide, peers, chunks)
-
-
-def combine_kernel(dims, kinds, section_count, grad_count, flags, *refs):
+
+
+def dispatch_kernel(dims, kinds, source_count, flags, *refs):
+    peers, chunks, base, tick = dims
+    sources = refs[:source_count]
+    gain, place, scale_hi, scale_lo, out_ref = refs[source_count : source_count + 5]
+    wide, rows = refs[-2:]
+    current = choose(sources, tick, flags[base + 2])
+    if source_count > 1:
+        refs[source_count + 5][...] = current
+    dispatch_rows(
+        (peers, chunks, base),
+        kinds,
+        current,
+        flags,
+        gain,
+        place,
+        scale_hi,
+        scale_lo,
+        out_ref,
+        wide,
+        rows,
+    )
+
+
+def opening_kernel(dims, flags, routes, gates, tokens, cotangent, gain, *refs):
+    peers, chunks = dims
+    tables, out_ref, first, wide, rows = refs[:6], *refs[6:]
+    make_tables(peers, routes, gates, *tables)
+    current = choose([tokens, cotangent], 0, flags[2])
+    first[...] = current
+    dispatch_rows(
+        (peers, chunks, 0), "FB", current, flags, gain, *tables[:3], out_ref, wide, rows
+    )
+
+
+def combine_kernel(dims, kinds, section_count, grad_count, has_final, flags, *refs):
     peers, chunks, base, grad_micro = dims
     returned = refs[0]
     sections = refs[1 : 1 + section_count]
     grads = refs[1 + section_count : 1 + section_count + grad_count]
-    gain, pick, mix_hi, mix_lo, out_ref, wide, rows = refs[1 + section_count + grad_count :]
+    gain, pick, mix_hi, mix_lo = refs[1 + section_count + grad_count :][:4]
+    out_ref, wide, rows = refs[-3:]
     is_forward, micro = flags[base], flags[base + 1]
     unpack(returned, rows, wide, peers, chunks)
 
@@ -145,7 +180,17 @@
         scaled = dot(pick[micro], rows[...]) * gain[...]
         normed = section_in * inverse
         shared = jnp.mean(scaled * normed, axis=-1, keepdims=True)
-        out_ref[...] = (grad_next + inverse * (scaled - normed * shared)).astype(BF16)
+        result = (grad_next + inverse * (scaled - normed * shared)).astype(BF16)
+        if has_final:
+            final = refs[-4]
+            out_ref[...] = final[...]
+
+            @pl.when(flags[base + 2 - 6] == 1)
+            def _():
+                out_ref[1] = result
+
+        else:
+            out_ref[...] = result
 
     if kinds == "F":
         forward()
@@ -156,11 +201,26 @@
         pl.when(is_forward == 0)(backward)
 
 
+def assemble_kernel(flags, *refs):
+    mixed, (hidden, input_grads) = refs[:-2], refs[-2:]
+    for micro in range(hidden.shape[0]):
+        kept = [mixed[micro], mixed[1 + micro], mixed[2 + micro], mixed[5 + micro]]
+        hidden[micro] = choose(kept, 0, flags[3])
+        kept = [mixed[min(6, 6 + micro - rank)] for rank in range(4)]
+        input_grads[micro] = choose(kept, 0, flags[3])
+
+
+def sum_kernel(*refs):
+    count = len(refs) // 3
+    for own, other, out in zip(refs[:count], refs[count : 2 * count], refs[2 * count :]):
+        out[...] = own[...].astype(F32) + other[...].astype(F32)
+
+
 def forward_kernel(
     dims, has_store, received, w_gate, w_up, w_down, in_a, in_b, down_a, down_b, *refs
 ):
     peers, chunks, low_rank, block, slot = dims
-    sent, rows, low_in, gate_pre, up_pre, wide, total = refs[4 * has_store :]
+    sent, rows, low_in, gate_pre, up_pre, wide, acts = refs[4 * has_store :]
     slots = rows.shape[1]
     unpack(received, rows.at[slot], wide, peers, chunks)
     slot_rows = rows[slot]
@@ -175,20 +235,26 @@
         up_pre[slot, :, piece] = up
         activated = (gate * jax.nn.sigmoid(gate) * up).astype(BF16)
         low_total += dot_nt(activated, down_a[:, piece])
-        part = dot(activated, w_down[piece, :])
-        total[...] = part if start == 0 else total[...] + part
-    total[...] += dot(low_total.astype(BF16), down_b[...])
-    pack_from(total, sent, wide, peers, chunks)
-
-
-def backward_kernel(dims, received_count, has_other, has_totals, flags, *refs):
+        acts[:, piece] = activated
+    low_down = low_total.astype(BF16)
+    pack(
+        lambda start, size: dot(acts[...], w_down[:, start : start + size])
+        + dot(low_down, down_b[:, start : start + size]),
+        sent,
+        wide,
+        peers,
+        chunks,
+    )
+
+
+def backward_kernel(dims, received_count, has_other, has_totals, is_last, flags, *refs):
     peers, chunks, low_rank, block, base = dims
     received = refs[:received_count]
     other = refs[received_count]
     refs = refs[received_count + has_other + 4 * has_totals :]
     (rows, low_in, gate_pre, up_pre, w_gate, w_up, w_down, in_a, in_b, down_a, down_b) = refs[:11]
     (sent, grad_in_a, grad_in_b, grad_down_a, grad_down_b) = refs[11:16]
-    (wide, grad_out, total) = refs[16:]
+    (wide, grad_out, total) = refs[-3:]
     active, slot = flags[base] == 1, flags[base + 1]
     slots = rows.shape[1]
 
@@ -230,8 +296,14 @@
             part = dot_nt(grad_gate, w_gate[:, piece]) + dot_nt(grad_up, w_up[:, piece])
             total[...] = part if start == 0 else total[...] + part
         low_grad = jnp.concatenate([gate_low, up_low], axis=1).astype(BF16)
-        total[...] += dot(low_grad, in_a[...])
-        pack_from(total, sent, wide, peers, chunks)
+        pack(
+            lambda start, size: total[:, start : start + size]
+            + dot(low_grad, in_a[:, start : start + size]),
+            sent,
+            wide,
+            peers,
+            chunks,
+        )
         store(grad_in_a, ..., dot_tn(low_grad, rows[slot]))
         store(grad_down_b, ..., dot_tn(low_total.astype(BF16), grad))
 
@@ -240,6 +312,10 @@
         @pl.when(jnp.logical_not(active))
         def _():
             sent[...] = other[...]
+
+    if is_last:
+        for total, rounded in zip(refs[12:16], refs[16:20]):
+            rounded[...] = total[...].astype(BF16)
 
 
 def params(megabytes):
@@ -254,6 +330,7 @@
     for rank in range(sections):
         for tick in range(ticks):
             row = table[rank, tick]
+            row[3] = rank
             forward = tick - rank if tick - rank in (0, 1) else None
             backward = tick - (2 * last - rank)
             backward = backward if backward in (0, 1) else None
@@ -313,14 +390,17 @@
     scalars = pl.BlockSpec(memory_space=pltpu.SMEM)
     table_in = jax.ShapeDtypeStruct((micros, slots, tok_rows), BF16)
     table_out = jax.ShapeDtypeStruct((micros, tok_rows, slots), BF16)
-    place, scale_hi, scale_lo, pick, mix_hi, mix_lo = pl.pallas_call(
-        functools.partial(tables_kernel, peers),
-        out_shape=[table_in] * 3 + [table_out] * 3,
-        in_specs=[held] * 2,
-        out_specs=[held] * 6,
-        compiler_params=params(8),
-        name="tables",
-    )(routes.transpose(0, 2, 1), gates.transpose(0, 2, 1))
+    *tables, placed_first, input_first = pl.pallas_call(
+        functools.partial(opening_kernel, (peers, chunks)),
+        out_shape=[table_in] * 3 + [table_out] * 3 + [buffer, block_rows],
+        in_specs=[scalars] + [held] * 5,
+        out_specs=[held] * 8,
+        scratch_shapes=[wide, pltpu.VMEM((tok_rows, model), BF16)],
+        compiler_params=params(20),
+        name="opening",
+    )(flags, routes.transpose(0, 2, 1), gates.transpose(0, 2, 1), tokens, cotangent, norm_gain)
+    place, scale_hi, scale_lo, pick, mix_hi, mix_lo = tables
+    weights = (w_gate, w_up, w_down, in_a, in_b, down_a, down_b)
 
     def exchange(rows):
         return lax.all_to_all(rows, "expert", split_axis=0, concat_axis=0, tiled=True)
@@ -335,14 +415,15 @@
             out_shape=[buffer] if single else [buffer, block_rows],
             in_specs=[scalars] + [held] * len(operands),
             out_specs=[held] * (1 if single else 2),
-            scratch_shapes=[wide, pltpu.VMEM((slots, model), F32)],
+            scratch_shapes=[wide, pltpu.VMEM((tok_rows, model), BF16)],
             compiler_params=params(20),
             name="dispatch",
         )(flags, *operands)
         return result[0], sources[0] if single else result[1]
 
-    def combine(tick, kinds, returned, section_inputs, grads):
-        operands = [returned, *section_inputs, *grads, norm_gain, pick, mix_hi, mix_lo]
+    def combine(tick, kinds, returned, section_inputs, grads, final):
+        finals = [] if final is None else [final]
+        operands = [returned, *section_inputs, *grads, norm_gain, pick, mix_hi, mix_lo, *finals]
         return pl.pallas_call(
             functools.partial(
                 combine_kernel,
@@ -350,16 +431,17 @@
                 kinds,
                 len(section_inputs),
                 len(grads),
+                len(finals) > 0,
             ),
-            out_shape=block_rows,
+            out_shape=block_rows if final is None else jax.ShapeDtypeStruct(final.shape, BF16),
             in_specs=[scalars] + [held] * len(operands),
             out_specs=held,
+            input_output_aliases={len(operands): 0} if finals else {},
             scratch_shapes=[wide, pltpu.VMEM((slots, model), BF16)],
             compiler_params=params(20),
             name="combine",
         )(flags, *operands)
 
-    weights = (w_gate, w_up, w_down, in_a, in_b, down_a, down_b)
     state_shapes = [
         jax.ShapeDtypeStruct((forward_ticks, slots, model), BF16),
         jax.ShapeDtypeStruct((forward_ticks, slots, 2 * low_rank), BF16),
@@ -374,7 +456,7 @@
             out_shape=[buffer] + state_shapes,
             in_specs=[held] * (12 if has_store else 8),
             out_specs=[held] * 5,
-            scratch_shapes=[wide, pltpu.VMEM((slots, model), F32)],
+            scratch_shapes=[wide, pltpu.VMEM((slots, hidden_width), BF16)],
             input_output_aliases={8: 1, 9: 2, 10: 3, 11: 4} if has_store else {},
             compiler_params=params(20),
             name="expert_forward",
@@ -386,6 +468,13 @@
         others = [] if other is None else [other]
         operands = [*received, *others, *totals, *state, *weights]
         first = 1 + len(received) + len(others)
+        is_last = tick == ticks - 1
+        sums = [
+            (2 * low_rank, model),
+            (2, low_rank, hidden_width),
+            (low_rank, hidden_width),
+            (low_rank, model),
+        ]
         return pl.pallas_call(
             functools.partial(
                 backward_kernel,
@@ -393,16 +482,13 @@
                 len(received),
                 len(others),
                 len(totals) > 0,
+                is_last,
             ),
-            out_shape=[
-                buffer,
-                jax.ShapeDtypeStruct((2 * low_rank, model), F32),
-                jax.ShapeDtypeStruct((2, low_rank, hidden_width), F32),
-                jax.ShapeDtypeStruct((low_rank, hidden_width), F32),
-                jax.ShapeDtypeStruct((low_rank, model), F32),
-            ],
+            out_shape=[buffer]
+            + [jax.ShapeDtypeStruct(shape, F32) for shape in sums]
+            + [jax.ShapeDtypeStruct(shape, BF16) for shape in sums * is_last],
             in_specs=[scalars] + [held] * len(operands),
-            out_specs=[held] * 5,
+            out_specs=[held] * (9 if is_last else 5),
             input_output_aliases={first + item: 1 + item for item in range(len(totals))},
             scratch_shapes=[
                 wide,
@@ -425,14 +511,15 @@
     inputs, got, sent, mixed = {}, {}, {}, {}
     state, totals = None, ()
     for tick in range(ticks):
+        if tick == 1:
+            sources = [tokens, incoming, cotangent]
+        elif tick > 1:
+            sources = [incoming]
+        kinds = {1: "FB", 2: "F", 3: "F", 4: "FB"}.get(tick, "B")
         if tick == 0:
-            sources = [tokens, cotangent]
-        elif tick == 1:
-            sources = [tokens, incoming, cotangent]
+            placed, inputs[tick] = placed_first, input_first
         else:
-            sources = [incoming]
-        kinds = {0: "FB", 1: "FB", 2: "F", 3: "F", 4: "FB"}.get(tick, "B")
-        placed, inputs[tick] = dispatch(tick, kinds, sources)
+            placed, inputs[tick] = dispatch(tick, kinds, sources)
         got[tick] = exchange(placed)
         if tick < forward_ticks:
             sent[tick], state = expert_forward(tick, got[tick], state)
@@ -442,35 +529,44 @@
             other = sent[{3: 3, 5: 3, 6: 4}[tick]] if tick in (3, 5, 6) else None
             answer, *totals = expert_backward(tick, received, other, state, totals)
         returned = exchange(answer)
+        if tick == ticks - 1:
+            returned, rounded = lax.optimization_barrier((returned, totals[4:]))
         section_inputs = {4: (4, 2), 5: (3, 1), 6: (2, 0, 4), 7: (1,)}.get(tick, (tick,))
         grads = {3: [cotangent], 4: [cotangent, inputs[tick]]}.get(
             tick, [inputs[tick]] if tick > 4 else []
         )
         kinds = "F" if tick < 3 else "B" if tick in (4, 7) else "FB"
+        final = input_grads if tick == ticks - 1 else None
         mixed[tick] = combine(
-            tick, kinds, returned, [inputs[index] for index in section_inputs], grads
+            tick, kinds, returned, [inputs[index] for index in section_inputs], grads, final
         )
         if tick < ticks - 1:
             incoming = lax.ppermute(mixed[tick], "pipe", hops[tick])
-
-    mixed, totals = lax.optimization_barrier((mixed, totals))
-
-    def by_rank(choices):
-        value = choices[0]
-        for rank in range(1, sections):
-            value = jnp.where(section_index == rank, choices[rank], value)
-        return value
-
-    def summed(total):
-        total = total.astype(BF16)
-        across = lax.ppermute(total, "dp", [(0, 1), (1, 0)])
-        return total.astype(F32) + across.astype(F32)
-
-    totals = [summed(total) for total in totals]
-    hidden = jnp.stack(
-        [by_rank([mixed[m], mixed[1 + m], mixed[2 + m], mixed[5 + m]]) for m in range(micros)]
-    )
-    input_grads = jnp.stack([by_rank([mixed[6 - r + m] for r in range(4)]) for m in range(micros)])
+        if tick == ticks - 2:
+            pair = jax.ShapeDtypeStruct((micros, tok_rows, model), BF16)
+            hidden, input_grads = pl.pallas_call(
+                assemble_kernel,
+                out_shape=[pair] * 2,
+                in_specs=[scalars] + [held] * (ticks - 1),
+                out_specs=[held] * 2,
+                compiler_params=params(8),
+                name="assemble",
+            )(flags, *[mixed[index] for index in range(ticks - 1)])
+            incoming, hidden, input_grads = lax.optimization_barrier(
+                (incoming, hidden, input_grads)
+            )
+
+    input_grads = mixed[ticks - 1]
+
+    across = [lax.ppermute(total, "dp", [(0, 1), (1, 0)]) for total in rounded]
+    totals = pl.pallas_call(
+        sum_kernel,
+        out_shape=[jax.ShapeDtypeStruct(total.shape, F32) for total in rounded],
+        in_specs=[held] * (2 * len(rounded)),
+        out_specs=[held] * len(rounded),
+        compiler_params=params(8),
+        name="sums",
+    )(*rounded, *across)
     return (
         hidden[None],
         input_grads[None],

time: 558 us -> 551 us (0.987)
  blocking collectives: 361 us -> 381 us
  waiting for transfers between devices: 55.8 us -> 39 us
    all_to_all x15 -> x16, blocking collectives: 361 us -> 381 us  [exchange(): lax.all_to_all(rows, 'expert', split_axis=0, concat_axis=0, tiled=True)]
    all_to_all x1 -> x0, waiting for transfers between devices: 14.9 us -> none  [exchange(): lax.all_to_all(rows, 'expert', split_axis=0, concat_axis=0, tiled=True)]
    pallas_call x8 -> x7, Pallas kernels: 17.8 us -> 12.7 us  [dispatch(): pl.pallas_call(functools.partial(dispatch_kernel, (peers, chunks, tick *...]
    unnamed x44 -> x42, local copies, waits for them, and re-layouts: 11.7 us -> 13.1 us
  transfers between devices with their start and end apart: 12 -> 11, of which waited for: 5 -> 4; matrix products, arithmetic and copies ran while one was open for 1% -> 0% of each run, Pallas kernels for 0% -> 1%
where the time goes in v3:
time: 551 us; the launch traced here: 541 us
  blocking collectives  381 us (69%)
  Pallas kernels  75.3 us (14%)
  waiting for transfers between devices  39 us (7%)
  starting transfers between devices  30.9 us (6%)
  local copies, waits for them, and re-layouts  13.8 us (3%)
    all_to_all x16, blocking collectives, exchange(): lax.all_to_all(rows, 'expert', split_axis=0, concat_axis=0, tiled=True)  381 us
    ppermute x7, waiting for transfers between devices, body(): incoming = lax.ppermute(mixed[tick], 'pipe', hops[tick])  39 us
    pallas_call x5, Pallas kernels, expert_forward(): pl.pallas_call(functools.partial(forward_kernel, (peers, chunks, low_rank...  24.2 us
    ppermute x4, starting transfers between devices, body(): across = [lax.ppermute(total, 'dp', [(0, 1), (1, 0)]) for total in rounded]  19 us
    pallas_call x8, Pallas kernels, combine(): pl.pallas_call(functools.partial(combine_kernel, (peers, chunks, tick * 1...  17.6 us
    pallas_call x5, Pallas kernels, expert_backward(): pl.pallas_call(functools.partial(backward_kernel, (peers, chunks, low_ran...  16 us
    unnamed x42, local copies, waits for them, and re-layouts  13.1 us
    pallas_call x7, Pallas kernels, dispatch(): pl.pallas_call(functools.partial(dispatch_kernel, (peers, chunks, tick *...  12.7 us
  transfers between devices with their start and end apart: 11, of which 4 were waited for; matrix products, arithmetic and copies ran while one was open for 0% of the time, Pallas kernels for 1%

profile of v3, /device:TPU:1, one launch (start us, length us, event | category | flops | bytes accessed | tf_op | source)
XLA Modules:
  0.0 541.4 jit_solution(4968297272806458860)
XLA Ops:
  5.5 2.1 opening.1
  7.6 32.7 %all_to_all.80.received.refs_0_ = bf16[32,96,128]{2,1,0:T(8,128)(2,1)S(1)} all-to-all(bf16[32,96,128]{2,1,0:T(8,128)(2,1)S(1)} %get-tuple-element.80), channel_id=1, replica_groups=mesh['pipe'=4,'expert'=32,'dp'=2] {'expert'}, dimensions={0} | all-to-all | bytes 1572864 | tf_op jit(solution)/shard_map/all_to_all | solution.py:406
  49.3 4.8 expert_forward.5
  54.2 25.6 %all_to_all.81.refs_0_ = bf16[32,96,128]{2,1,0:T(8,128)(2,1)S(1)} all-to-all(bf16[32,96,128]{2,1,0:T(8,128)(2,1)S(1)} %get-tuple-element.81), channel_id=1, replica_groups=mesh['pipe'=4,'expert'=32,'dp'=2] {'expert'}, dimensions={0} | all-to-all | bytes 1572864 | tf_op jit(solution)/shard_map/all_to_all | solution.py:406
  81.8 3.2 collective-permute-start
  85.1 3.3 collective-permute-done.refs_1_
  90.2 27.1 %all_to_all.82.received.refs_0_ = bf16[32,96,128]{2,1,0:T(8,128)(2,1)S(1)} all-to-all(bf16[32,96,128]{2,1,0:T(8,128)(2,1)S(1)} %get-tuple-element.89), channel_id=1, replica_groups=mesh['pipe'=4,'expert'=32,'dp'=2] {'expert'}, dimensions={0} | all-to-all | bytes 1572864 | tf_op jit(solution)/shard_map/all_to_all | solution.py:406
  117.3 4.9 expert_forward.6
  122.2 24.9 %all_to_all.83.refs_0_ = bf16[32,96,128]{2,1,0:T(8,128)(2,1)S(1)} all-to-all(bf16[32,96,128]{2,1,0:T(8,128)(2,1)S(1)} %get-tuple-element.94), channel_id=1, replica_groups=mesh['pipe'=4,'expert'=32,'dp'=2] {'expert'}, dimensions={0} | all-to-all | bytes 1572864 | tf_op jit(solution)/shard_map/all_to_all | solution.py:406
  149.2 4.1 collective-permute-start.1
  153.3 3.3 collective-permute-done.1.refs_0_.refs_1_.refs_2_
  158.4 23.9 %all_to_all.84.received = bf16[32,96,128]{2,1,0:T(8,128)(2,1)S(1)} all-to-all(bf16[32,96,128]{2,1,0:T(8,128)(2,1)S(1)} %dispatch.8), channel_id=1, replica_groups=mesh['pipe'=4,'expert'=32,'dp'=2] {'expert'}, dimensions={0} | all-to-all | bytes 1572864 | tf_op jit(solution)/shard_map/all_to_all | solution.py:406
  182.2 4.9 expert_forward.7
  187.1 24.7 %all_to_all.85.refs_0_ = bf16[32,96,128]{2,1,0:T(8,128)(2,1)S(1)} all-to-all(bf16[32,96,128]{2,1,0:T(8,128)(2,1)S(1)} %get-tuple-element.100), channel_id=1, replica_groups=mesh['pipe'=4,'expert'=32,'dp'=2] {'expert'}, dimensions={0} | all-to-all | bytes 1572864 | tf_op jit(solution)/shard_map/all_to_all | solution.py:406
  216.4 24.2 %all_to_all.86.received = bf16[32,96,128]{2,1,0:T(8,128)(2,1)S(1)} all-to-all(bf16[32,96,128]{2,1,0:T(8,128)(2,1)S(1)} %dispatch.9), channel_id=1, replica_groups=mesh['pipe'=4,'expert'=32,'dp'=2] {'expert'}, dimensions={0} | all-to-all | bytes 1572864 | tf_op jit(solution)/shard_map/all_to_all | solution.py:406
  240.6 4.8 expert_forward.8
  246.1 24.3 %all_to_all.87.refs_0_ = bf16[32,96,128]{2,1,0:T(8,128)(2,1)S(1)} all-to-all(bf16[32,96,128]{2,1,0:T(8,128)(2,1)S(1)} %get-tuple-element.110), channel_id=1, replica_groups=mesh['pipe'=4,'expert'=32,'dp'=2] {'expert'}, dimensions={0} | all-to-all | bytes 1572864 | tf_op jit(solution)/shard_map/all_to_all | solution.py:406
  275.0 24.1 %all_to_all.88.received.refs_1_ = bf16[32,96,128]{2,1,0:T(8,128)(2,1)S(1)} all-to-all(bf16[32,96,128]{2,1,0:T(8,128)(2,1)S(1)} %dispatch.10), channel_id=1, replica_groups=mesh['pipe'=4,'expert'=32,'dp'=2] {'expert'}, dimensions={0} | all-to-all | bytes 1572864 | tf_op jit(solution)/shard_map/all_to_all | solution.py:406
  299.1 4.8 expert_forward.9
  304.8 24.1 %all_to_all.89.refs_0_ = bf16[32,96,128]{2,1,0:T(8,128)(2,1)S(1)} all-to-all(bf16[32,96,128]{2,1,0:T(8,128)(2,1)S(1)} %get-tuple-element.119), channel_id=1, replica_groups=mesh['pipe'=4,'expert'=32,'dp'=2] {'expert'}, dimensions={0} | all-to-all | bytes 1572864 | tf_op jit(solution)/shard_map/all_to_all | solution.py:406
  333.4 24.0 %all_to_all.90.refs_0_ = bf16[32,96,128]{2,1,0:T(8,128)(2,1)S(1)} all-to-all(bf16[32,96,128]{2,1,0:T(8,128)(2,1)S(1)} %dispatch.11), channel_id=1, replica_groups=mesh['pipe'=4,'expert'=32,'dp'=2] {'expert'}, dimensions={0} | all-to-all | bytes 1572864 | tf_op jit(solution)/shard_map/all_to_all | solution.py:406
  358.1 23.9 %all_to_all.91.refs_0_ = bf16[32,96,128]{2,1,0:T(8,128)(2,1)S(1)} all-to-all(bf16[32,96,128]{2,1,0:T(8,128)(2,1)S(1)} %get-tuple-element.124), channel_id=1, replica_groups=mesh['pipe'=4,'expert'=32,'dp'=2] {'expert'}, dimensions={0} | all-to-all | bytes 1572864 | tf_op jit(solution)/shard_map/all_to_all | solution.py:406
  385.3 28.1 %collective-permute-done.5.refs_0_.refs_4_ = bf16[64,2048]{1,0:T(8,128)(2,1)S(1)} collective-permute-done((bf16[64,2048]{1,0:T(8,128)(2,1)S(1)}, bf16[64,2048]{1,0:T(8,128)(2,1)S(1)}, u32[]{:S(2)}, u32[]{:S(2)}) %collective-permute-start.5) | collective-permute-done | bytes 262176 | tf_op jit(solution)/shard_map/ppermute | solution.py:544
  415.1 19.3 %all_to_all.92.refs_0_ = bf16[32,96,128]{2,1,0:T(8,128)(2,1)S(1)} all-to-all(bf16[32,96,128]{2,1,0:T(8,128)(2,1)S(1)} %dispatch.12), channel_id=1, replica_groups=mesh['pipe'=4,'expert'=32,'dp'=2] {'expert'}, dimensions={0} | all-to-all | bytes 1572864 | tf_op jit(solution)/shard_map/all_to_all | solution.py:406
  434.4 6.9 %expert_backward.8 = (bf16[32,96,128]{2,1,0:T(8,128)(2,1)S(1)}, f32[32,2048]{1,0:T(8,128)S(1)}, f32[2,16,768]{2,1,0:T(8,128)S(1)}, f32[16,768]{1,0:T(8,128)S(1)}, f32[16,2048]{1,0:T(8,128)S(1)}) custom-call(s32[96]{0:T(128)S(1)} %dynamic-slice_bitcast_fusion.flags, ...), custom_call_target="tpu_custom_call", output_to_operand_aliasing={{1}: (3, {}), {2}: (4, {}), {3}: (5, {}), {4}: (6, {})} | custom-call | tf_op jit(solution)/shard_map/expert_backward/pallas_call | solution.py:478
  441.4 19.4 %all_to_all.93.refs_0_ = bf16[32,96,128]{2,1,0:T(8,128)(2,1)S(1)} all-to-all(bf16[32,96,128]{2,1,0:T(8,128)(2,1)S(1)} %get-tuple-element.130), channel_id=1, replica_groups=mesh['pipe'=4,'expert'=32,'dp'=2] {'expert'}, dimensions={0} | all-to-all | bytes 1572864 | tf_op jit(solution)/shard_map/all_to_all | solution.py:406
  465.8 4.4 collective-permute-done.6.refs_0_.refs_2_
  472.0 19.4 %all_to_all.94.refs_0_ = bf16[32,96,128]{2,1,0:T(8,128)(2,1)S(1)} all-to-all(bf16[32,96,128]{2,1,0:T(8,128)(2,1)S(1)} %dispatch.13), channel_id=1, replica_groups=mesh['pipe'=4,'expert'=32,'dp'=2] {'expert'}, dimensions={0} | all-to-all | bytes 1572864 | tf_op jit(solution)/shard_map/all_to_all | solution.py:406
  491.4 7.1 %expert_backward.9 = (bf16[32,96,128]{2,1,0:T(8,128)(2,1)S(1)}, f32[32,2048]{1,0:T(8,128)S(1)}, f32[2,16,768]{2,1,0:T(8,128)S(1)}, f32[16,768]{1,0:T(8,128)S(1)}...) custom-call(s32[96]{0:T(128)S(1)} %dynamic-slice_bitcast_fusion.flag, ...), custom_call_target="tpu_custom_call", output_to_operand_aliasing={{1}: (2, {}), {2}: (3, {}), {3}: (4, {}), {4}: (5, {})} | custom-call | tf_op jit(solution)/shard_map/expert_backward/pallas_call | solution.py:478
  498.5 19.5 %all_to_all.95.refs_0_ = bf16[32,96,128]{2,1,0:T(8,128)(2,1)S(1)} all-to-all(bf16[32,96,128]{2,1,0:T(8,128)(2,1)S(1)} %get-tuple-element.139), channel_id=1, replica_groups=mesh['pipe'=4,'expert'=32,'dp'=2] {'expert'}, dimensions={0} | all-to-all | bytes 1572864 | tf_op jit(solution)/shard_map/all_to_all | solution.py:406
  518.0 18.4 %collective-permute-start.7 = (bf16[32,2048]{1,0:T(8,128)(2,1)S(1)}, bf16[32,2048]{1,0:T(8,128)(2,1)S(1)}, u32[]{:S(2)}, u32[]{:S(2)}) collective-permute-start(bf16[32,2048]{1,0:T(8,128)(2,1)S(1)} %get-tuple-element.146.refs_0_), channel_id=1, source_target_pairs={{0,1},{1,0},{2,3},{3,2},{4,5},{5,4},{6,7},{7,6},{8,9},{9,8},{10,11... | collective-permute-start | bytes 393224 | tf_op jit(solution)/shard_map/ppermute | solution.py:561
  536.9 3.4 combine.15
  (77 shorter events, 50.5 us)
Async XLA Ops:
  1.3 1.0 copy-start.7
  2.4 0.7 copy-start.15
  3.1 1.0 copy-start.17
  4.1 0.7 copy-start.19
  4.8 0.7 copy-start.20
  40.4 1.9 copy-start
  42.2 1.9 copy-start.2
  44.1 1.9 copy-start.4
  46.0 0.9 copy-start.6
  46.9 0.8 copy-start.9
  47.8 0.8 copy-start.11
  48.6 0.7 copy-start.13
  49.3 30.5 %copy-start.16 = (f32[1,2048]{1,0:T(1,128)S(1)}, f32[1,2048]{1,0:T(1,128)}, u32[]{:S(2)}) copy-start(f32[1,2048]{1,0:T(1,128)} %refs_3_.7) | copy-start | bytes 24580
  49.3 39.0 %copy-start.8 = (bf16[2,64,2048]{2,1,0:T(8,128)(2,1)S(1)}, bf16[2,64,2048]{2,1,0:T(8,128)(2,1)}, u32[]{:S(2)}) copy-start(bf16[2,64,2048]{2,1,0:T(8,128)(2,1)} %refs_3_.6) | copy-start | bytes 1572868
  49.3 39.0 %copy-start.18 = (bf16[2,64,2048]{2,1,0:T(8,128)(2,1)S(1)}, bf16[2,64,2048]{2,1,0:T(8,128)(2,1)}, u32[]{:S(2)}) copy-start(bf16[2,64,2048]{2,1,0:T(8,128)(2,1)} %refs_0_.1) | copy-start | bytes 1572868
  49.3 68.0 %copy-start.5 = (bf16[1,1,768,2048]{3,2,1,0:T(8,128)(2,1)S(1)}, bf16[1,1,768,2048]{3,2,1,0:T(8,128)(2,1)}, u32[]{:S(2)}) copy-start(bf16[1,1,768,2048]{3,2,1,0:T(8,128)(2,1)} %param.20) | copy-start | bytes 9437188
  54.1 63.2 %copy-start.1 = (bf16[1,1,2048,768]{3,2,1,0:T(8,128)(2,1)S(1)}, bf16[1,1,2048,768]{3,2,1,0:T(8,128)(2,1)}, u32[]{:S(2)}) copy-start(bf16[1,1,2048,768]{3,2,1,0:T(8,128)(2,1)} %param.18) | copy-start | bytes 9437188
  54.2 63.2 %copy-start.3 = (bf16[1,1,2048,768]{3,2,1,0:T(8,128)(2,1)S(1)}, bf16[1,1,2048,768]{3,2,1,0:T(8,128)(2,1)}, u32[]{:S(2)}) copy-start(bf16[1,1,2048,768]{3,2,1,0:T(8,128)(2,1)} %param.19) | copy-start | bytes 9437188
  81.8 6.5 %collective-permute-start = (bf16[64,2048]{1,0:T(8,128)(2,1)S(1)}, bf16[64,2048]{1,0:T(8,128)(2,1)S(1)}, u32[]{:S(2)}, u32[]{:S(2)}) collective-permute-start(bf16[64,2048]{1,0:T(8,128)(2,1)S(1)} %combine.8.refs_0_), channel_id=1, source_target_pairs={{0,64},{1,65},{2,66},{3,67},{4,68},{5,69},{6,70},{7,71},{8,72},{9,... | collective-permute-start | bytes 786440 | tf_op jit(solution)/shard_map/ppermute | solution.py:544
  149.2 7.4 %collective-permute-start.1 = (bf16[64,2048]{1,0:T(8,128)(2,1)S(1)}, bf16[64,2048]{1,0:T(8,128)(2,1)S(1)}, u32[]{:S(2)}, u32[]{:S(2)}) collective-permute-start(bf16[64,2048]{1,0:T(8,128)(2,1)S(1)} %combine.9.refs_1_), channel_id=1, source_target_pairs={{64,128},{0,64},{65,129},{1,65},{66,130},{2,66},{67,131},{3,67},{6... | collective-permute-start | bytes 786440 | tf_op jit(solution)/shard_map/ppermute | solution.py:544
  213.9 0.7 collective-permute-start.2
  240.6 4.9 copy-start.10
  246.1 53.1 %copy-start.12 = (bf16[1,1,2,16,768]{4,3,2,1,0:T(8,128)(2,1)S(1)}, bf16[1,1,2,16,768]{4,3,2,1,0:T(8,128)(2,1)}, u32[]{:S(2)}) copy-start(bf16[1,1,2,16,768]{4,3,2,1,0:T(8,128)(2,1)} %param.22) | copy-start | bytes 147460
  246.1 53.0 %copy-start.14 = (bf16[1,1,768,16]{2,3,1,0:T(8,128)(2,1)S(1)}, bf16[1,1,768,16]{2,3,1,0:T(8,128)(2,1)}, u32[]{:S(2)}) copy-start(bf16[1,1,768,16]{2,3,1,0:T(8,128)(2,1)} %param.23) | copy-start | bytes 73732
  272.5 0.7 collective-permute-start.3
  330.9 0.7 collective-permute-start.4
  384.0 29.4 %collective-permute-start.5 = (bf16[64,2048]{1,0:T(8,128)(2,1)S(1)}, bf16[64,2048]{1,0:T(8,128)(2,1)S(1)}, u32[]{:S(2)}, u32[]{:S(2)}) collective-permute-start(bf16[64,2048]{1,0:T(8,128)(2,1)S(1)} %combine.13.refs_5_), channel_id=1, source_target_pairs={{64,0},{128,64},{65,1},{129,65},{66,2},{130,66},{67,3},{131,67},{6... | collective-permute-start | bytes 786440 | tf_op jit(solution)/shard_map/ppermute | solution.py:544
  462.8 7.4 %collective-permute-start.6 = (bf16[64,2048]{1,0:T(8,128)(2,1)S(1)}, bf16[64,2048]{1,0:T(8,128)(2,1)S(1)}, u32[]{:S(2)}, u32[]{:S(2)}) collective-permute-start(bf16[64,2048]{1,0:T(8,128)(2,1)S(1)} %combine.14.refs_6_), channel_id=1, source_target_pairs={{64,0},{65,1},{66,2},{67,3},{68,4},{69,5},{70,6},{71,7},{72,8},{73... | collective-permute-start | bytes 786440 | tf_op jit(solution)/shard_map/ppermute | solution.py:544
  518.0 22.4 %collective-permute-start.7 = (bf16[32,2048]{1,0:T(8,128)(2,1)S(1)}, bf16[32,2048]{1,0:T(8,128)(2,1)S(1)}, u32[]{:S(2)}, u32[]{:S(2)}) collective-permute-start(bf16[32,2048]{1,0:T(8,128)(2,1)S(1)} %get-tuple-element.146.refs_0_), channel_id=1, source_target_pairs={{0,1},{1,0},{2,3},{3,2},{4,5},{5,4},{6,7},{7,6},{8,9},{9,8},{10,11... | collective-permute-start | bytes 393224 | tf_op jit(solution)/shard_map/ppermute | solution.py:561
  536.4 3.9 collective-permute-start.10
  536.4 3.9 collective-permute-start.8
  536.9 3.4 collective-permute-start.9

commit v4 on v3

--- a/solution.py
+++ b/solution.py
@@ -148,7 +148,11 @@
     )
 
 
-def opening_kernel(dims, flags, routes, gates, tokens, cotangent, gain, *refs):
+def first_kernel(*refs):
+    refs[-1][...] = jnp.zeros_like(refs[-1])
+
+
+def opening_kernel(dims, flags, routes, gates, tokens, cotangent, gain, mark, *refs):
     peers, chunks = dims
     tables, out_ref, first, wide, rows = refs[:6], *refs[6:]
     make_tables(peers, routes, gates, *tables)
@@ -390,17 +394,25 @@
     scalars = pl.BlockSpec(memory_space=pltpu.SMEM)
     table_in = jax.ShapeDtypeStruct((micros, slots, tok_rows), BF16)
     table_out = jax.ShapeDtypeStruct((micros, tok_rows, slots), BF16)
+    weights = (w_gate, w_up, w_down, in_a, in_b, down_a, down_b)
+    mark = pl.pallas_call(
+        first_kernel,
+        out_shape=jax.ShapeDtypeStruct((8, LANES), F32),
+        in_specs=[pl.BlockSpec(memory_space=pl.ANY)] * (len(weights) + 3),
+        out_specs=held,
+        compiler_params=params(60),
+        name="first",
+    )(*weights, tokens, cotangent, norm_gain)
     *tables, placed_first, input_first = pl.pallas_call(
         functools.partial(opening_kernel, (peers, chunks)),
         out_shape=[table_in] * 3 + [table_out] * 3 + [buffer, block_rows],
-        in_specs=[scalars] + [held] * 5,
+        in_specs=[scalars] + [held] * 6,
         out_specs=[held] * 8,
         scratch_shapes=[wide, pltpu.VMEM((tok_rows, model), BF16)],
-        compiler_params=params(20),
+        compiler_params=params(10),
         name="opening",
-    )(flags, routes.transpose(0, 2, 1), gates.transpose(0, 2, 1), tokens, cotangent, norm_gain)
+    )(flags, routes.transpose(0, 2, 1), gates.transpose(0, 2, 1), tokens, cotangent, norm_gain, mark)
     place, scale_hi, scale_lo, pick, mix_hi, mix_lo = tables
-    weights = (w_gate, w_up, w_down, in_a, in_b, down_a, down_b)
 
     def exchange(rows):
         return lax.all_to_all(rows, "expert", split_axis=0, concat_axis=0, tiled=True)

time: 551 us -> 544 us (0.987)
  local copies, waits for them, and re-layouts: 13.8 us -> 6.8 us
    unnamed x42 -> x30, local copies, waits for them, and re-layouts: 13.1 us -> 6.11 us
where the time goes in v4:
time: 544 us; the launch traced here: 535 us
  blocking collectives  381 us (70%)
  Pallas kernels  75.8 us (14%)
  waiting for transfers between devices  39.2 us (7%)
  starting transfers between devices  30.9 us (6%)
  local copies, waits for them, and re-layouts  6.8 us (1%)
    all_to_all x16, blocking collectives, exchange(): lax.all_to_all(rows, 'expert', split_axis=0, concat_axis=0, tiled=True)  381 us
    ppermute x7, waiting for transfers between devices, body(): incoming = lax.ppermute(mixed[tick], 'pipe', hops[tick])  39.2 us
    pallas_call x5, Pallas kernels, expert_forward(): pl.pallas_call(functools.partial(forward_kernel, (peers, chunks, low_rank...  24.1 us
    ppermute x4, starting transfers between devices, body(): across = [lax.ppermute(total, 'dp', [(0, 1), (1, 0)]) for total in rounded]  18.9 us
    pallas_call x8, Pallas kernels, combine(): pl.pallas_call(functools.partial(combine_kernel, (peers, chunks, tick * 1...  17.6 us
    pallas_call x5, Pallas kernels, expert_backward(): pl.pallas_call(functools.partial(backward_kernel, (peers, chunks, low_ran...  16.1 us
    pallas_call x7, Pallas kernels, dispatch(): pl.pallas_call(functools.partial(dispatch_kernel, (peers, chunks, tick *...  12.8 us
    ppermute x7, starting transfers between devices, body(): incoming = lax.ppermute(mixed[tick], 'pipe', hops[tick])  12 us
  transfers between devices with their start and end apart: 11, of which 4 were waited for; matrix products, arithmetic and copies ran while one was open for 0% of the time, Pallas kernels for 1%

profile of v4, /device:TPU:1, one launch (start us, length us, event | category | flops | bytes accessed | tf_op | source)
XLA Modules:
  0.0 534.9 jit_solution(4142476331101518165)
XLA Ops:
  4.3 2.1 opening.1
  6.4 32.7 %all_to_all.80.received.refs_0_ = bf16[32,96,128]{2,1,0:T(8,128)(2,1)S(1)} all-to-all(bf16[32,96,128]{2,1,0:T(8,128)(2,1)S(1)} %get-tuple-element.80), channel_id=1, replica_groups=mesh['pipe'=4,'expert'=32,'dp'=2] {'expert'}, dimensions={0} | all-to-all | bytes 1572864 | tf_op jit(solution)/shard_map/all_to_all | solution.py:418
  43.0 4.8 expert_forward.5
  47.8 25.6 %all_to_all.81.refs_0_ = bf16[32,96,128]{2,1,0:T(8,128)(2,1)S(1)} all-to-all(bf16[32,96,128]{2,1,0:T(8,128)(2,1)S(1)} %get-tuple-element.81), channel_id=1, replica_groups=mesh['pipe'=4,'expert'=32,'dp'=2] {'expert'}, dimensions={0} | all-to-all | bytes 1572864 | tf_op jit(solution)/shard_map/all_to_all | solution.py:418
  75.5 3.2 collective-permute-start
  78.7 3.3 collective-permute-done.refs_1_
  83.9 27.1 %all_to_all.82.received.refs_0_ = bf16[32,96,128]{2,1,0:T(8,128)(2,1)S(1)} all-to-all(bf16[32,96,128]{2,1,0:T(8,128)(2,1)S(1)} %get-tuple-element.89), channel_id=1, replica_groups=mesh['pipe'=4,'expert'=32,'dp'=2] {'expert'}, dimensions={0} | all-to-all | bytes 1572864 | tf_op jit(solution)/shard_map/all_to_all | solution.py:418
  110.9 4.8 expert_forward.6
  115.8 24.6 %all_to_all.83.refs_0_ = bf16[32,96,128]{2,1,0:T(8,128)(2,1)S(1)} all-to-all(bf16[32,96,128]{2,1,0:T(8,128)(2,1)S(1)} %get-tuple-element.94), channel_id=1, replica_groups=mesh['pipe'=4,'expert'=32,'dp'=2] {'expert'}, dimensions={0} | all-to-all | bytes 1572864 | tf_op jit(solution)/shard_map/all_to_all | solution.py:418
  142.4 4.1 collective-permute-start.1
  146.6 3.3 collective-permute-done.1.refs_0_.refs_1_.refs_2_
  151.6 24.2 %all_to_all.84.received = bf16[32,96,128]{2,1,0:T(8,128)(2,1)S(1)} all-to-all(bf16[32,96,128]{2,1,0:T(8,128)(2,1)S(1)} %dispatch.8), channel_id=1, replica_groups=mesh['pipe'=4,'expert'=32,'dp'=2] {'expert'}, dimensions={0} | all-to-all | bytes 1572864 | tf_op jit(solution)/shard_map/all_to_all | solution.py:418
  175.8 4.8 expert_forward.7
  180.7 24.7 %all_to_all.85.refs_0_ = bf16[32,96,128]{2,1,0:T(8,128)(2,1)S(1)} all-to-all(bf16[32,96,128]{2,1,0:T(8,128)(2,1)S(1)} %get-tuple-element.100), channel_id=1, replica_groups=mesh['pipe'=4,'expert'=32,'dp'=2] {'expert'}, dimensions={0} | all-to-all | bytes 1572864 | tf_op jit(solution)/shard_map/all_to_all | solution.py:418
  209.9 24.2 %all_to_all.86.received = bf16[32,96,128]{2,1,0:T(8,128)(2,1)S(1)} all-to-all(bf16[32,96,128]{2,1,0:T(8,128)(2,1)S(1)} %dispatch.9), channel_id=1, replica_groups=mesh['pipe'=4,'expert'=32,'dp'=2] {'expert'}, dimensions={0} | all-to-all | bytes 1572864 | tf_op jit(solution)/shard_map/all_to_all | solution.py:418
  234.1 4.8 expert_forward.8
  239.5 24.2 %all_to_all.87.refs_0_ = bf16[32,96,128]{2,1,0:T(8,128)(2,1)S(1)} all-to-all(bf16[32,96,128]{2,1,0:T(8,128)(2,1)S(1)} %get-tuple-element.110), channel_id=1, replica_groups=mesh['pipe'=4,'expert'=32,'dp'=2] {'expert'}, dimensions={0} | all-to-all | bytes 1572864 | tf_op jit(solution)/shard_map/all_to_all | solution.py:418
  268.3 24.1 %all_to_all.88.received.refs_1_ = bf16[32,96,128]{2,1,0:T(8,128)(2,1)S(1)} all-to-all(bf16[32,96,128]{2,1,0:T(8,128)(2,1)S(1)} %dispatch.10), channel_id=1, replica_groups=mesh['pipe'=4,'expert'=32,'dp'=2] {'expert'}, dimensions={0} | all-to-all | bytes 1572864 | tf_op jit(solution)/shard_map/all_to_all | solution.py:418
  292.4 4.8 expert_forward.9
  298.0 24.1 %all_to_all.89.refs_0_ = bf16[32,96,128]{2,1,0:T(8,128)(2,1)S(1)} all-to-all(bf16[32,96,128]{2,1,0:T(8,128)(2,1)S(1)} %get-tuple-element.119), channel_id=1, replica_groups=mesh['pipe'=4,'expert'=32,'dp'=2] {'expert'}, dimensions={0} | all-to-all | bytes 1572864 | tf_op jit(solution)/shard_map/all_to_all | solution.py:418
  326.7 24.0 %all_to_all.90.refs_0_ = bf16[32,96,128]{2,1,0:T(8,128)(2,1)S(1)} all-to-all(bf16[32,96,128]{2,1,0:T(8,128)(2,1)S(1)} %dispatch.11), channel_id=1, replica_groups=mesh['pipe'=4,'expert'=32,'dp'=2] {'expert'}, dimensions={0} | all-to-all | bytes 1572864 | tf_op jit(solution)/shard_map/all_to_all | solution.py:418
  351.3 23.9 %all_to_all.91.refs_0_ = bf16[32,96,128]{2,1,0:T(8,128)(2,1)S(1)} all-to-all(bf16[32,96,128]{2,1,0:T(8,128)(2,1)S(1)} %get-tuple-element.124), channel_id=1, replica_groups=mesh['pipe'=4,'expert'=32,'dp'=2] {'expert'}, dimensions={0} | all-to-all | bytes 1572864 | tf_op jit(solution)/shard_map/all_to_all | solution.py:418
  378.5 28.3 %collective-permute-done.5.refs_0_.refs_4_ = bf16[64,2048]{1,0:T(8,128)(2,1)S(1)} collective-permute-done((bf16[64,2048]{1,0:T(8,128)(2,1)S(1)}, bf16[64,2048]{1,0:T(8,128)(2,1)S(1)}, u32[]{:S(2)}, u32[]{:S(2)}) %collective-permute-start.5) | collective-permute-done | bytes 262176 | tf_op jit(solution)/shard_map/ppermute | solution.py:556
  408.6 19.3 %all_to_all.92.refs_0_ = bf16[32,96,128]{2,1,0:T(8,128)(2,1)S(1)} all-to-all(bf16[32,96,128]{2,1,0:T(8,128)(2,1)S(1)} %dispatch.12), channel_id=1, replica_groups=mesh['pipe'=4,'expert'=32,'dp'=2] {'expert'}, dimensions={0} | all-to-all | bytes 1572864 | tf_op jit(solution)/shard_map/all_to_all | solution.py:418
  427.9 7.0 %expert_backward.8 = (bf16[32,96,128]{2,1,0:T(8,128)(2,1)S(1)}, f32[32,2048]{1,0:T(8,128)S(1)}, f32[2,16,768]{2,1,0:T(8,128)S(1)}, f32[16,768]{1,0:T(8,128)S(1)}, f32[16,2048]{1,0:T(8,128)S(1)}) custom-call(s32[96]{0:T(128)S(1)} %dynamic-slice_bitcast_fusion.flags, ...), custom_call_target="tpu_custom_call", output_to_operand_aliasing={{1}: (3, {}), {2}: (4, {}), {3}: (5, {}), {4}: (6, {})} | custom-call | tf_op jit(solution)/shard_map/expert_backward/pallas_call | solution.py:490
  434.8 19.4 %all_to_all.93.refs_0_ = bf16[32,96,128]{2,1,0:T(8,128)(2,1)S(1)} all-to-all(bf16[32,96,128]{2,1,0:T(8,128)(2,1)S(1)} %get-tuple-element.130), channel_id=1, replica_groups=mesh['pipe'=4,'expert'=32,'dp'=2] {'expert'}, dimensions={0} | all-to-all | bytes 1572864 | tf_op jit(solution)/shard_map/all_to_all | solution.py:418
  459.3 4.4 collective-permute-done.6.refs_0_.refs_2_
  465.5 19.4 %all_to_all.94.refs_0_ = bf16[32,96,128]{2,1,0:T(8,128)(2,1)S(1)} all-to-all(bf16[32,96,128]{2,1,0:T(8,128)(2,1)S(1)} %dispatch.13), channel_id=1, replica_groups=mesh['pipe'=4,'expert'=32,'dp'=2] {'expert'}, dimensions={0} | all-to-all | bytes 1572864 | tf_op jit(solution)/shard_map/all_to_all | solution.py:418
  484.9 7.2 %expert_backward.9 = (bf16[32,96,128]{2,1,0:T(8,128)(2,1)S(1)}, f32[32,2048]{1,0:T(8,128)S(1)}, f32[2,16,768]{2,1,0:T(8,128)S(1)}, f32[16,768]{1,0:T(8,128)S(1)}...) custom-call(s32[96]{0:T(128)S(1)} %dynamic-slice_bitcast_fusion.flag, ...), custom_call_target="tpu_custom_call", output_to_operand_aliasing={{1}: (2, {}), {2}: (3, {}), {3}: (4, {}), {4}: (5, {})} | custom-call | tf_op jit(solution)/shard_map/expert_backward/pallas_call | solution.py:490
  492.1 19.5 %all_to_all.95.refs_0_ = bf16[32,96,128]{2,1,0:T(8,128)(2,1)S(1)} all-to-all(bf16[32,96,128]{2,1,0:T(8,128)(2,1)S(1)} %get-tuple-element.139), channel_id=1, replica_groups=mesh['pipe'=4,'expert'=32,'dp'=2] {'expert'}, dimensions={0} | all-to-all | bytes 1572864 | tf_op jit(solution)/shard_map/all_to_all | solution.py:418
  511.5 18.4 %collective-permute-start.7 = (bf16[32,2048]{1,0:T(8,128)(2,1)S(1)}, bf16[32,2048]{1,0:T(8,128)(2,1)S(1)}, u32[]{:S(2)}, u32[]{:S(2)}) collective-permute-start(bf16[32,2048]{1,0:T(8,128)(2,1)S(1)} %get-tuple-element.146.refs_0_), channel_id=1, source_target_pairs={{0,1},{1,0},{2,3},{3,2},{4,5},{5,4},{6,7},{7,6},{8,9},{9,8},{10,11... | collective-permute-start | bytes 393224 | tf_op jit(solution)/shard_map/ppermute | solution.py:573
  530.4 3.4 combine.15
  (66 shorter events, 44.0 us)
Async XLA Ops:
  1.3 1.0 copy-start.5
  1.3 1.0 copy-start.11
  1.3 1.0 copy-start.13
  1.3 1.0 copy-start.14
  1.3 37.8 %copy-start = (bf16[1,1,2048,768]{3,2,1,0:T(8,128)(2,1)S(1)}, bf16[1,1,2048,768]{3,2,1,0:T(8,128)(2,1)}, u32[]{:S(2)}) copy-start(bf16[1,1,2048,768]{3,2,1,0:T(8,128)(2,1)} %param.18) | copy-start | bytes 9437188
  1.4 37.8 %copy-start.4 = (bf16[1,1,2048,32]{2,3,1,0:T(8,128)(2,1)S(1)}, bf16[1,1,2048,32]{2,3,1,0:T(8,128)(2,1)}, u32[]{:S(2)}) copy-start(bf16[1,1,2048,32]{2,3,1,0:T(8,128)(2,1)} %param.21) | copy-start | bytes 393220
  1.4 37.8 %copy-start.6 = (bf16[1,1,16,2048]{3,2,1,0:T(8,128)(2,1)S(1)}, bf16[1,1,16,2048]{3,2,1,0:T(8,128)(2,1)}, u32[]{:S(2)}) copy-start(bf16[1,1,16,2048]{3,2,1,0:T(8,128)(2,1)} %param.24) | copy-start | bytes 196612
  1.4 37.8 %copy-start.7 = (bf16[1,1,2,16,768]{4,3,2,1,0:T(8,128)(2,1)S(1)}, bf16[1,1,2,16,768]{4,3,2,1,0:T(8,128)(2,1)}, u32[]{:S(2)}) copy-start(bf16[1,1,2,16,768]{4,3,2,1,0:T(8,128)(2,1)} %param.22) | copy-start | bytes 147460
  1.4 37.8 %copy-start.10 = (bf16[1,1,768,16]{2,3,1,0:T(8,128)(2,1)S(1)}, bf16[1,1,768,16]{2,3,1,0:T(8,128)(2,1)}, u32[]{:S(2)}) copy-start(bf16[1,1,768,16]{2,3,1,0:T(8,128)(2,1)} %param.23) | copy-start | bytes 73732
  2.4 1.2 copy-start.8
  3.6 0.7 copy-start.12
  39.2 1.9 copy-start.1
  41.1 1.9 copy-start.3
  47.8 34.2 %copy-start.9 = (bf16[2,64,2048]{2,1,0:T(8,128)(2,1)S(1)}, bf16[2,64,2048]{2,1,0:T(8,128)(2,1)}, u32[]{:S(2)}) copy-start(bf16[2,64,2048]{2,1,0:T(8,128)(2,1)} %refs_0_.1) | copy-start | bytes 1572868
  47.8 63.1 %copy-start.2 = (bf16[1,1,2048,768]{3,2,1,0:T(8,128)(2,1)S(1)}, bf16[1,1,2048,768]{3,2,1,0:T(8,128)(2,1)}, u32[]{:S(2)}) copy-start(bf16[1,1,2048,768]{3,2,1,0:T(8,128)(2,1)} %param.19) | copy-start | bytes 9437188
  75.5 6.5 %collective-permute-start = (bf16[64,2048]{1,0:T(8,128)(2,1)S(1)}, bf16[64,2048]{1,0:T(8,128)(2,1)S(1)}, u32[]{:S(2)}, u32[]{:S(2)}) collective-permute-start(bf16[64,2048]{1,0:T(8,128)(2,1)S(1)} %combine.8.refs_0_), channel_id=1, source_target_pairs={{0,64},{1,65},{2,66},{3,67},{4,68},{5,69},{6,70},{7,71},{8,72},{9,... | collective-permute-start | bytes 786440 | tf_op jit(solution)/shard_map/ppermute | solution.py:556
  142.4 7.4 %collective-permute-start.1 = (bf16[64,2048]{1,0:T(8,128)(2,1)S(1)}, bf16[64,2048]{1,0:T(8,128)(2,1)S(1)}, u32[]{:S(2)}, u32[]{:S(2)}) collective-permute-start(bf16[64,2048]{1,0:T(8,128)(2,1)S(1)} %combine.9.refs_1_), channel_id=1, source_target_pairs={{64,128},{0,64},{65,129},{1,65},{66,130},{2,66},{67,131},{3,67},{6... | collective-permute-start | bytes 786440 | tf_op jit(solution)/shard_map/ppermute | solution.py:556
  207.4 0.7 collective-permute-start.2
  265.7 0.7 collective-permute-start.3
  324.2 0.7 collective-permute-start.4
  377.2 29.6 %collective-permute-start.5 = (bf16[64,2048]{1,0:T(8,128)(2,1)S(1)}, bf16[64,2048]{1,0:T(8,128)(2,1)S(1)}, u32[]{:S(2)}, u32[]{:S(2)}) collective-permute-start(bf16[64,2048]{1,0:T(8,128)(2,1)S(1)} %combine.13.refs_5_), channel_id=1, source_target_pairs={{64,0},{128,64},{65,1},{129,65},{66,2},{130,66},{67,3},{131,67},{6... | collective-permute-start | bytes 786440 | tf_op jit(solution)/shard_map/ppermute | solution.py:556
  456.3 7.4 %collective-permute-start.6 = (bf16[64,2048]{1,0:T(8,128)(2,1)S(1)}, bf16[64,2048]{1,0:T(8,128)(2,1)S(1)}, u32[]{:S(2)}, u32[]{:S(2)}) collective-permute-start(bf16[64,2048]{1,0:T(8,128)(2,1)S(1)} %combine.14.refs_6_), channel_id=1, source_target_pairs={{64,0},{65,1},{66,2},{67,3},{68,4},{69,5},{70,6},{71,7},{72,8},{73... | collective-permute-start | bytes 786440 | tf_op jit(solution)/shard_map/ppermute | solution.py:556
  511.5 22.3 %collective-permute-start.7 = (bf16[32,2048]{1,0:T(8,128)(2,1)S(1)}, bf16[32,2048]{1,0:T(8,128)(2,1)S(1)}, u32[]{:S(2)}, u32[]{:S(2)}) collective-permute-start(bf16[32,2048]{1,0:T(8,128)(2,1)S(1)} %get-tuple-element.146.refs_0_), channel_id=1, source_target_pairs={{0,1},{1,0},{2,3},{3,2},{4,5},{5,4},{6,7},{7,6},{8,9},{9,8},{10,11... | collective-permute-start | bytes 393224 | tf_op jit(solution)/shard_map/ppermute | solution.py:573
  529.9 3.9 collective-permute-start.10
  529.9 3.9 collective-permute-start.8
  530.4 3.4 collective-permute-start.9

commit v5 on v4

--- a/solution.py
+++ b/solution.py
@@ -410,6 +410,7 @@
         out_specs=[held] * 8,
         scratch_shapes=[wide, pltpu.VMEM((tok_rows, model), BF16)],
         compiler_params=params(10),
+        cost_estimate=pl.CostEstimate(flops=2 * 10**10, bytes_accessed=10**7, transcendentals=0),
         name="opening",
     )(flags, routes.transpose(0, 2, 1), gates.transpose(0, 2, 1), tokens, cotangent, norm_gain, mark)
     place, scale_hi, scale_lo, pick, mix_hi, mix_lo = tables
@@ -464,7 +465,9 @@
     def expert_forward(tick, received, state):
         has_store = state is not None
         result = pl.pallas_call(
-            functools.partial(forward_kernel, (peers, chunks, low_rank, block, tick), has_store),
+            functools.partial(
+                forward_kernel, (peers, chunks, low_rank, hidden_width, tick), has_store
+            ),
             out_shape=[buffer] + state_shapes,
             in_specs=[held] * (12 if has_store else 8),
             out_specs=[held] * 5,

time: 544 us -> 538 us (0.989)
  no operation moved by 1% of the time
where the time goes in v5:
time: 538 us; the launch traced here: 529 us
  blocking collectives  381 us (71%)
  Pallas kernels  75.1 us (14%)
  waiting for transfers between devices  39.1 us (7%)
  starting transfers between devices  30.8 us (6%)
    all_to_all x16, blocking collectives, exchange(): lax.all_to_all(rows, 'expert', split_axis=0, concat_axis=0, tiled=True)  381 us
    ppermute x7, waiting for transfers between devices, body(): incoming = lax.ppermute(mixed[tick], 'pipe', hops[tick])  39.1 us
    pallas_call x5, Pallas kernels, expert_forward(): pl.pallas_call(functools.partial(forward_kernel, (peers, chunks, low_rank...  23.4 us
    ppermute x4, starting transfers between devices, body(): across = [lax.ppermute(total, 'dp', [(0, 1), (1, 0)]) for total in rounded]  18.9 us
    pallas_call x8, Pallas kernels, combine(): pl.pallas_call(functools.partial(combine_kernel, (peers, chunks, tick * 1...  17.6 us
    pallas_call x5, Pallas kernels, expert_backward(): pl.pallas_call(functools.partial(backward_kernel, (peers, chunks, low_ran...  16.1 us
    pallas_call x7, Pallas kernels, dispatch(): pl.pallas_call(functools.partial(dispatch_kernel, (peers, chunks, tick *...  12.8 us
    ppermute x7, starting transfers between devices, body(): incoming = lax.ppermute(mixed[tick], 'pipe', hops[tick])  12 us
  transfers between devices with their start and end apart: 11, of which 4 were waited for; matrix products, arithmetic and copies ran while one was open for 0% of the time, Pallas kernels for 1%

profile of v5, /device:TPU:1, one launch (start us, length us, event | category | flops | bytes accessed | tf_op | source)
XLA Modules:
  0.0 529.2 jit_solution(13266411488132103958)
XLA Ops:
  3.3 2.1 opening.1
  5.4 32.9 %all_to_all.80.received.refs_0_ = bf16[32,96,128]{2,1,0:T(8,128)(2,1)S(1)} all-to-all(bf16[32,96,128]{2,1,0:T(8,128)(2,1)S(1)} %get-tuple-element.80), channel_id=1, replica_groups=mesh['pipe'=4,'expert'=32,'dp'=2] {'expert'}, dimensions={0} | all-to-all | bytes 1572864 | tf_op jit(solution)/shard_map/all_to_all | solution.py:419
  38.4 4.7 expert_forward.5
  43.0 25.3 %all_to_all.81.refs_0_ = bf16[32,96,128]{2,1,0:T(8,128)(2,1)S(1)} all-to-all(bf16[32,96,128]{2,1,0:T(8,128)(2,1)S(1)} %get-tuple-element.81), channel_id=1, replica_groups=mesh['pipe'=4,'expert'=32,'dp'=2] {'expert'}, dimensions={0} | all-to-all | bytes 1572864 | tf_op jit(solution)/shard_map/all_to_all | solution.py:419
  70.4 3.2 collective-permute-start
  73.6 3.3 collective-permute-done.refs_1_
  78.8 27.1 %all_to_all.82.received.refs_0_ = bf16[32,96,128]{2,1,0:T(8,128)(2,1)S(1)} all-to-all(bf16[32,96,128]{2,1,0:T(8,128)(2,1)S(1)} %get-tuple-element.89), channel_id=1, replica_groups=mesh['pipe'=4,'expert'=32,'dp'=2] {'expert'}, dimensions={0} | all-to-all | bytes 1572864 | tf_op jit(solution)/shard_map/all_to_all | solution.py:419
  105.9 4.7 expert_forward.6
  110.6 24.6 %all_to_all.83.refs_0_ = bf16[32,96,128]{2,1,0:T(8,128)(2,1)S(1)} all-to-all(bf16[32,96,128]{2,1,0:T(8,128)(2,1)S(1)} %get-tuple-element.94), channel_id=1, replica_groups=mesh['pipe'=4,'expert'=32,'dp'=2] {'expert'}, dimensions={0} | all-to-all | bytes 1572864 | tf_op jit(solution)/shard_map/all_to_all | solution.py:419
  137.2 4.1 collective-permute-start.1
  141.4 3.3 collective-permute-done.1.refs_0_.refs_1_.refs_2_
  146.4 24.2 %all_to_all.84.received = bf16[32,96,128]{2,1,0:T(8,128)(2,1)S(1)} all-to-all(bf16[32,96,128]{2,1,0:T(8,128)(2,1)S(1)} %dispatch.8), channel_id=1, replica_groups=mesh['pipe'=4,'expert'=32,'dp'=2] {'expert'}, dimensions={0} | all-to-all | bytes 1572864 | tf_op jit(solution)/shard_map/all_to_all | solution.py:419
  170.6 4.7 expert_forward.7
  175.3 24.7 %all_to_all.85.refs_0_ = bf16[32,96,128]{2,1,0:T(8,128)(2,1)S(1)} all-to-all(bf16[32,96,128]{2,1,0:T(8,128)(2,1)S(1)} %get-tuple-element.100), channel_id=1, replica_groups=mesh['pipe'=4,'expert'=32,'dp'=2] {'expert'}, dimensions={0} | all-to-all | bytes 1572864 | tf_op jit(solution)/shard_map/all_to_all | solution.py:419
  204.6 24.2 %all_to_all.86.received = bf16[32,96,128]{2,1,0:T(8,128)(2,1)S(1)} all-to-all(bf16[32,96,128]{2,1,0:T(8,128)(2,1)S(1)} %dispatch.9), channel_id=1, replica_groups=mesh['pipe'=4,'expert'=32,'dp'=2] {'expert'}, dimensions={0} | all-to-all | bytes 1572864 | tf_op jit(solution)/shard_map/all_to_all | solution.py:419
  228.8 4.7 expert_forward.8
  234.1 24.2 %all_to_all.87.refs_0_ = bf16[32,96,128]{2,1,0:T(8,128)(2,1)S(1)} all-to-all(bf16[32,96,128]{2,1,0:T(8,128)(2,1)S(1)} %get-tuple-element.110), channel_id=1, replica_groups=mesh['pipe'=4,'expert'=32,'dp'=2] {'expert'}, dimensions={0} | all-to-all | bytes 1572864 | tf_op jit(solution)/shard_map/all_to_all | solution.py:419
  262.9 24.1 %all_to_all.88.received.refs_1_ = bf16[32,96,128]{2,1,0:T(8,128)(2,1)S(1)} all-to-all(bf16[32,96,128]{2,1,0:T(8,128)(2,1)S(1)} %dispatch.10), channel_id=1, replica_groups=mesh['pipe'=4,'expert'=32,'dp'=2] {'expert'}, dimensions={0} | all-to-all | bytes 1572864 | tf_op jit(solution)/shard_map/all_to_all | solution.py:419
  287.0 4.7 expert_forward.9
  292.5 24.1 %all_to_all.89.refs_0_ = bf16[32,96,128]{2,1,0:T(8,128)(2,1)S(1)} all-to-all(bf16[32,96,128]{2,1,0:T(8,128)(2,1)S(1)} %get-tuple-element.119), channel_id=1, replica_groups=mesh['pipe'=4,'expert'=32,'dp'=2] {'expert'}, dimensions={0} | all-to-all | bytes 1572864 | tf_op jit(solution)/shard_map/all_to_all | solution.py:419
  321.2 24.0 %all_to_all.90.refs_0_ = bf16[32,96,128]{2,1,0:T(8,128)(2,1)S(1)} all-to-all(bf16[32,96,128]{2,1,0:T(8,128)(2,1)S(1)} %dispatch.11), channel_id=1, replica_groups=mesh['pipe'=4,'expert'=32,'dp'=2] {'expert'}, dimensions={0} | all-to-all | bytes 1572864 | tf_op jit(solution)/shard_map/all_to_all | solution.py:419
  345.8 23.9 %all_to_all.91.refs_0_ = bf16[32,96,128]{2,1,0:T(8,128)(2,1)S(1)} all-to-all(bf16[32,96,128]{2,1,0:T(8,128)(2,1)S(1)} %get-tuple-element.124), channel_id=1, replica_groups=mesh['pipe'=4,'expert'=32,'dp'=2] {'expert'}, dimensions={0} | all-to-all | bytes 1572864 | tf_op jit(solution)/shard_map/all_to_all | solution.py:419
  373.0 28.1 %collective-permute-done.5.refs_0_.refs_4_ = bf16[64,2048]{1,0:T(8,128)(2,1)S(1)} collective-permute-done((bf16[64,2048]{1,0:T(8,128)(2,1)S(1)}, bf16[64,2048]{1,0:T(8,128)(2,1)S(1)}, u32[]{:S(2)}, u32[]{:S(2)}) %collective-permute-start.5) | collective-permute-done | bytes 262176 | tf_op jit(solution)/shard_map/ppermute | solution.py:559
  402.9 19.3 %all_to_all.92.refs_0_ = bf16[32,96,128]{2,1,0:T(8,128)(2,1)S(1)} all-to-all(bf16[32,96,128]{2,1,0:T(8,128)(2,1)S(1)} %dispatch.12), channel_id=1, replica_groups=mesh['pipe'=4,'expert'=32,'dp'=2] {'expert'}, dimensions={0} | all-to-all | bytes 1572864 | tf_op jit(solution)/shard_map/all_to_all | solution.py:419
  422.2 7.0 %expert_backward.8 = (bf16[32,96,128]{2,1,0:T(8,128)(2,1)S(1)}, f32[32,2048]{1,0:T(8,128)S(1)}, f32[2,16,768]{2,1,0:T(8,128)S(1)}, f32[16,768]{1,0:T(8,128)S(1)}, f32[16,2048]{1,0:T(8,128)S(1)}) custom-call(s32[96]{0:T(128)S(1)} %dynamic-slice_bitcast_fusion.flags, ...), custom_call_target="tpu_custom_call", output_to_operand_aliasing={{1}: (3, {}), {2}: (4, {}), {3}: (5, {}), {4}: (6, {})} | custom-call | tf_op jit(solution)/shard_map/expert_backward/pallas_call | solution.py:493
  429.2 19.4 %all_to_all.93.refs_0_ = bf16[32,96,128]{2,1,0:T(8,128)(2,1)S(1)} all-to-all(bf16[32,96,128]{2,1,0:T(8,128)(2,1)S(1)} %get-tuple-element.130), channel_id=1, replica_groups=mesh['pipe'=4,'expert'=32,'dp'=2] {'expert'}, dimensions={0} | all-to-all | bytes 1572864 | tf_op jit(solution)/shard_map/all_to_all | solution.py:419
  453.6 4.4 collective-permute-done.6.refs_0_.refs_2_
  459.9 19.4 %all_to_all.94.refs_0_ = bf16[32,96,128]{2,1,0:T(8,128)(2,1)S(1)} all-to-all(bf16[32,96,128]{2,1,0:T(8,128)(2,1)S(1)} %dispatch.13), channel_id=1, replica_groups=mesh['pipe'=4,'expert'=32,'dp'=2] {'expert'}, dimensions={0} | all-to-all | bytes 1572864 | tf_op jit(solution)/shard_map/all_to_all | solution.py:419
  479.2 7.2 %expert_backward.9 = (bf16[32,96,128]{2,1,0:T(8,128)(2,1)S(1)}, f32[32,2048]{1,0:T(8,128)S(1)}, f32[2,16,768]{2,1,0:T(8,128)S(1)}, f32[16,768]{1,0:T(8,128)S(1)}...) custom-call(s32[96]{0:T(128)S(1)} %dynamic-slice_bitcast_fusion.flag, ...), custom_call_target="tpu_custom_call", output_to_operand_aliasing={{1}: (2, {}), {2}: (3, {}), {3}: (4, {}), {4}: (5, {})} | custom-call | tf_op jit(solution)/shard_map/expert_backward/pallas_call | solution.py:493
  486.4 19.5 %all_to_all.95.refs_0_ = bf16[32,96,128]{2,1,0:T(8,128)(2,1)S(1)} all-to-all(bf16[32,96,128]{2,1,0:T(8,128)(2,1)S(1)} %get-tuple-element.139), channel_id=1, replica_groups=mesh['pipe'=4,'expert'=32,'dp'=2] {'expert'}, dimensions={0} | all-to-all | bytes 1572864 | tf_op jit(solution)/shard_map/all_to_all | solution.py:419
  505.9 18.4 %collective-permute-start.7 = (bf16[32,2048]{1,0:T(8,128)(2,1)S(1)}, bf16[32,2048]{1,0:T(8,128)(2,1)S(1)}, u32[]{:S(2)}, u32[]{:S(2)}) collective-permute-start(bf16[32,2048]{1,0:T(8,128)(2,1)S(1)} %get-tuple-element.146.refs_0_), channel_id=1, source_target_pairs={{0,1},{1,0},{2,3},{3,2},{4,5},{5,4},{6,7},{7,6},{8,9},{9,8},{10,11... | collective-permute-start | bytes 393224 | tf_op jit(solution)/shard_map/ppermute | solution.py:576
  524.8 3.4 combine.15
  (62 shorter events, 39.2 us)
Async XLA Ops:
  1.3 1.0 copy-start.4
  1.3 1.0 copy-start.8
  1.3 1.2 copy-start.9
  1.3 1.2 copy-start.11
  1.3 1.2 copy-start.12
  2.6 0.7 copy-start.10
  3.2 35.1 %copy-start = (bf16[1,1,2048,768]{3,2,1,0:T(8,128)(2,1)S(1)}, bf16[1,1,2048,768]{3,2,1,0:T(8,128)(2,1)}, u32[]{:S(2)}) copy-start(bf16[1,1,2048,768]{3,2,1,0:T(8,128)(2,1)} %param.18) | copy-start | bytes 9437188
  3.2 35.1 %copy-start.1 = (bf16[1,1,2048,768]{3,2,1,0:T(8,128)(2,1)S(1)}, bf16[1,1,2048,768]{3,2,1,0:T(8,128)(2,1)}, u32[]{:S(2)}) copy-start(bf16[1,1,2048,768]{3,2,1,0:T(8,128)(2,1)} %param.19) | copy-start | bytes 9437188
  3.2 35.1 %copy-start.2 = (bf16[1,1,768,2048]{3,2,1,0:T(8,128)(2,1)S(1)}, bf16[1,1,768,2048]{3,2,1,0:T(8,128)(2,1)}, u32[]{:S(2)}) copy-start(bf16[1,1,768,2048]{3,2,1,0:T(8,128)(2,1)} %param.20) | copy-start | bytes 9437188
  3.2 35.1 %copy-start.3 = (bf16[1,1,2048,32]{2,3,1,0:T(8,128)(2,1)S(1)}, bf16[1,1,2048,32]{2,3,1,0:T(8,128)(2,1)}, u32[]{:S(2)}) copy-start(bf16[1,1,2048,32]{2,3,1,0:T(8,128)(2,1)} %param.21) | copy-start | bytes 393220
  3.3 35.1 %copy-start.5 = (bf16[1,1,16,2048]{3,2,1,0:T(8,128)(2,1)S(1)}, bf16[1,1,16,2048]{3,2,1,0:T(8,128)(2,1)}, u32[]{:S(2)}) copy-start(bf16[1,1,16,2048]{3,2,1,0:T(8,128)(2,1)} %param.24) | copy-start | bytes 196612
  3.3 35.1 %copy-start.6 = (bf16[1,1,2,16,768]{4,3,2,1,0:T(8,128)(2,1)S(1)}, bf16[1,1,2,16,768]{4,3,2,1,0:T(8,128)(2,1)}, u32[]{:S(2)}) copy-start(bf16[1,1,2,16,768]{4,3,2,1,0:T(8,128)(2,1)} %param.22) | copy-start | bytes 147460
  3.3 35.1 %copy-start.7 = (bf16[1,1,768,16]{2,3,1,0:T(8,128)(2,1)S(1)}, bf16[1,1,768,16]{2,3,1,0:T(8,128)(2,1)}, u32[]{:S(2)}) copy-start(bf16[1,1,768,16]{2,3,1,0:T(8,128)(2,1)} %param.23) | copy-start | bytes 73732
  70.4 6.5 %collective-permute-start = (bf16[64,2048]{1,0:T(8,128)(2,1)S(1)}, bf16[64,2048]{1,0:T(8,128)(2,1)S(1)}, u32[]{:S(2)}, u32[]{:S(2)}) collective-permute-start(bf16[64,2048]{1,0:T(8,128)(2,1)S(1)} %combine.8.refs_0_), channel_id=1, source_target_pairs={{0,64},{1,65},{2,66},{3,67},{4,68},{5,69},{6,70},{7,71},{8,72},{9,... | collective-permute-start | bytes 786440 | tf_op jit(solution)/shard_map/ppermute | solution.py:559
  137.2 7.4 %collective-permute-start.1 = (bf16[64,2048]{1,0:T(8,128)(2,1)S(1)}, bf16[64,2048]{1,0:T(8,128)(2,1)S(1)}, u32[]{:S(2)}, u32[]{:S(2)}) collective-permute-start(bf16[64,2048]{1,0:T(8,128)(2,1)S(1)} %combine.9.refs_1_), channel_id=1, source_target_pairs={{64,128},{0,64},{65,129},{1,65},{66,130},{2,66},{67,131},{3,67},{6... | collective-permute-start | bytes 786440 | tf_op jit(solution)/shard_map/ppermute | solution.py:559
  202.1 0.7 collective-permute-start.2
  260.3 0.7 collective-permute-start.3
  318.7 0.7 collective-permute-start.4
  371.7 29.4 %collective-permute-start.5 = (bf16[64,2048]{1,0:T(8,128)(2,1)S(1)}, bf16[64,2048]{1,0:T(8,128)(2,1)S(1)}, u32[]{:S(2)}, u32[]{:S(2)}) collective-permute-start(bf16[64,2048]{1,0:T(8,128)(2,1)S(1)} %combine.13.refs_5_), channel_id=1, source_target_pairs={{64,0},{128,64},{65,1},{129,65},{66,2},{130,66},{67,3},{131,67},{6... | collective-permute-start | bytes 786440 | tf_op jit(solution)/shard_map/ppermute | solution.py:559
  450.6 7.4 %collective-permute-start.6 = (bf16[64,2048]{1,0:T(8,128)(2,1)S(1)}, bf16[64,2048]{1,0:T(8,128)(2,1)S(1)}, u32[]{:S(2)}, u32[]{:S(2)}) collective-permute-start(bf16[64,2048]{1,0:T(8,128)(2,1)S(1)} %combine.14.refs_6_), channel_id=1, source_target_pairs={{64,0},{65,1},{66,2},{67,3},{68,4},{69,5},{70,6},{71,7},{72,8},{73... | collective-permute-start | bytes 786440 | tf_op jit(solution)/shard_map/ppermute | solution.py:559
  505.9 22.3 %collective-permute-start.7 = (bf16[32,2048]{1,0:T(8,128)(2,1)S(1)}, bf16[32,2048]{1,0:T(8,128)(2,1)S(1)}, u32[]{:S(2)}, u32[]{:S(2)}) collective-permute-start(bf16[32,2048]{1,0:T(8,128)(2,1)S(1)} %get-tuple-element.146.refs_0_), channel_id=1, source_target_pairs={{0,1},{1,0},{2,3},{3,2},{4,5},{5,4},{6,7},{7,6},{8,9},{9,8},{10,11... | collective-permute-start | bytes 393224 | tf_op jit(solution)/shard_map/ppermute | solution.py:576
  524.3 3.9 collective-permute-start.10
  524.3 3.9 collective-permute-start.8
  524.8 3.4 collective-permute-start.9
